TPU v7x, 128 devices: a whole 4x4x4 slice. The times are simulated.
128 devices in a mesh: blk: 16 (over x, z), group: 8 (over y, core).
Axes of the slice: x: 4, y: 4, z: 4, core: 2. Of those that a mesh axis runs over, the one named last changes fastest.
Arguments:
- activations: bfloat16 [524288, 2048], P(('blk', 'group')), may hold values from -8 to 8
- grad_out: bfloat16 [524288, 512], P(('blk', 'group')), may hold values from -8 to 8
- weights: float32 [2048, 512], P(('blk', 'group')), may hold values from -6 to 6
- momentum: float32 [2048, 512], P(('blk', 'group')), may hold values from -6 to 6
Outputs:
- new_weights: float32 [2048, 512], P(('blk', 'group'))
- new_momentum: float32 [2048, 512], P(('blk', 'group'))
All inputs are finite; a program needn't handle non-finite values.
Results may differ from a plain program's by a relative error of at most 0.0003.
Values sent between devices are 32-bit elements; how exact they have to be, the bound alone decides.
No kernel may reach another device: no remote copies, remote signals or barrier semaphores. Data moves between devices by JAX's collectives and lax.ppermute only.
A program may use at most 128 MiB of HBM per device.

v0:
```python
import math

import jax
import jax.numpy as jnp
from jax import lax
from jax.sharding import PartitionSpec as P

epsilon = 1e-06


def in_blocks(shard, dim, size):
    before, after = (shard.shape[:dim], shard.shape[dim + 1 :])
    return jnp.moveaxis(shard.reshape(*before, size, -1, *after), dim, 0)


def sent_and_summed(shard, axis, dim):
    tiles = in_blocks(shard, dim, lax.axis_size(axis))
    arrived = lax.all_to_all(tiles, axis, split_axis=0, concat_axis=0, tiled=True)
    return arrived.sum(axis=0)


def swapped(value, axis, distance):
    mask = 2**distance
    pairs = [(source, source ^ mask) for source in range(lax.axis_size(axis))]
    return lax.ppermute(value, axis, pairs)


def from_everyone(shard, axis):
    copies = jnp.broadcast_to(shard, (lax.axis_size(axis), *shard.shape))
    return lax.all_to_all(copies, axis, split_axis=0, concat_axis=0, tiled=True)


def over_copies(shard, axis):
    return from_everyone(shard, axis).sum(axis=0)


def shards(activations, grad_out, weights, momentum):
    blk_count = lax.axis_size("blk")
    group_count = lax.axis_size("group")
    levels = group_count.bit_length() - 1
    tok_rows = activations.shape[0]
    grad_scale = 1.0 / math.sqrt(tok_rows * blk_count)
    contract = (((0,), (0,)), ((), ()))
    current = sent_and_summed(
        lax.dot_general(activations, grad_out, contract, preferred_element_type=jnp.float32)
        * grad_scale,
        "blk",
        0,
    )
    group_index = lax.axis_index("group")
    for level_step in range(levels):
        pair_bit = levels - 1 - level_step
        half_rows = current.shape[0] // 2
        upper_side = group_index >> pair_bit & 1
        lower_half = current[:half_rows]
        upper_half = current[half_rows:]
        kept_half = jnp.where(upper_side == 1, upper_half, lower_half)
        sent_half = jnp.where(upper_side == 1, lower_half, upper_half)
        received = swapped(sent_half, "group", pair_bit)
        first_part = jnp.where(upper_side == 0, kept_half, received)
        second_part = jnp.where(upper_side == 0, received, kept_half)
        partial_value = jnp.stack(
            [
                jnp.sum(first_part * second_part),
                jnp.sum(first_part * first_part),
                jnp.sum(second_part * second_part),
            ]
        )
        sums_now = over_copies(partial_value, "blk")
        for other_bit in range(pair_bit, levels):
            sums_now = sums_now + swapped(sums_now, "group", other_bit)
        coef_first = 1.0 - sums_now[0] / (2.0 * (sums_now[1] + epsilon))
        coef_second = 1.0 - sums_now[0] / (2.0 * (sums_now[2] + epsilon))
        current = coef_first * first_part + coef_second * second_part
    new_momentum = 0.9 * momentum + current
    new_weights = (1.0 - 0.1 * 0.1) * weights - 0.1 * new_momentum
    return (new_weights, new_momentum)


def solution(mesh):
    in_specs = (
        P(("blk", "group"), None),
        P(("blk", "group"), None),
        P(("blk", "group"), None),
        P(("blk", "group"), None),
    )
    out_specs = (P(("blk", "group"), None), P(("blk", "group"), None))
    return jax.shard_map(shards, mesh=mesh, in_specs=in_specs, out_specs=out_specs, check_vma=False)
```

profile of v0, /device:TPU:1, one launch (start us, length us, event | category | flops | bytes accessed | tf_op | source)
XLA Modules:
  0.0 183.2 jit_solution(15275408565530637046)
XLA Ops:
  0.6 15.0 %convolution_multiply_fusion = f32[2048,512]{1,0:T(8,128)} fusion(bf16[4096,2048]{1,0:T(8,128)(2,1)} %param.4, bf16[4096,512]{1,0:T(8,128)(2,1)} %param.5), kind=kOutput, calls=%fused_computation | convolution fusion | flops 8590983168 | bytes 25165824 | tf_op jit(solution)/shard_map/dot_general | solution.py:45
  15.6 8.5 %all-to-all-start = ((f32[16,128,512]{2,1,0:T(8,128)}), f32[16,128,512]{2,1,0:T(8,128)}, u32[]{:S(2)}, u32[]{:S(2)}) async-start(f32[16,128,512]{2,1,0:T(8,128)} %bitcast.18), calls=%async_computation | async-start | bytes 8388608 | tf_op jit(solution)/shard_map/all_to_all | solution.py:18
  24.1 0.0 copy-start
  24.1 0.0 copy-start.1
  24.1 61.2 %all-to-all-done = f32[16,128,512]{2,1,0:T(8,128)} async-done(((f32[16,128,512]{2,1,0:T(8,128)}), f32[16,128,512]{2,1,0:T(8,128)}, u32[]{:S(2)}, u32[]{:S(2)}) %all-to-all-start) | async-done | bytes 4194336 | tf_op jit(solution)/shard_map/all_to_all | solution.py:18
  85.4 2.6 %reduce_sum.117 = f32[128,512]{1,0:T(8,128)S(1)} reduce(f32[16,128,512]{2,1,0:T(8,128)} %all-to-all-done, f32[]{:T(128)} %constant.40.clone.1), dimensions={0}, to_apply=%region_0.0 | reduce | flops 983040 | bytes 4456452 | tf_op jit(solution)/shard_map/reduce_sum | solution.py:19
  88.0 3.0 %collective-permute-start = (f32[64,512]{1,0:T(8,128)S(1)}, f32[64,512]{1,0:T(8,128)S(1)}, u32[]{:S(2)}, u32[]{:S(2)}) collective-permute-start(f32[64,512]{1,0:T(8,128)S(1)} %slice_select_fusion), channel_id=1, source_target_pairs={{0,4},{1,5},{2,6},{3,7},{4,0},{5,1},{6,2},{7,3},{8,12},{9,13},{10,... | collective-permute-start | bytes 393224 | tf_op jit(solution)/shard_map/ppermute | solution.py:25
  91.0 2.4 %collective-permute-done = f32[64,512]{1,0:T(8,128)S(1)} collective-permute-done((f32[64,512]{1,0:T(8,128)S(1)}, f32[64,512]{1,0:T(8,128)S(1)}, u32[]{:S(2)}, u32[]{:S(2)}) %collective-permute-start) | collective-permute-done | bytes 131104 | tf_op jit(solution)/shard_map/ppermute | solution.py:25
  93.4 0.7 multiply_reduce_fusion.2
  94.2 2.1 %pad_maximum_fusion = f32[3]{0:T(128)S(1)} fusion(f32[1]{0:T(128)} %bitcast.3, f32[1]{0:T(128)} %bitcast.2, f32[1]{0:T(128)} %bitcast.1), kind=kLoop, calls=%fused_computation.26 | loop fusion | flops 6 | bytes 24 | tf_op jit(solution)/shard_map/stack | solution.py:62
  96.2 0.6 broadcast_in_dim.9
  96.8 10.4 %all-to-all-start.1 = ((f32[16,1,3]{2,1,0:T(1,128)}), f32[16,1,3]{2,1,0:T(1,128)S(1)}, u32[]{:S(2)}, u32[]{:S(2)}) async-start(f32[16,1,3]{2,1,0:T(1,128)} %broadcast_in_dim.9), calls=%async_computation.1 | async-start | bytes 16384 | tf_op jit(solution)/shard_map/all_to_all | solution.py:30
  107.2 6.3 %all-to-all-done.1 = f32[16,1,3]{2,1,0:T(1,128)S(1)} async-done(((f32[16,1,3]{2,1,0:T(1,128)}), f32[16,1,3]{2,1,0:T(1,128)S(1)}, u32[]{:S(2)}, u32[]{:S(2)}) %all-to-all-start.1) | async-done | bytes 224 | tf_op jit(solution)/shard_map/all_to_all | solution.py:30
  113.6 2.4 %collective-permute-start.1 = (f32[3]{0:T(128)S(1)}, f32[3]{0:T(128)S(1)}, u32[]{:S(2)}, u32[]{:S(2)}) collective-permute-start(f32[3]{0:T(128)S(1)} %reduce_sum.121), channel_id=1, source_target_pairs={{0,4},{1,5},{2,6},{3,7},{4,0},{5,1},{6,2},{7,3},{8,12},{9,13},{10,... | collective-permute-start | bytes 44 | tf_op jit(solution)/shard_map/ppermute | solution.py:25
  116.1 1.5 collective-permute-done.1
  117.6 0.7 fusion.2
  121.0 1.1 collective-permute-start.2
  122.1 2.1 %collective-permute-done.2 = f32[32,512]{1,0:T(8,128)S(1)} collective-permute-done((f32[32,512]{1,0:T(8,128)S(1)}, f32[32,512]{1,0:T(8,128)S(1)}, u32[]{:S(2)}, u32[]{:S(2)}) %collective-permute-start.2) | collective-permute-done | bytes 65568 | tf_op jit(solution)/shard_map/ppermute | solution.py:25
  124.2 0.7 multiply_reduce_fusion.5
  124.9 2.1 %pad_maximum_fusion.1 = f32[3]{0:T(128)S(1)} fusion(f32[1]{0:T(128)} %bitcast.8, f32[1]{0:T(128)} %bitcast.7, f32[1]{0:T(128)} %bitcast.6), kind=kLoop, calls=%fused_computation.27 | loop fusion | flops 6 | bytes 24 | tf_op jit(solution)/shard_map/stack | solution.py:62
  127.0 0.6 broadcast_in_dim.10
  127.6 3.5 %all-to-all-start.2 = ((f32[16,1,3]{2,1,0:T(1,128)}), f32[16,1,3]{2,1,0:T(1,128)S(1)}, u32[]{:S(2)}, u32[]{:S(2)}) async-start(f32[16,1,3]{2,1,0:T(1,128)} %broadcast_in_dim.10), calls=%async_computation.2 | async-start | bytes 16384 | tf_op jit(solution)/shard_map/all_to_all | solution.py:30
  131.0 6.3 %all-to-all-done.2 = f32[16,1,3]{2,1,0:T(1,128)S(1)} async-done(((f32[16,1,3]{2,1,0:T(1,128)}), f32[16,1,3]{2,1,0:T(1,128)S(1)}, u32[]{:S(2)}, u32[]{:S(2)}) %all-to-all-start.2) | async-done | bytes 224 | tf_op jit(solution)/shard_map/all_to_all | solution.py:30
  137.3 1.1 collective-permute-start.3
  138.4 1.4 collective-permute-done.3
  139.8 2.4 %collective-permute-start.4 = (f32[3]{0:T(128)S(1)}, f32[3]{0:T(128)S(1)}, u32[]{:S(2)}, u32[]{:S(2)}) collective-permute-start(f32[3]{0:T(128)S(1)} %add.58), channel_id=1, source_target_pairs={{0,4},{1,5},{2,6},{3,7},{4,0},{5,1},{6,2},{7,3},{8,12},{9,13},{10,... | collective-permute-start | bytes 44 | tf_op jit(solution)/shard_map/ppermute | solution.py:25
  142.2 1.5 collective-permute-done.4
  143.7 0.7 fusion.1
  147.1 10.6 %collective-permute-start.5 = (f32[16,512]{1,0:T(8,128)S(1)}, f32[16,512]{1,0:T(8,128)S(1)}, u32[]{:S(2)}, u32[]{:S(2)}) collective-permute-start(f32[16,512]{1,0:T(8,128)S(1)} %slice_select_fusion.4), channel_id=1, source_target_pairs={{0,1},{1,0},{2,3},{3,2},{4,5},{5,4},{6,7},{7,6},{8,9},{9,8},{10,11... | collective-permute-start | bytes 98312 | tf_op jit(solution)/shard_map/ppermute | solution.py:25
  157.7 0.9 collective-permute-done.5
  158.6 0.7 multiply_reduce_fusion.8
  159.3 2.1 %pad_maximum_fusion.2 = f32[3]{0:T(128)S(1)} fusion(f32[1]{0:T(128)} %bitcast.13, f32[1]{0:T(128)} %bitcast.12, f32[1]{0:T(128)} %bitcast.11), kind=kLoop, calls=%fused_computation.28 | loop fusion | flops 6 | bytes 24 | tf_op jit(solution)/shard_map/stack | solution.py:62
  161.3 9.1 %all_to_all.23 = f32[16,1,3]{2,1,0:T(1,128)S(1)} all-to-all(f32[16,1,3]{2,1,0:T(1,128)S(1)} %broadcast_in_dim.11), channel_id=1, replica_groups=mesh['blk'=16,'group'=8] {'blk'}, dimensions={0} | all-to-all | bytes 384 | tf_op jit(solution)/shard_map/all_to_all | solution.py:30
  170.5 1.8 %collective-permute-start.6 = (f32[3]{0:T(128)S(1)}, f32[3]{0:T(128)S(1)}, u32[]{:S(2)}, u32[]{:S(2)}) collective-permute-start(f32[3]{0:T(128)S(1)} %reduce_sum.129), channel_id=1, source_target_pairs={{0,1},{1,0},{2,3},{3,2},{4,5},{5,4},{6,7},{7,6},{8,9},{9,8},{10,11... | collective-permute-start | bytes 44 | tf_op jit(solution)/shard_map/ppermute | solution.py:25
  172.4 0.8 collective-permute-done.6
  173.2 1.4 collective-permute-start.7
  174.6 1.0 collective-permute-done.7
  175.6 2.7 %collective-permute-start.8 = (f32[3]{0:T(128)S(1)}, f32[3]{0:T(128)S(1)}, u32[]{:S(2)}, u32[]{:S(2)}) collective-permute-start(f32[3]{0:T(128)S(1)} %add.64), channel_id=1, source_target_pairs={{0,4},{1,5},{2,6},{3,7},{4,0},{5,1},{6,2},{7,3},{8,12},{9,13},{10,... | collective-permute-start | bytes 44 | tf_op jit(solution)/shard_map/ppermute | solution.py:25
  178.3 1.2 collective-permute-done.8
  179.5 0.6 fusion
  182.5 0.0 copy-done
  182.5 0.0 copy-done.1
  182.5 0.6 multiply_subtract_fusion
  (15 shorter events, 0.2 us)
Async XLA Ops:
  15.6 69.7 %all-to-all-start = ((f32[16,128,512]{2,1,0:T(8,128)}), f32[16,128,512]{2,1,0:T(8,128)}, u32[]{:S(2)}, u32[]{:S(2)}) async-start(f32[16,128,512]{2,1,0:T(8,128)} %bitcast.18), calls=%async_computation | async-start | bytes 8388608 | tf_op jit(solution)/shard_map/all_to_all | solution.py:18
  24.1 158.4 %copy-start = (f32[16,512]{1,0:T(8,128)S(1)}, f32[16,512]{1,0:T(8,128)}, u32[]{:S(2)}) copy-start(f32[16,512]{1,0:T(8,128)} %param.6) | copy-start | bytes 98308
  24.1 158.4 %copy-start.1 = (f32[16,512]{1,0:T(8,128)S(1)}, f32[16,512]{1,0:T(8,128)}, u32[]{:S(2)}) copy-start(f32[16,512]{1,0:T(8,128)} %param.7) | copy-start | bytes 98308
  88.0 5.4 %collective-permute-start = (f32[64,512]{1,0:T(8,128)S(1)}, f32[64,512]{1,0:T(8,128)S(1)}, u32[]{:S(2)}, u32[]{:S(2)}) collective-permute-start(f32[64,512]{1,0:T(8,128)S(1)} %slice_select_fusion), channel_id=1, source_target_pairs={{0,4},{1,5},{2,6},{3,7},{4,0},{5,1},{6,2},{7,3},{8,12},{9,13},{10,... | collective-permute-start | bytes 393224 | tf_op jit(solution)/shard_map/ppermute | solution.py:25
  96.8 16.7 %all-to-all-start.1 = ((f32[16,1,3]{2,1,0:T(1,128)}), f32[16,1,3]{2,1,0:T(1,128)S(1)}, u32[]{:S(2)}, u32[]{:S(2)}) async-start(f32[16,1,3]{2,1,0:T(1,128)} %broadcast_in_dim.9), calls=%async_computation.1 | async-start | bytes 16384 | tf_op jit(solution)/shard_map/all_to_all | solution.py:30
  113.6 4.0 %collective-permute-start.1 = (f32[3]{0:T(128)S(1)}, f32[3]{0:T(128)S(1)}, u32[]{:S(2)}, u32[]{:S(2)}) collective-permute-start(f32[3]{0:T(128)S(1)} %reduce_sum.121), channel_id=1, source_target_pairs={{0,4},{1,5},{2,6},{3,7},{4,0},{5,1},{6,2},{7,3},{8,12},{9,13},{10,... | collective-permute-start | bytes 44 | tf_op jit(solution)/shard_map/ppermute | solution.py:25
  121.0 3.2 %collective-permute-start.2 = (f32[32,512]{1,0:T(8,128)S(1)}, f32[32,512]{1,0:T(8,128)S(1)}, u32[]{:S(2)}, u32[]{:S(2)}) collective-permute-start(f32[32,512]{1,0:T(8,128)S(1)} %slice_select_fusion.2), channel_id=1, source_target_pairs={{0,2},{1,3},{2,0},{3,1},{4,6},{5,7},{6,4},{7,5},{8,10},{9,11},{10,... | collective-permute-start | bytes 196616 | tf_op jit(solution)/shard_map/ppermute | solution.py:25
  127.6 9.8 %all-to-all-start.2 = ((f32[16,1,3]{2,1,0:T(1,128)}), f32[16,1,3]{2,1,0:T(1,128)S(1)}, u32[]{:S(2)}, u32[]{:S(2)}) async-start(f32[16,1,3]{2,1,0:T(1,128)} %broadcast_in_dim.10), calls=%async_computation.2 | async-start | bytes 16384 | tf_op jit(solution)/shard_map/all_to_all | solution.py:30
  137.3 2.5 %collective-permute-start.3 = (f32[3]{0:T(128)S(1)}, f32[3]{0:T(128)S(1)}, u32[]{:S(2)}, u32[]{:S(2)}) collective-permute-start(f32[3]{0:T(128)S(1)} %reduce_sum.125), channel_id=1, source_target_pairs={{0,2},{1,3},{2,0},{3,1},{4,6},{5,7},{6,4},{7,5},{8,10},{9,11},{10,... | collective-permute-start | bytes 44 | tf_op jit(solution)/shard_map/ppermute | solution.py:25
  139.8 3.9 %collective-permute-start.4 = (f32[3]{0:T(128)S(1)}, f32[3]{0:T(128)S(1)}, u32[]{:S(2)}, u32[]{:S(2)}) collective-permute-start(f32[3]{0:T(128)S(1)} %add.58), channel_id=1, source_target_pairs={{0,4},{1,5},{2,6},{3,7},{4,0},{5,1},{6,2},{7,3},{8,12},{9,13},{10,... | collective-permute-start | bytes 44 | tf_op jit(solution)/shard_map/ppermute | solution.py:25
  147.1 11.5 %collective-permute-start.5 = (f32[16,512]{1,0:T(8,128)S(1)}, f32[16,512]{1,0:T(8,128)S(1)}, u32[]{:S(2)}, u32[]{:S(2)}) collective-permute-start(f32[16,512]{1,0:T(8,128)S(1)} %slice_select_fusion.4), channel_id=1, source_target_pairs={{0,1},{1,0},{2,3},{3,2},{4,5},{5,4},{6,7},{7,6},{8,9},{9,8},{10,11... | collective-permute-start | bytes 98312 | tf_op jit(solution)/shard_map/ppermute | solution.py:25
  170.5 2.7 %collective-permute-start.6 = (f32[3]{0:T(128)S(1)}, f32[3]{0:T(128)S(1)}, u32[]{:S(2)}, u32[]{:S(2)}) collective-permute-start(f32[3]{0:T(128)S(1)} %reduce_sum.129), channel_id=1, source_target_pairs={{0,1},{1,0},{2,3},{3,2},{4,5},{5,4},{6,7},{7,6},{8,9},{9,8},{10,11... | collective-permute-start | bytes 44 | tf_op jit(solution)/shard_map/ppermute | solution.py:25
  173.2 2.4 %collective-permute-start.7 = (f32[3]{0:T(128)S(1)}, f32[3]{0:T(128)S(1)}, u32[]{:S(2)}, u32[]{:S(2)}) collective-permute-start(f32[3]{0:T(128)S(1)} %add.63), channel_id=1, source_target_pairs={{0,2},{1,3},{2,0},{3,1},{4,6},{5,7},{6,4},{7,5},{8,10},{9,11},{10,... | collective-permute-start | bytes 44 | tf_op jit(solution)/shard_map/ppermute | solution.py:25
  175.6 3.9 %collective-permute-start.8 = (f32[3]{0:T(128)S(1)}, f32[3]{0:T(128)S(1)}, u32[]{:S(2)}, u32[]{:S(2)}) collective-permute-start(f32[3]{0:T(128)S(1)} %add.64), channel_id=1, source_target_pairs={{0,4},{1,5},{2,6},{3,7},{4,0},{5,1},{6,2},{7,3},{8,12},{9,13},{10,... | collective-permute-start | bytes 44 | tf_op jit(solution)/shard_map/ppermute | solution.py:25
where the time goes:
time: 185 us; the launch traced here: 183 us
  waiting for transfers between devices  86.6 us (47%)
  starting transfers between devices  48.9 us (26%)
  matrix products  15 us (8%)
  other arithmetic  11.8 us (6%)
  blocking collectives  9.15 us (5%)
  between operations  8.58 us (5%)
  local copies, waits for them, and re-layouts  3.17 us (2%)
    all_to_all x1, waiting for transfers between devices, sent_and_summed(): lax.all_to_all(tiles, axis, split_axis=0, concat_axis=0, tiled=True)  61.2 us
    ppermute x9, starting transfers between devices, swapped(): return lax.ppermute(value, axis, pairs)  26.5 us
    dot_general x1, matrix products, shards(): lax.dot_general(activations, grad_out, contract, preferred_element_type=j...  15 us
    all_to_all x2, starting transfers between devices, from_everyone(): return lax.all_to_all(copies, axis, split_axis=0, concat_axis=0, tiled=True)  13.9 us
    ppermute x9, waiting for transfers between devices, swapped(): return lax.ppermute(value, axis, pairs)  12.8 us
    all_to_all x2, waiting for transfers between devices, from_everyone(): return lax.all_to_all(copies, axis, split_axis=0, concat_axis=0, tiled=True)  12.6 us
    all_to_all x1, blocking collectives, from_everyone(): return lax.all_to_all(copies, axis, split_axis=0, concat_axis=0, tiled=True)  9.15 us
    all_to_all x1, starting transfers between devices, sent_and_summed(): lax.all_to_all(tiles, axis, split_axis=0, concat_axis=0, tiled=True)  8.49 us
  transfers between devices with their start and end apart: 12, of which 12 were waited for; matrix products, arithmetic and copies ran while one was open for 0% of the time, Pallas kernels for 0%

commit v1 on v0

v1 whole, which is shorter than its diff:
```python
import math

import jax
import jax.numpy as jnp
from jax import lax
from jax.experimental import pallas as pl
from jax.experimental.pallas import tpu as pltpu
from jax.sharding import PartitionSpec as P

EPSILON = 1e-06
GROUPS = 8
SIDE = 4
ROWS = 16
HALF = 256
PIECE = GROUPS * ROWS
TOTAL = 128
CONTRACT = (((0,), (0,)), ((), ()))


def exchanged(value, axis, mask):
    return lax.ppermute(value, axis, [(k, k ^ mask) for k in range(lax.axis_size(axis))])


def pair_slots():
    return [(i, j) for i in range(GROUPS) for j in range(i, GROUPS)]


def gram_kernel(place_ref, *refs):
    *block_refs, sums_ref, ordered_ref = refs
    y = place_ref[0]
    slots = [[block_ref[core] for core in range(2)] for block_ref in block_refs]
    for bit in (1, 2):
        moved = (y & bit) != 0
        slots = [
            [jnp.where(moved, slots[k ^ bit][core], slots[k][core]) for core in range(2)]
            for k in range(SIDE)
        ]
    groups = [slots[i // 2][i % 2] for i in range(GROUPS)]
    for i in range(GROUPS):
        ordered_ref[i] = groups[i]
    rows = []
    for i, j in pair_slots():
        product = groups[i] * groups[j]
        product = product[0] + product[1]
        product = product[:8] + product[8:]
        product = product[:, :128] + product[:, 128:]
        rows.append(jnp.sum(product, axis=0, keepdims=True))
    rows.append(jnp.zeros((128 - len(rows), 128), jnp.float32))
    sums_ref[...] = lax.dot_general(
        jnp.ones((TOTAL, 128), jnp.float32),
        jnp.concatenate(rows, axis=0),
        (((1,), (1,)), ((), ())),
        precision=lax.Precision.HIGHEST,
        preferred_element_type=jnp.float32,
    )


def finish_kernel(sums_ref, ordered_ref, weights_ref, momentum_ref, new_weights_ref, new_momentum_ref):
    sums = jnp.sum(sums_ref[...], axis=0, keepdims=True)
    gram = {}
    for place, (i, j) in enumerate(pair_slots()):
        gram[i, j] = gram[j, i] = sums[:, place : place + 1]
    shares = [1.0] * GROUPS
    count = GROUPS
    while count > 1:
        half = count // 2
        coef = [None] * count
        for i in range(half):
            cross = gram[i, i + half]
            coef[i] = 1.0 - cross / (2.0 * (jnp.maximum(gram[i, i], 0.0) + EPSILON))
            coef[i + half] = 1.0 - cross / (2.0 * (jnp.maximum(gram[i + half, i + half], 0.0) + EPSILON))
        shares = [shares[g] * coef[g % count] for g in range(GROUPS)]
        later = {}
        for i in range(half):
            for j in range(i, half):
                later[i, j] = later[j, i] = (
                    coef[i] * coef[j] * gram[i, j]
                    + coef[i + half] * coef[j + half] * gram[i + half, j + half]
                ) + (
                    coef[i] * coef[j + half] * gram[i, j + half]
                    + coef[i + half] * coef[j] * gram[i + half, j]
                )
        gram = later
        count = half
    for part in range(2):
        columns = slice(part * HALF, (part + 1) * HALF)
        combined = shares[0] * ordered_ref[0, part]
        for i in range(1, GROUPS):
            combined = combined + shares[i] * ordered_ref[i, part]
        new_momentum = 0.9 * momentum_ref[:, columns] + combined
        new_momentum_ref[:, columns] = new_momentum
        new_weights_ref[:, columns] = (1.0 - 0.1 * 0.1) * weights_ref[:, columns] - 0.1 * new_momentum


def in_vmem(count):
    return [pl.BlockSpec(memory_space=pltpu.VMEM)] * count


def shards(activations, grad_out, weights, momentum):
    blk = lax.axis_index("blk")
    group = lax.axis_index("group")
    x, z = blk // SIDE, blk % SIDE
    y, core = group // 2, group % 2
    grad_scale = 1.0 / math.sqrt(activations.shape[0] * lax.axis_size("blk"))
    grad = lax.dot_general(activations, grad_out, CONTRACT, preferred_element_type=jnp.float32)
    part_a = grad[:, :HALF].reshape(SIDE, SIDE, PIECE, HALF)
    part_b = grad[:, HALF:].reshape(SIDE, SIDE, PIECE, HALF)

    def taken(value, index, dim):
        return lax.dynamic_index_in_dim(value, index, dim, keepdims=False)

    def reduced(value_a, place_a, dim_a, mask_a, value_b, place_b, dim_b, mask_b):
        arrived_a, arrived_b = [], []
        for s in (2, 1, 3):
            arrived_a.append(exchanged(taken(value_a, place_a ^ s, dim_a), "blk", s * mask_a))
            arrived_b.append(exchanged(taken(value_b, place_b ^ s, dim_b), "blk", s * mask_b))
        sum_a = taken(value_a, place_a, dim_a) + arrived_a[0] + arrived_a[1] + arrived_a[2]
        sum_b = taken(value_b, place_b, dim_b) + arrived_b[0] + arrived_b[1] + arrived_b[2]
        return sum_a, sum_b

    rows_a, rows_b = reduced(part_a, x, 0, SIDE, part_b, z, 1, 1)
    mine_a, mine_b = reduced(rows_a, z, 0, 1, rows_b, x, 0, SIDE)
    mine = jnp.stack(
        [
            mine_a.reshape(SIDE, 2, ROWS, HALF),
            mine_b.reshape(SIDE, 2, ROWS, HALF),
        ],
        axis=2,
    ) * grad_scale
    kept = taken(mine, core, 1)
    came = exchanged(taken(mine, core ^ 1, 1), "group", 1)
    both = jnp.where(core == 0, jnp.stack([kept, came], 1), jnp.stack([came, kept], 1))
    blocks = [taken(both, y, 0)]
    for s in (1, 2, 3):
        blocks.append(exchanged(taken(both, y ^ s, 0), "group", 2 * s))
    sums, ordered = pl.pallas_call(
        gram_kernel,
        in_specs=[pl.BlockSpec(memory_space=pltpu.SMEM)] + in_vmem(SIDE),
        out_specs=in_vmem(2),
        out_shape=[
            jax.ShapeDtypeStruct((TOTAL, 128), jnp.float32),
            jax.ShapeDtypeStruct((GROUPS, 2, ROWS, HALF), jnp.float32),
        ],
        name="gram",
    )(y.reshape(1).astype(jnp.int32), *blocks)
    sums = lax.all_to_all(sums, ("blk", "group"), split_axis=0, concat_axis=0, tiled=True)
    return tuple(
        pl.pallas_call(
            finish_kernel,
            in_specs=in_vmem(4),
            out_specs=in_vmem(2),
            out_shape=[jax.ShapeDtypeStruct(weights.shape, jnp.float32)] * 2,
            name="finish",
        )(sums, ordered, weights, momentum)
    )


def solution(mesh):
    spec = P(("blk", "group"), None)
    return jax.shard_map(
        shards, mesh=mesh, in_specs=(spec,) * 4, out_specs=(spec,) * 2, check_vma=False
    )
```

time: 185 us -> 97.5 us (0.53)
  waiting for transfers between devices: 86.6 us -> 25.5 us
  starting transfers between devices: 48.9 us -> 26.9 us
  other arithmetic: 11.8 us -> 3.26 us
  blocking collectives: 9.15 us -> 17.4 us
  between operations: 8.58 us -> 0.74 us
  Pallas kernels: 0 us -> 3.93 us
  local copies, waits for them, and re-layouts: 3.17 us -> 6.52 us
  matrix products: 15 us -> 12.9 us
    all_to_all x3 -> x0, waiting for transfers between devices: 73.8 us -> none  [the longest x1 61.2 us: sent_and_summed(): lax.all_to_all(tiles, axis, split_axis=0, concat_axis=0, tiled=True)]
    all_to_all x3 -> x0, starting transfers between devices: 22.3 us -> none  [the longest x2 13.9 us: from_everyone(): return lax.all_to_all(copies, axis, split_axis=0, concat_axis=0, tiled=True)]
    ppermute x9 -> x16, waiting for transfers between devices: 12.8 us -> 25.5 us  [exchanged(): lax.ppermute(value, axis, [(k, k ^ mask) for k in range(lax.axis_size(axi...]
    all_to_all x1, blocking collectives: 9.15 us -> 17.4 us  [shards(): lax.all_to_all(sums, ('blk', 'group'), split_axis=0, concat_axis=0, tiled...]
    another operation x3 -> x0, other arithmetic: 6.16 us -> none  [shards(): jnp.stack([jnp.sum(first_part * second_part), jnp.sum(first_part * first_...]
    reduce_sum x7 -> x0, other arithmetic: 4.9 us -> none  [the longest x1 2.63 us: sent_and_summed(): return arrived.sum(axis=0)]
    squeeze x0 -> x5, local copies, waits for them, and re-layouts: none -> 4.26 us  [taken(): return lax.dynamic_index_in_dim(value, index, dim, keepdims=False)]
    pallas_call x0 -> x2, Pallas kernels: none -> 3.93 us  [the longest x1 2.04 us: shards(): pl.pallas_call(finish_kernel, in_specs=in_vmem(4), out_specs=in_vmem(2),...]
  transfers between devices with their start and end apart: 12 -> 16, of which waited for: 12 -> 8; matrix products, arithmetic and copies ran while one was open for 0% -> 5% of each run, Pallas kernels for 0% -> 0%
where the time goes in v1:
time: 97.5 us; the launch traced here: 97.2 us
  starting transfers between devices  26.9 us (28%)
  waiting for transfers between devices  25.5 us (26%)
  blocking collectives  17.4 us (18%)
  matrix products  12.9 us (13%)
  local copies, waits for them, and re-layouts  6.52 us (7%)
  Pallas kernels  3.93 us (4%)
  other arithmetic  3.26 us (3%)
    ppermute x16, starting transfers between devices, exchanged(): lax.ppermute(value, axis, [(k, k ^ mask) for k in range(lax.axis_size(axi...  26.9 us
    ppermute x16, waiting for transfers between devices, exchanged(): lax.ppermute(value, axis, [(k, k ^ mask) for k in range(lax.axis_size(axi...  25.5 us
    all_to_all x1, blocking collectives, shards(): lax.all_to_all(sums, ('blk', 'group'), split_axis=0, concat_axis=0, tiled...  17.4 us
    dot_general x1, matrix products, shards(): lax.dot_general(activations, grad_out, CONTRACT, preferred_element_type=j...  12.9 us
    squeeze x5, local copies, waits for them, and re-layouts, taken(): return lax.dynamic_index_in_dim(value, index, dim, keepdims=False)  4.26 us
    pallas_call x1, Pallas kernels, shards(): pl.pallas_call(finish_kernel, in_specs=in_vmem(4), out_specs=in_vmem(2),...  2.04 us
  transfers between devices with their start and end apart: 16, of which 8 were waited for; matrix products, arithmetic and copies ran while one was open for 5% of the time, Pallas kernels for 0%

profile of v1, /device:TPU:1, one launch (start us, length us, event | category | flops | bytes accessed | tf_op | source)
XLA Modules:
  0.0 97.2 jit_solution(15505591385494514688)
XLA Ops:
  0.7 12.9 %fusion.9 = f32[2048,512]{1,0:T(8,128)S(1)} fusion(bf16[4096,2048]{1,0:T(8,128)(2,1)} %param.4, bf16[4096,512]{1,0:T(8,128)(2,1)} %param.5), kind=kOutput, calls=%fused_computation.33 | convolution fusion | flops 8589934592 | bytes 25165824 | tf_op jit(solution)/shard_map/dot_general | solution.py:105
  13.6 1.6 %fusion.8 = (f32[2048,256]{1,0:T(8,128)S(1)}, f32[2048,256]{1,0:T(8,128)}) fusion(f32[2048,512]{1,0:T(8,128)S(1)} %fusion.9), kind=kLoop, calls=%fused_computation.32 | loop fusion | bytes 8388608 | tf_op jit(solution)/shard_map/slice | solution.py:106
  15.2 2.3 %dynamic-slice_bitcast_fusion.2 = (f32[4,128,256]{2,1,0:T(8,128)S(1)}, f32[4,128,256]{2,1,0:T(8,128)}, f32[4,128,256]{2,1,0:T(8,128)S(1)}) fusion(f32[4,4,128,256]{3,2,1,0:T(8,128)} %bitcast.72, s32[]{:T(128)S(6)} %select_n.91, s32[]{:T(128)S(6)} %select_n.93, s32[]{:T(128)S(6)} %select_n.92), kind=kLoop, calls=%fused_computation.8 | loop fusion | bytes 3145740 | tf_op jit(solution)/shard_map/jit(dynamic_index_in_dim)/squeeze | solution.py:110
  17.5 4.6 %collective-permute-start.8 = (f32[4,128,256]{2,1,0:T(8,128)}, f32[4,128,256]{2,1,0:T(8,128)}, u32[]{:S(2)}, u32[]{:S(2)}) collective-permute-start(f32[4,128,256]{2,1,0:T(8,128)} %get-tuple-element.12), channel_id=1, source_target_pairs={{0,24},{8,16},{16,8},{24,0},{32,56},{40,48},{48,40},{56,32},{64,88... | collective-permute-start | bytes 1572872 | tf_op jit(solution)/shard_map/ppermute | solution.py:21
  22.1 0.0 collective-permute-start.7
  22.1 1.2 %collective-permute-start.6 = (f32[4,128,256]{2,1,0:T(8,128)S(1)}, f32[4,128,256]{2,1,0:T(8,128)}, u32[]{:S(2)}, u32[]{:S(2)}) collective-permute-start(f32[4,128,256]{2,1,0:T(8,128)S(1)} %get-tuple-element.11), channel_id=1, source_target_pairs={{0,16},{8,24},{16,0},{24,8},{32,48},{40,56},{48,32},{56,40},{64,80... | collective-permute-start | bytes 1572872 | tf_op jit(solution)/shard_map/ppermute | solution.py:21
  23.3 1.2 %dynamic-slice_bitcast_fusion.5 = (f32[4,128,256]{2,1,0:T(8,128)}, f32[4,128,256]{2,1,0:T(8,128)}, f32[4,128,256]{2,1,0:T(8,128)}) fusion(f32[4,4,128,256]{3,2,1,0:T(8,128)S(1)} %bitcast.70, s32[]{:T(128)S(6)} %select_n.86, s32[]{:T(128)S(6)} %select_n.88, s32[]{:T(128)S(6)} %select_n.87), kind=kLoop, calls=%fused_computation.11 | loop fusion | bytes 3145740 | tf_op jit(solution)/shard_map/jit(dynamic_index_in_dim)/squeeze | solution.py:110
  24.5 2.5 %collective-permute-start.2 = (f32[4,128,256]{2,1,0:T(8,128)}, f32[4,128,256]{2,1,0:T(8,128)}, u32[]{:S(2)}, u32[]{:S(2)}) collective-permute-start(f32[4,128,256]{2,1,0:T(8,128)} %get-tuple-element.9), channel_id=1, source_target_pairs={{0,96},{8,104},{16,112},{24,120},{32,64},{40,72},{48,80},{56,88},{... | collective-permute-start | bytes 1572872 | tf_op jit(solution)/shard_map/ppermute | solution.py:21
  27.0 0.0 collective-permute-start.1
  27.0 7.1 %collective-permute-done.8 = f32[4,128,256]{2,1,0:T(8,128)} collective-permute-done((f32[4,128,256]{2,1,0:T(8,128)}, f32[4,128,256]{2,1,0:T(8,128)}, u32[]{:S(2)}, u32[]{:S(2)}) %collective-permute-start.8) | collective-permute-done | bytes 524320 | tf_op jit(solution)/shard_map/ppermute | solution.py:21
  34.1 2.7 %collective-permute-start = (f32[4,128,256]{2,1,0:T(8,128)}, f32[4,128,256]{2,1,0:T(8,128)}, u32[]{:S(2)}, u32[]{:S(2)}) collective-permute-start(f32[4,128,256]{2,1,0:T(8,128)} %get-tuple-element.8), channel_id=1, source_target_pairs={{0,64},{8,72},{16,80},{24,88},{32,96},{40,104},{48,112},{56,120},{... | collective-permute-start | bytes 1572872 | tf_op jit(solution)/shard_map/ppermute | solution.py:21
  36.8 0.0 collective-permute-done.7
  36.8 9.1 %collective-permute-done.6 = f32[4,128,256]{2,1,0:T(8,128)} collective-permute-done((f32[4,128,256]{2,1,0:T(8,128)S(1)}, f32[4,128,256]{2,1,0:T(8,128)}, u32[]{:S(2)}, u32[]{:S(2)}) %collective-permute-start.6) | collective-permute-done | bytes 524320 | tf_op jit(solution)/shard_map/ppermute | solution.py:21
  45.9 1.7 %fusion.1 = f32[4,128,256]{2,1,0:T(8,128)S(1)} fusion(f32[4,128,256]{2,1,0:T(8,128)} %collective-permute-done.8, f32[4,128,256]{2,1,0:T(8,128)} %collective-permute-done.7, f32[4,128,256]{2,1,0:T(8,128)} %collective-permute-done.6, f32[4,4,128,256]{3,2,1,0:T(8,128)} %bitcast.73, s32[]{:T(128)S(6)} %select_n.90), kind=kLoop, calls=%fused_computation.2 | loop fusion | flops 393216 | bytes 2621444 | tf_op jit(solution)/shard_map/add | solution.py:118
  47.6 2.6 %collective-permute-start.11 = (f32[128,256]{1,0:T(8,128)S(1)}, f32[128,256]{1,0:T(8,128)S(1)}, u32[]{:S(2)}, u32[]{:S(2)}) collective-permute-start(f32[128,256]{1,0:T(8,128)S(1)} %get-tuple-element.18), channel_id=1, source_target_pairs={{0,96},{8,104},{16,112},{24,120},{32,64},{40,72},{48,80},{56,88},{... | collective-permute-start | bytes 393224 | tf_op jit(solution)/shard_map/ppermute | solution.py:21
  50.2 0.0 collective-permute-start.10
  50.2 0.0 collective-permute-done.2
  50.2 1.4 %collective-permute-start.9 = (f32[128,256]{1,0:T(8,128)S(1)}, f32[128,256]{1,0:T(8,128)S(1)}, u32[]{:S(2)}, u32[]{:S(2)}) collective-permute-start(f32[128,256]{1,0:T(8,128)S(1)} %get-tuple-element.17), channel_id=1, source_target_pairs={{0,64},{8,72},{16,80},{24,88},{32,96},{40,104},{48,112},{56,120},{... | collective-permute-start | bytes 393224 | tf_op jit(solution)/shard_map/ppermute | solution.py:21
  51.6 0.0 collective-permute-done.1
  51.6 0.0 collective-permute-done
  51.6 1.5 %fusion.3 = f32[4,128,256]{2,1,0:T(8,128)S(1)} fusion(f32[4,128,256]{2,1,0:T(8,128)} %collective-permute-done.2, f32[4,128,256]{2,1,0:T(8,128)} %collective-permute-done.1, f32[4,128,256]{2,1,0:T(8,128)} %collective-permute-done, f32[4,4,128,256]{3,2,1,0:T(8,128)S(1)} %bitcast.71, s32[]{:T(128)S(6)} %select_n.85), kind=kLoop, calls=%fused_computation.5 | loop fusion | flops 393216 | bytes 2621444 | tf_op jit(solution)/shard_map/add | solution.py:117
  53.1 2.4 %collective-permute-start.5 = (f32[128,256]{1,0:T(8,128)S(1)}, f32[128,256]{1,0:T(8,128)S(1)}, u32[]{:S(2)}, u32[]{:S(2)}) collective-permute-start(f32[128,256]{1,0:T(8,128)S(1)} %get-tuple-element.15), channel_id=1, source_target_pairs={{0,24},{8,16},{16,8},{24,0},{32,56},{40,48},{48,40},{56,32},{64,88... | collective-permute-start | bytes 393224 | tf_op jit(solution)/shard_map/ppermute | solution.py:21
  55.6 0.0 collective-permute-start.4
  55.6 0.0 collective-permute-done.11
  55.6 1.5 %collective-permute-start.3 = (f32[128,256]{1,0:T(8,128)S(1)}, f32[128,256]{1,0:T(8,128)S(1)}, u32[]{:S(2)}, u32[]{:S(2)}) collective-permute-start(f32[128,256]{1,0:T(8,128)S(1)} %get-tuple-element.14), channel_id=1, source_target_pairs={{0,16},{8,24},{16,0},{24,8},{32,48},{40,56},{48,32},{56,40},{64,80... | collective-permute-start | bytes 393224 | tf_op jit(solution)/shard_map/ppermute | solution.py:21
  57.1 0.0 collective-permute-done.10
  57.1 0.0 collective-permute-done.9
  57.1 1.4 %collective-permute-done.5 = f32[128,256]{1,0:T(8,128)S(1)} collective-permute-done((f32[128,256]{1,0:T(8,128)S(1)}, f32[128,256]{1,0:T(8,128)S(1)}, u32[]{:S(2)}, u32[]{:S(2)}) %collective-permute-start.5) | collective-permute-done | bytes 131104 | tf_op jit(solution)/shard_map/ppermute | solution.py:21
  58.5 0.8 collective-permute-done.4
  59.4 1.6 %collective-permute-done.3 = f32[128,256]{1,0:T(8,128)S(1)} collective-permute-done((f32[128,256]{1,0:T(8,128)S(1)}, f32[128,256]{1,0:T(8,128)S(1)}, u32[]{:S(2)}, u32[]{:S(2)}) %collective-permute-start.3) | collective-permute-done | bytes 131104 | tf_op jit(solution)/shard_map/ppermute | solution.py:21
  61.1 4.1 %collective-permute-start.12 = (f32[4,2,16,256]{3,2,1,0:T(8,128)S(1)}, f32[4,2,16,256]{3,2,1,0:T(8,128)S(1)}, u32[]{:S(2)}, u32[]{:S(2)}) collective-permute-start(f32[4,2,16,256]{3,2,1,0:T(8,128)S(1)} %get-tuple-element.25), channel_id=1, source_target_pairs={{0,1},{1,0},{2,3},{3,2},{4,5},{5,4},{6,7},{7,6},{8,9},{9,8},{10,11... | collective-permute-start | bytes 393224 | tf_op jit(solution)/shard_map/ppermute | solution.py:21
  65.2 1.0 %collective-permute-done.12 = f32[4,2,16,256]{3,2,1,0:T(8,128)S(1)} collective-permute-done((f32[4,2,16,256]{3,2,1,0:T(8,128)S(1)}, f32[4,2,16,256]{3,2,1,0:T(8,128)S(1)}, u32[]{:S(2)}, u32[]{:S(2)}) %collective-permute-start.12) | collective-permute-done | bytes 131104 | tf_op jit(solution)/shard_map/ppermute | solution.py:21
  66.2 0.6 dynamic-slice_bitcast_fusion.13
  66.9 1.3 %collective-permute-start.13 = (f32[2,2,16,256]{3,2,1,0:T(8,128)S(1)}, f32[2,2,16,256]{3,2,1,0:T(8,128)S(1)}, u32[]{:S(2)}, u32[]{:S(2)}) collective-permute-start(f32[2,2,16,256]{3,2,1,0:T(8,128)S(1)} %get-tuple-element.22), channel_id=1, source_target_pairs={{0,2},{1,3},{2,0},{3,1},{4,6},{5,7},{6,4},{7,5},{8,10},{9,11},{10,... | collective-permute-start | bytes 196616 | tf_op jit(solution)/shard_map/ppermute | solution.py:21
  68.2 2.6 %collective-permute-start.14 = (f32[2,2,16,256]{3,2,1,0:T(8,128)S(1)}, f32[2,2,16,256]{3,2,1,0:T(8,128)S(1)}, u32[]{:S(2)}, u32[]{:S(2)}) collective-permute-start(f32[2,2,16,256]{3,2,1,0:T(8,128)S(1)} %get-tuple-element.21), channel_id=1, source_target_pairs={{0,4},{1,5},{2,6},{3,7},{4,0},{5,1},{6,2},{7,3},{8,12},{9,13},{10,... | collective-permute-start | bytes 196616 | tf_op jit(solution)/shard_map/ppermute | solution.py:21
  70.8 0.0 collective-permute-start.15
  70.8 0.0 collective-permute-done.13.refs_1_
  70.8 0.0 copy-start
  70.8 2.9 %collective-permute-done.14.refs_2_ = f32[2,2,16,256]{3,2,1,0:T(8,128)S(1)} collective-permute-done((f32[2,2,16,256]{3,2,1,0:T(8,128)S(1)}, f32[2,2,16,256]{3,2,1,0:T(8,128)S(1)}, u32[]{:S(2)}, u32[]{:S(2)}) %collective-permute-start.14) | collective-permute-done | bytes 65568 | tf_op jit(solution)/shard_map/ppermute | solution.py:21
  73.8 0.0 copy-start.1
  73.8 1.5 %collective-permute-done.15.refs_3_ = f32[2,2,16,256]{3,2,1,0:T(8,128)S(1)} collective-permute-done((f32[2,2,16,256]{3,2,1,0:T(8,128)S(1)}, f32[2,2,16,256]{3,2,1,0:T(8,128)S(1)}, u32[]{:S(2)}, u32[]{:S(2)}) %collective-permute-start.15) | collective-permute-done | bytes 65568 | tf_op jit(solution)/shard_map/ppermute | solution.py:21
  75.3 0.0 copy-start.2
  75.3 0.0 copy-done
  75.3 0.0 copy-done.1
  75.3 0.6 copy-done.2
  75.9 1.9 %gram.1 = (f32[128,128]{1,0:T(8,128)}, f32[8,2,16,256]{3,2,1,0:T(8,128)}) custom-call(s32[1]{0:T(128)} %bitcast.place_ref, f32[2,2,16,256]{3,2,1,0:T(8,128)} %get-tuple-element.23.refs_0_, f32[2,2,16,256]{3,2,1,0:T(8,128)} %copy-done, f32[2,2,16,256]{3,2,1,0:T(8,128)} %copy-done.1, f32[2,2,16,256]{3,2,1,0:T(8,128)} %copy-done.2), custom_call_target="tpu_custom_call" | custom-call | tf_op jit(solution)/shard_map/gram/pallas_call | solution.py:136
  77.8 17.4 %all_to_all.11 = f32[128,1,128]{2,1,0:T(1,128)} all-to-all(f32[128,1,128]{2,1,0:T(1,128)} %bitcast.78), channel_id=1, replica_groups=mesh['blk'=16,'group'=8] {'blk','group'}, dimensions={0} | all-to-all | bytes 131072 | tf_op jit(solution)/shard_map/all_to_all | solution.py:146
  95.2 2.0 %finish.1 = (f32[16,512]{1,0:T(8,128)}, f32[16,512]{1,0:T(8,128)}) custom-call(f32[128,128]{1,0:T(8,128)} %bitcast.76, f32[8,2,16,256]{3,2,1,0:T(8,128)} %get-tuple-element.5.ordered_ref, f32[16,512]{1,0:T(8,128)} %weights_ref.1, f32[16,512]{1,0:T(8,128)} %momentum_ref.1), custom_call_target="tpu_custom_call" | custom-call | tf_op jit(solution)/shard_map/finish/pallas_call | solution.py:148
  (7 shorter events, 0.2 us)
Async XLA Ops:
  17.5 16.6 %collective-permute-start.8 = (f32[4,128,256]{2,1,0:T(8,128)}, f32[4,128,256]{2,1,0:T(8,128)}, u32[]{:S(2)}, u32[]{:S(2)}) collective-permute-start(f32[4,128,256]{2,1,0:T(8,128)} %get-tuple-element.12), channel_id=1, source_target_pairs={{0,24},{8,16},{16,8},{24,0},{32,56},{40,48},{48,40},{56,32},{64,88... | collective-permute-start | bytes 1572872 | tf_op jit(solution)/shard_map/ppermute | solution.py:21
  22.1 14.7 %collective-permute-start.7 = (f32[4,128,256]{2,1,0:T(8,128)S(1)}, f32[4,128,256]{2,1,0:T(8,128)}, u32[]{:S(2)}, u32[]{:S(2)}) collective-permute-start(f32[4,128,256]{2,1,0:T(8,128)S(1)} %get-tuple-element.13), channel_id=1, source_target_pairs={{0,8},{8,0},{16,24},{24,16},{32,40},{40,32},{48,56},{56,48},{64,72... | collective-permute-start | bytes 1572872 | tf_op jit(solution)/shard_map/ppermute | solution.py:21
  22.1 23.8 %collective-permute-start.6 = (f32[4,128,256]{2,1,0:T(8,128)S(1)}, f32[4,128,256]{2,1,0:T(8,128)}, u32[]{:S(2)}, u32[]{:S(2)}) collective-permute-start(f32[4,128,256]{2,1,0:T(8,128)S(1)} %get-tuple-element.11), channel_id=1, source_target_pairs={{0,16},{8,24},{16,0},{24,8},{32,48},{40,56},{48,32},{56,40},{64,80... | collective-permute-start | bytes 1572872 | tf_op jit(solution)/shard_map/ppermute | solution.py:21
  24.5 25.7 %collective-permute-start.2 = (f32[4,128,256]{2,1,0:T(8,128)}, f32[4,128,256]{2,1,0:T(8,128)}, u32[]{:S(2)}, u32[]{:S(2)}) collective-permute-start(f32[4,128,256]{2,1,0:T(8,128)} %get-tuple-element.9), channel_id=1, source_target_pairs={{0,96},{8,104},{16,112},{24,120},{32,64},{40,72},{48,80},{56,88},{... | collective-permute-start | bytes 1572872 | tf_op jit(solution)/shard_map/ppermute | solution.py:21
  27.0 24.6 %collective-permute-start.1 = (f32[4,128,256]{2,1,0:T(8,128)}, f32[4,128,256]{2,1,0:T(8,128)}, u32[]{:S(2)}, u32[]{:S(2)}) collective-permute-start(f32[4,128,256]{2,1,0:T(8,128)} %get-tuple-element.10), channel_id=1, source_target_pairs={{0,32},{8,40},{16,48},{24,56},{32,0},{40,8},{48,16},{56,24},{64,96... | collective-permute-start | bytes 1572872 | tf_op jit(solution)/shard_map/ppermute | solution.py:21
  34.1 17.5 %collective-permute-start = (f32[4,128,256]{2,1,0:T(8,128)}, f32[4,128,256]{2,1,0:T(8,128)}, u32[]{:S(2)}, u32[]{:S(2)}) collective-permute-start(f32[4,128,256]{2,1,0:T(8,128)} %get-tuple-element.8), channel_id=1, source_target_pairs={{0,64},{8,72},{16,80},{24,88},{32,96},{40,104},{48,112},{56,120},{... | collective-permute-start | bytes 1572872 | tf_op jit(solution)/shard_map/ppermute | solution.py:21
  47.6 7.9 %collective-permute-start.11 = (f32[128,256]{1,0:T(8,128)S(1)}, f32[128,256]{1,0:T(8,128)S(1)}, u32[]{:S(2)}, u32[]{:S(2)}) collective-permute-start(f32[128,256]{1,0:T(8,128)S(1)} %get-tuple-element.18), channel_id=1, source_target_pairs={{0,96},{8,104},{16,112},{24,120},{32,64},{40,72},{48,80},{56,88},{... | collective-permute-start | bytes 393224 | tf_op jit(solution)/shard_map/ppermute | solution.py:21
  50.2 6.9 %collective-permute-start.10 = (f32[128,256]{1,0:T(8,128)S(1)}, f32[128,256]{1,0:T(8,128)S(1)}, u32[]{:S(2)}, u32[]{:S(2)}) collective-permute-start(f32[128,256]{1,0:T(8,128)S(1)} %get-tuple-element.19), channel_id=1, source_target_pairs={{0,32},{8,40},{16,48},{24,56},{32,0},{40,8},{48,16},{56,24},{64,96... | collective-permute-start | bytes 393224 | tf_op jit(solution)/shard_map/ppermute | solution.py:21
  50.2 6.9 %collective-permute-start.9 = (f32[128,256]{1,0:T(8,128)S(1)}, f32[128,256]{1,0:T(8,128)S(1)}, u32[]{:S(2)}, u32[]{:S(2)}) collective-permute-start(f32[128,256]{1,0:T(8,128)S(1)} %get-tuple-element.17), channel_id=1, source_target_pairs={{0,64},{8,72},{16,80},{24,88},{32,96},{40,104},{48,112},{56,120},{... | collective-permute-start | bytes 393224 | tf_op jit(solution)/shard_map/ppermute | solution.py:21
  53.1 5.4 %collective-permute-start.5 = (f32[128,256]{1,0:T(8,128)S(1)}, f32[128,256]{1,0:T(8,128)S(1)}, u32[]{:S(2)}, u32[]{:S(2)}) collective-permute-start(f32[128,256]{1,0:T(8,128)S(1)} %get-tuple-element.15), channel_id=1, source_target_pairs={{0,24},{8,16},{16,8},{24,0},{32,56},{40,48},{48,40},{56,32},{64,88... | collective-permute-start | bytes 393224 | tf_op jit(solution)/shard_map/ppermute | solution.py:21
  55.6 3.8 %collective-permute-start.4 = (f32[128,256]{1,0:T(8,128)S(1)}, f32[128,256]{1,0:T(8,128)S(1)}, u32[]{:S(2)}, u32[]{:S(2)}) collective-permute-start(f32[128,256]{1,0:T(8,128)S(1)} %get-tuple-element.16), channel_id=1, source_target_pairs={{0,8},{8,0},{16,24},{24,16},{32,40},{40,32},{48,56},{56,48},{64,72... | collective-permute-start | bytes 393224 | tf_op jit(solution)/shard_map/ppermute | solution.py:21
  55.6 5.4 %collective-permute-start.3 = (f32[128,256]{1,0:T(8,128)S(1)}, f32[128,256]{1,0:T(8,128)S(1)}, u32[]{:S(2)}, u32[]{:S(2)}) collective-permute-start(f32[128,256]{1,0:T(8,128)S(1)} %get-tuple-element.14), channel_id=1, source_target_pairs={{0,16},{8,24},{16,0},{24,8},{32,48},{40,56},{48,32},{56,40},{64,80... | collective-permute-start | bytes 393224 | tf_op jit(solution)/shard_map/ppermute | solution.py:21
  61.1 5.1 %collective-permute-start.12 = (f32[4,2,16,256]{3,2,1,0:T(8,128)S(1)}, f32[4,2,16,256]{3,2,1,0:T(8,128)S(1)}, u32[]{:S(2)}, u32[]{:S(2)}) collective-permute-start(f32[4,2,16,256]{3,2,1,0:T(8,128)S(1)} %get-tuple-element.25), channel_id=1, source_target_pairs={{0,1},{1,0},{2,3},{3,2},{4,5},{5,4},{6,7},{7,6},{8,9},{9,8},{10,11... | collective-permute-start | bytes 393224 | tf_op jit(solution)/shard_map/ppermute | solution.py:21
  66.9 3.9 %collective-permute-start.13 = (f32[2,2,16,256]{3,2,1,0:T(8,128)S(1)}, f32[2,2,16,256]{3,2,1,0:T(8,128)S(1)}, u32[]{:S(2)}, u32[]{:S(2)}) collective-permute-start(f32[2,2,16,256]{3,2,1,0:T(8,128)S(1)} %get-tuple-element.22), channel_id=1, source_target_pairs={{0,2},{1,3},{2,0},{3,1},{4,6},{5,7},{6,4},{7,5},{8,10},{9,11},{10,... | collective-permute-start | bytes 196616 | tf_op jit(solution)/shard_map/ppermute | solution.py:21
  68.2 5.6 %collective-permute-start.14 = (f32[2,2,16,256]{3,2,1,0:T(8,128)S(1)}, f32[2,2,16,256]{3,2,1,0:T(8,128)S(1)}, u32[]{:S(2)}, u32[]{:S(2)}) collective-permute-start(f32[2,2,16,256]{3,2,1,0:T(8,128)S(1)} %get-tuple-element.21), channel_id=1, source_target_pairs={{0,4},{1,5},{2,6},{3,7},{4,0},{5,1},{6,2},{7,3},{8,12},{9,13},{10,... | collective-permute-start | bytes 196616 | tf_op jit(solution)/shard_map/ppermute | solution.py:21
  70.8 4.5 %collective-permute-start.15 = (f32[2,2,16,256]{3,2,1,0:T(8,128)S(1)}, f32[2,2,16,256]{3,2,1,0:T(8,128)S(1)}, u32[]{:S(2)}, u32[]{:S(2)}) collective-permute-start(f32[2,2,16,256]{3,2,1,0:T(8,128)S(1)} %get-tuple-element.20), channel_id=1, source_target_pairs={{0,6},{1,7},{2,4},{3,5},{4,2},{5,3},{6,0},{7,1},{8,14},{9,15},{10,... | collective-permute-start | bytes 196616 | tf_op jit(solution)/shard_map/ppermute | solution.py:21
  70.8 4.5 %copy-start = (f32[2,2,16,256]{3,2,1,0:T(8,128)}, f32[2,2,16,256]{3,2,1,0:T(8,128)S(1)}, u32[]{:S(2)}) copy-start(f32[2,2,16,256]{3,2,1,0:T(8,128)S(1)} %collective-permute-done.13.refs_1_) | copy-start | bytes 196612
  73.8 1.5 %copy-start.1 = (f32[2,2,16,256]{3,2,1,0:T(8,128)}, f32[2,2,16,256]{3,2,1,0:T(8,128)S(1)}, u32[]{:S(2)}) copy-start(f32[2,2,16,256]{3,2,1,0:T(8,128)S(1)} %collective-permute-done.14.refs_2_) | copy-start | bytes 196612
  75.3 0.6 copy-start.2

commit v2 on v1

--- a/solution.py
+++ b/solution.py
@@ -1,3 +1,4 @@
+import functools
 import math
 
 import jax
@@ -11,14 +12,89 @@
 GROUPS = 8
 SIDE = 4
 ROWS = 16
-HALF = 256
+COLS = 512
 PIECE = GROUPS * ROWS
+DEPTH = 1024
 TOTAL = 128
 CONTRACT = (((0,), (0,)), ((), ()))
 
 
 def exchanged(value, axis, mask):
     return lax.ppermute(value, axis, [(k, k ^ mask) for k in range(lax.axis_size(axis))])
+
+
+def in_vmem(count):
+    return [pl.BlockSpec(memory_space=pltpu.VMEM)] * count
+
+
+def piece_blocks(x, z, s):
+    along_x = [(x ^ s) * SIDE + ((x ^ s) & 1) + 2 * k for k in range(2)]
+    along_z = [((((z ^ s) & 1) ^ 1) + 2 * k) * SIDE + (z ^ s) for k in range(2)]
+    return along_x + along_z
+
+
+def product_kernel(masks, depth, added, place_ref, act_ref, out_ref, *refs):
+    base_refs, refs = refs[: 2 * added], refs[2 * added :]
+    pieces = refs[: 2 * len(masks)]
+    held, grad, sems = refs[2 * len(masks) :]
+    chunks = out_ref.shape[0] // depth
+    blocks = [piece_blocks(place_ref[0], place_ref[1], s) for s in masks]
+
+    def copies(k):
+        rows = pl.ds(k * depth, depth)
+        ends = [(out_ref.at[rows], grad.at[rows])]
+        for n in range(len(masks)):
+            for c in range(4):
+                start = pl.multiple_of(blocks[n][c] * PIECE, PIECE)
+                ends.append(
+                    (act_ref.at[rows, pl.ds(start, PIECE)], held.at[n, rows, pl.ds(c * PIECE, PIECE)])
+                )
+        return [
+            pltpu.make_async_copy(source, target, sems.at[k, place])
+            for place, (source, target) in enumerate(ends)
+        ]
+
+    for k in range(chunks):
+        for copy in copies(k):
+            copy.start()
+    for k in range(chunks):
+        for copy in copies(k):
+            copy.wait()
+        rows = pl.ds(k * depth, depth)
+        for n in range(len(masks)):
+            part = lax.dot_general(
+                held[n, rows], grad[rows], CONTRACT, preferred_element_type=jnp.float32
+            )
+            for way in range(2):
+                piece = pieces[2 * n + way]
+                mine = part[way * 2 * PIECE : (way + 1) * 2 * PIECE]
+                if k:
+                    piece[...] += mine
+                elif added:
+                    piece[...] = base_refs[way][...] + mine
+                else:
+                    piece[...] = mine
+
+
+def products(activations, grad_out, place, masks, depth, vmem, base=()):
+    tokens, cols = grad_out.shape
+    count = 2 * len(masks)
+    return pl.pallas_call(
+        functools.partial(product_kernel, masks, depth, len(base) // 2),
+        in_specs=[pl.BlockSpec(memory_space=pltpu.SMEM)]
+        + [pl.BlockSpec(memory_space=pl.ANY)] * 2
+        + in_vmem(len(base)),
+        out_specs=in_vmem(count),
+        out_shape=[jax.ShapeDtypeStruct((2 * PIECE, cols), jnp.float32)] * count,
+        scratch_shapes=[
+            pltpu.VMEM((len(masks), tokens, 4 * PIECE), activations.dtype),
+            pltpu.VMEM((tokens, cols), grad_out.dtype),
+            pltpu.SemaphoreType.DMA((tokens // depth, 1 + 4 * len(masks))),
+        ],
+        compiler_params=pltpu.CompilerParams(vmem_limit_bytes=vmem << 20),
+        cost_estimate=pl.CostEstimate(flops=1000, bytes_accessed=1000, transcendentals=0),
+        name="products",
+    )(place, activations, grad_out, *base)
 
 
 def pair_slots():
@@ -41,8 +117,8 @@
     rows = []
     for i, j in pair_slots():
         product = groups[i] * groups[j]
-        product = product[0] + product[1]
         product = product[:8] + product[8:]
+        product = product[:, :256] + product[:, 256:]
         product = product[:, :128] + product[:, 128:]
         rows.append(jnp.sum(product, axis=0, keepdims=True))
     rows.append(jnp.zeros((128 - len(rows), 128), jnp.float32))
@@ -82,18 +158,21 @@
                 )
         gram = later
         count = half
-    for part in range(2):
-        columns = slice(part * HALF, (part + 1) * HALF)
-        combined = shares[0] * ordered_ref[0, part]
-        for i in range(1, GROUPS):
-            combined = combined + shares[i] * ordered_ref[i, part]
-        new_momentum = 0.9 * momentum_ref[:, columns] + combined
-        new_momentum_ref[:, columns] = new_momentum
-        new_weights_ref[:, columns] = (1.0 - 0.1 * 0.1) * weights_ref[:, columns] - 0.1 * new_momentum
-
-
-def in_vmem(count):
-    return [pl.BlockSpec(memory_space=pltpu.VMEM)] * count
+    combined = shares[0] * ordered_ref[0]
+    for i in range(1, GROUPS):
+        combined = combined + shares[i] * ordered_ref[i]
+    new_momentum = 0.9 * momentum_ref[...] + combined
+    new_momentum_ref[...] = new_momentum
+    new_weights_ref[...] = (1.0 - 0.1 * 0.1) * weights_ref[...] - 0.1 * new_momentum
+
+
+def second_pairs(s):
+    pairs = []
+    for k in range(SIDE * SIDE):
+        x, z = k // SIDE, k % SIDE
+        along_z = ((x ^ z) & 1 == 0) == (s == 2)
+        pairs.append((k, k ^ s if along_z else k ^ (SIDE * s)))
+    return pairs
 
 
 def shards(activations, grad_out, weights, momentum):
@@ -102,31 +181,33 @@
     x, z = blk // SIDE, blk % SIDE
     y, core = group // 2, group % 2
     grad_scale = 1.0 / math.sqrt(activations.shape[0] * lax.axis_size("blk"))
-    grad = lax.dot_general(activations, grad_out, CONTRACT, preferred_element_type=jnp.float32)
-    part_a = grad[:, :HALF].reshape(SIDE, SIDE, PIECE, HALF)
-    part_b = grad[:, HALF:].reshape(SIDE, SIDE, PIECE, HALF)
+    place = jnp.stack([x, z]).astype(jnp.int32)
 
     def taken(value, index, dim):
         return lax.dynamic_index_in_dim(value, index, dim, keepdims=False)
 
-    def reduced(value_a, place_a, dim_a, mask_a, value_b, place_b, dim_b, mask_b):
-        arrived_a, arrived_b = [], []
-        for s in (2, 1, 3):
-            arrived_a.append(exchanged(taken(value_a, place_a ^ s, dim_a), "blk", s * mask_a))
-            arrived_b.append(exchanged(taken(value_b, place_b ^ s, dim_b), "blk", s * mask_b))
-        sum_a = taken(value_a, place_a, dim_a) + arrived_a[0] + arrived_a[1] + arrived_a[2]
-        sum_b = taken(value_b, place_b, dim_b) + arrived_b[0] + arrived_b[1] + arrived_b[2]
-        return sum_a, sum_b
-
-    rows_a, rows_b = reduced(part_a, x, 0, SIDE, part_b, z, 1, 1)
-    mine_a, mine_b = reduced(rows_a, z, 0, 1, rows_b, x, 0, SIDE)
-    mine = jnp.stack(
-        [
-            mine_a.reshape(SIDE, 2, ROWS, HALF),
-            mine_b.reshape(SIDE, 2, ROWS, HALF),
-        ],
-        axis=2,
-    ) * grad_scale
+    def both_ways(pair, s):
+        return [exchanged(pair[0], "blk", SIDE * s), exchanged(pair[1], "blk", s)]
+
+    far = products(activations, grad_out, place, (2,), DEPTH, 62)
+    far_came = both_ways(far, 2)
+    place, far = lax.optimization_barrier((place, far))
+    near = products(activations, grad_out, place, (1, 3), DEPTH, 50)
+    near_came = both_ways(near[:2], 1), both_ways(near[2:], 3)
+    place, near = lax.optimization_barrier((place, near))
+    kept = products(activations, grad_out, place, (0,), DEPTH, 50, far_came)
+    rows = jnp.concatenate(
+        [own + a + b for own, a, b in zip(kept, *near_came)], axis=0
+    ).reshape(4, PIECE, COLS)
+    odd = (x ^ z) & 1
+    mine = taken(rows, jnp.where(odd == 0, z >> 1, 2 + (x >> 1)), 0)
+    for s in (2, 1, 3):
+        if s == 2:
+            sent = jnp.where(odd == 0, (z ^ 2) >> 1, 2 + ((x ^ 2) >> 1))
+        else:
+            sent = jnp.where(odd == 0, 2 + ((x ^ s) >> 1), (z ^ s) >> 1)
+        mine = mine + lax.ppermute(taken(rows, sent, 0), "blk", second_pairs(s))
+    mine = (mine * grad_scale).reshape(SIDE, 2, ROWS, COLS)
     kept = taken(mine, core, 1)
     came = exchanged(taken(mine, core ^ 1, 1), "group", 1)
     both = jnp.where(core == 0, jnp.stack([kept, came], 1), jnp.stack([came, kept], 1))
@@ -139,8 +220,9 @@
         out_specs=in_vmem(2),
         out_shape=[
             jax.ShapeDtypeStruct((TOTAL, 128), jnp.float32),
-            jax.ShapeDtypeStruct((GROUPS, 2, ROWS, HALF), jnp.float32),
+            jax.ShapeDtypeStruct((GROUPS, ROWS, COLS), jnp.float32),
         ],
+        compiler_params=pltpu.CompilerParams(vmem_limit_bytes=4 << 20),
         name="gram",
     )(y.reshape(1).astype(jnp.int32), *blocks)
     sums = lax.all_to_all(sums, ("blk", "group"), split_axis=0, concat_axis=0, tiled=True)
@@ -150,6 +232,7 @@
             in_specs=in_vmem(4),
             out_specs=in_vmem(2),
             out_shape=[jax.ShapeDtypeStruct(weights.shape, jnp.float32)] * 2,
+            compiler_params=pltpu.CompilerParams(vmem_limit_bytes=4 << 20),
             name="finish",
         )(sums, ordered, weights, momentum)
     )

time: 97.5 us -> 83.9 us (0.86)
  Pallas kernels: 3.93 us -> 20.1 us
  matrix products: 12.9 us -> 0 us
  local copies, waits for them, and re-layouts: 6.52 us -> 0.14 us
  starting transfers between devices: 26.9 us -> 21.4 us
  waiting for transfers between devices: 25.5 us -> 20.5 us
    pallas_call x0 -> x3, Pallas kernels: none -> 18.7 us  [products(): pl.pallas_call(functools.partial(product_kernel, masks, depth, len(base)...]
    ppermute x16 -> x10, waiting for transfers between devices: 25.5 us -> 10.5 us  [exchanged(): lax.ppermute(value, axis, [(k, k ^ mask) for k in range(lax.axis_size(axi...]
    dot_general x1 -> x0, matrix products: 12.9 us -> none  [shards(): lax.dot_general(activations, grad_out, CONTRACT, preferred_element_type=j...]
    ppermute x16 -> x10, starting transfers between devices: 26.9 us -> 16 us  [exchanged(): lax.ppermute(value, axis, [(k, k ^ mask) for k in range(lax.axis_size(axi...]
    ppermute x0 -> x3, waiting for transfers between devices: none -> 9.99 us  [shards(): mine = mine + lax.ppermute(taken(rows, sent, 0), 'blk', second_pairs(s))]
    ppermute x0 -> x3, starting transfers between devices: none -> 5.44 us  [shards(): mine = mine + lax.ppermute(taken(rows, sent, 0), 'blk', second_pairs(s))]
    squeeze x5 -> x2, local copies, waits for them, and re-layouts: 4.26 us -> 0.1 us  [taken(): return lax.dynamic_index_in_dim(value, index, dim, keepdims=False)]
    slice x1 -> x0, local copies, waits for them, and re-layouts: 1.6 us -> none  [shards(): part_a = grad[:, :HALF].reshape(SIDE, SIDE, PIECE, HALF)]
  transfers between devices with their start and end apart: 16 -> 13, of which waited for: 8 -> 9; matrix products, arithmetic and copies ran while one was open for 5% -> 2% of each run, Pallas kernels for 0% -> 15%
where the time goes in v2:
time: 83.9 us; the launch traced here: 83.7 us
  starting transfers between devices  21.4 us (26%)
  waiting for transfers between devices  20.5 us (24%)
  Pallas kernels  20.1 us (24%)
  blocking collectives  17.2 us (21%)
  other arithmetic  3.56 us (4%)
    pallas_call x3, Pallas kernels, products(): pl.pallas_call(functools.partial(product_kernel, masks, depth, len(base)...  18.7 us
    all_to_all x1, blocking collectives, shards(): lax.all_to_all(sums, ('blk', 'group'), split_axis=0, concat_axis=0, tiled...  17.2 us
    ppermute x10, starting transfers between devices, exchanged(): lax.ppermute(value, axis, [(k, k ^ mask) for k in range(lax.axis_size(axi...  16 us
    ppermute x10, waiting for transfers between devices, exchanged(): lax.ppermute(value, axis, [(k, k ^ mask) for k in range(lax.axis_size(axi...  10.5 us
    ppermute x3, waiting for transfers between devices, shards(): mine = mine + lax.ppermute(taken(rows, sent, 0), 'blk', second_pairs(s))  9.99 us
    ppermute x3, starting transfers between devices, shards(): mine = mine + lax.ppermute(taken(rows, sent, 0), 'blk', second_pairs(s))  5.44 us
    add x2, other arithmetic, shards(): own + a + b  2.73 us
  transfers between devices with their start and end apart: 13, of which 9 were waited for; matrix products, arithmetic and copies ran while one was open for 2% of the time, Pallas kernels for 15%

profile of v2, /device:TPU:1, one launch (start us, length us, event | category | flops | bytes accessed | tf_op | source)
XLA Modules:
  0.0 83.7 jit_solution(2139031959456402685)
XLA Ops:
  0.7 0.7 pad_add_fusion.place_ref
  1.3 0.0 copy-start.2
  1.3 6.1 %products.3 = (f32[256,512]{1,0:T(8,128)}, f32[256,512]{1,0:T(8,128)}) custom-call(s32[2]{0:T(128)} %pad_add_fusion.place_ref, bf16[4096,2048]{1,0:T(8,128)(2,1)} %act_ref.5, bf16[4096,512]{1,0:T(8,128)(2,1)} %out_ref.5), custom_call_target="tpu_custom_call" | custom-call | flops 1000 | bytes 1000 | tf_op jit(solution)/shard_map/products/pallas_call | solution.py:82
  7.4 3.7 %collective-permute-start = (f32[256,512]{1,0:T(8,128)}, f32[256,512]{1,0:T(8,128)S(1)}, u32[]{:S(2)}, u32[]{:S(2)}) collective-permute-start(f32[256,512]{1,0:T(8,128)} %get-tuple-element.14), channel_id=1, source_target_pairs={{0,64},{8,72},{16,80},{24,88},{32,96},{40,104},{48,112},{56,120},{... | collective-permute-start | bytes 1572872 | tf_op jit(solution)/shard_map/ppermute | solution.py:23
  11.0 3.6 %collective-permute-start.1 = (f32[256,512]{1,0:T(8,128)}, f32[256,512]{1,0:T(8,128)S(1)}, u32[]{:S(2)}, u32[]{:S(2)}) collective-permute-start(f32[256,512]{1,0:T(8,128)} %get-tuple-element.15), channel_id=1, source_target_pairs={{0,16},{8,24},{16,0},{24,8},{32,48},{40,56},{48,32},{56,40},{64,80... | collective-permute-start | bytes 1572872 | tf_op jit(solution)/shard_map/ppermute | solution.py:23
  14.6 0.0 copy-done.2
  14.6 7.7 %products.4 = (f32[256,512]{1,0:T(8,128)}, f32[256,512]{1,0:T(8,128)S(1)}, f32[256,512]{1,0:T(8,128)S(1)}, f32[256,512]{1,0:T(8,128)S(1)}) custom-call(s32[2]{0:T(128)S(1)} %copy-done.2, bf16[4096,2048]{1,0:T(8,128)(2,1)} %act_ref.5, bf16[4096,512]{1,0:T(8,128)(2,1)} %out_ref.5), custom_call_target="tpu_custom_call" | custom-call | flops 1000 | bytes 1000 | tf_op jit(solution)/shard_map/products/pallas_call | solution.py:82
  22.4 0.0 copy-start
  22.4 0.0 copy-start.1
  22.4 0.4 collective-permute-start.2
  22.8 0.6 collective-permute-start.3
  23.4 0.7 collective-permute-start.4
  24.2 0.0 collective-permute-done.refs_0_
  24.2 2.4 %collective-permute-start.5 = (f32[256,512]{1,0:T(8,128)S(1)}, f32[256,512]{1,0:T(8,128)}, u32[]{:S(2)}, u32[]{:S(2)}) collective-permute-start(f32[256,512]{1,0:T(8,128)S(1)} %get-tuple-element.20), channel_id=1, source_target_pairs={{0,24},{8,16},{16,8},{24,0},{32,56},{40,48},{48,40},{56,32},{64,88... | collective-permute-start | bytes 1572872 | tf_op jit(solution)/shard_map/ppermute | solution.py:23
  26.6 0.0 collective-permute-done.1.refs_1_
  26.6 4.9 %products.5 = (f32[256,512]{1,0:T(8,128)S(1)}, f32[256,512]{1,0:T(8,128)S(1)}) custom-call(s32[2]{0:T(128)S(1)} %copy-done.2, bf16[4096,2048]{1,0:T(8,128)(2,1)} %act_ref.5, bf16[4096,512]{1,0:T(8,128)(2,1)} %out_ref.5, f32[256,512]{1,0:T(8,128)S(1)} %collective-permute-done.refs_0_, f32[256,512]{1,0:T(8,128)S(1)} %collective-permute-done.1.refs_1_), custom_call_target="tpu_custom_call" | custom-call | flops 1000 | bytes 1000 | tf_op jit(solution)/shard_map/products/pallas_call | solution.py:82
  31.5 3.5 %collective-permute-done.2 = f32[256,512]{1,0:T(8,128)} collective-permute-done((f32[256,512]{1,0:T(8,128)}, f32[256,512]{1,0:T(8,128)}, u32[]{:S(2)}, u32[]{:S(2)}) %collective-permute-start.2) | collective-permute-done | bytes 524320 | tf_op jit(solution)/shard_map/ppermute | solution.py:23
  35.0 1.0 %collective-permute-done.3 = f32[256,512]{1,0:T(8,128)} collective-permute-done((f32[256,512]{1,0:T(8,128)S(1)}, f32[256,512]{1,0:T(8,128)}, u32[]{:S(2)}, u32[]{:S(2)}) %collective-permute-start.3) | collective-permute-done | bytes 524320 | tf_op jit(solution)/shard_map/ppermute | solution.py:23
  36.0 1.4 %add_add_fusion.1 = f32[256,512]{1,0:T(8,128)S(1)} fusion(f32[256,512]{1,0:T(8,128)} %collective-permute-done.3, f32[256,512]{1,0:T(8,128)S(1)} %get-tuple-element.22, f32[256,512]{1,0:T(8,128)} %collective-permute-done.2), kind=kLoop, calls=%fused_computation.2 | loop fusion | flops 262144 | bytes 2097152 | tf_op jit(solution)/shard_map/add | solution.py:200
  37.4 0.6 collective-permute-done.4
  37.9 0.0 collective-permute-done.5
  37.9 1.4 %add_add_fusion = f32[256,512]{1,0:T(8,128)S(1)} fusion(f32[256,512]{1,0:T(8,128)} %collective-permute-done.5, f32[256,512]{1,0:T(8,128)S(1)} %get-tuple-element.23, f32[256,512]{1,0:T(8,128)} %collective-permute-done.4), kind=kLoop, calls=%fused_computation.1 | loop fusion | flops 262144 | bytes 2097152 | tf_op jit(solution)/shard_map/add | solution.py:200
  39.3 0.1 pad_maximum_fusion
  39.4 0.1 dynamic-slice_bitcast_fusion.2
  39.5 2.0 %collective-permute-start.6 = (f32[128,512]{1,0:T(8,128)S(1)}, f32[128,512]{1,0:T(8,128)S(1)}, u32[]{:S(2)}, u32[]{:S(2)}) collective-permute-start(f32[128,512]{1,0:T(8,128)S(1)} %get-tuple-element.26), channel_id=1, source_target_pairs={{0,16},{8,72},{16,0},{24,88},{32,96},{40,56},{48,112},{56,40},{64,... | collective-permute-start | bytes 786440 | tf_op jit(solution)/shard_map/ppermute | solution.py:209
  41.5 0.0 collective-permute-start.7
  41.5 3.4 %collective-permute-start.8 = (f32[128,512]{1,0:T(8,128)S(1)}, f32[128,512]{1,0:T(8,128)S(1)}, u32[]{:S(2)}, u32[]{:S(2)}) collective-permute-start(f32[128,512]{1,0:T(8,128)S(1)} %get-tuple-element.27), channel_id=1, source_target_pairs={{0,96},{8,16},{16,112},{24,0},{32,56},{40,72},{48,40},{56,88},{64,... | collective-permute-start | bytes 786440 | tf_op jit(solution)/shard_map/ppermute | solution.py:209
  44.9 2.0 %collective-permute-done.6 = f32[128,512]{1,0:T(8,128)S(1)} collective-permute-done((f32[128,512]{1,0:T(8,128)S(1)}, f32[128,512]{1,0:T(8,128)S(1)}, u32[]{:S(2)}, u32[]{:S(2)}) %collective-permute-start.6) | collective-permute-done | bytes 262176 | tf_op jit(solution)/shard_map/ppermute | solution.py:209
  46.9 0.1 collective-permute-done.7
  47.0 7.9 %collective-permute-done.8 = f32[128,512]{1,0:T(8,128)S(1)} collective-permute-done((f32[128,512]{1,0:T(8,128)S(1)}, f32[128,512]{1,0:T(8,128)S(1)}, u32[]{:S(2)}, u32[]{:S(2)}) %collective-permute-start.8) | collective-permute-done | bytes 262176 | tf_op jit(solution)/shard_map/ppermute | solution.py:209
  54.9 0.1 fusion.2
  55.0 0.6 collective-permute-start.9
  55.6 1.0 %collective-permute-done.9 = f32[4,16,512]{2,1,0:T(8,128)S(1)} collective-permute-done((f32[4,16,512]{2,1,0:T(8,128)S(1)}, f32[4,16,512]{2,1,0:T(8,128)S(1)}, u32[]{:S(2)}, u32[]{:S(2)}) %collective-permute-start.9) | collective-permute-done | bytes 131104 | tf_op jit(solution)/shard_map/ppermute | solution.py:23
  56.6 1.4 %collective-permute-start.10 = (f32[2,16,512]{2,1,0:T(8,128)S(1)}, f32[2,16,512]{2,1,0:T(8,128)S(1)}, u32[]{:S(2)}, u32[]{:S(2)}) collective-permute-start(f32[2,16,512]{2,1,0:T(8,128)S(1)} %get-tuple-element.31), channel_id=1, source_target_pairs={{0,2},{1,3},{2,0},{3,1},{4,6},{5,7},{6,4},{7,5},{8,10},{9,11},{10,... | collective-permute-start | bytes 196616 | tf_op jit(solution)/shard_map/ppermute | solution.py:23
  58.0 2.6 %collective-permute-start.11 = (f32[2,16,512]{2,1,0:T(8,128)S(1)}, f32[2,16,512]{2,1,0:T(8,128)S(1)}, u32[]{:S(2)}, u32[]{:S(2)}) collective-permute-start(f32[2,16,512]{2,1,0:T(8,128)S(1)} %get-tuple-element.30), channel_id=1, source_target_pairs={{0,4},{1,5},{2,6},{3,7},{4,0},{5,1},{6,2},{7,3},{8,12},{9,13},{10,... | collective-permute-start | bytes 196616 | tf_op jit(solution)/shard_map/ppermute | solution.py:23
  60.6 0.0 collective-permute-start.12
  60.6 0.0 collective-permute-done.10.refs_1_
  60.6 3.0 %collective-permute-done.11.refs_2_ = f32[2,16,512]{2,1,0:T(8,128)S(1)} collective-permute-done((f32[2,16,512]{2,1,0:T(8,128)S(1)}, f32[2,16,512]{2,1,0:T(8,128)S(1)}, u32[]{:S(2)}, u32[]{:S(2)}) %collective-permute-start.11) | collective-permute-done | bytes 65568 | tf_op jit(solution)/shard_map/ppermute | solution.py:23
  63.6 1.5 %collective-permute-done.12.refs_3_ = f32[2,16,512]{2,1,0:T(8,128)S(1)} collective-permute-done((f32[2,16,512]{2,1,0:T(8,128)S(1)}, f32[2,16,512]{2,1,0:T(8,128)S(1)}, u32[]{:S(2)}, u32[]{:S(2)}) %collective-permute-start.12) | collective-permute-done | bytes 65568 | tf_op jit(solution)/shard_map/ppermute | solution.py:23
  65.1 0.3 gram.1
  65.4 17.2 %all_to_all.11 = f32[128,1,128]{2,1,0:T(1,128)S(1)} all-to-all(f32[128,1,128]{2,1,0:T(1,128)S(1)} %bitcast.35), channel_id=1, replica_groups=mesh['blk'=16,'group'=8] {'blk','group'}, dimensions={0} | all-to-all | bytes 131072 | tf_op jit(solution)/shard_map/all_to_all | solution.py:228
  82.7 0.0 copy-done
  82.7 0.0 copy-done.1
  82.7 1.1 %finish.1 = (f32[16,512]{1,0:T(8,128)}, f32[16,512]{1,0:T(8,128)}) custom-call(f32[128,128]{1,0:T(8,128)S(1)} %bitcast.34, f32[8,16,512]{2,1,0:T(8,128)S(1)} %get-tuple-element.25.ordered_ref, f32[16,512]{1,0:T(8,128)S(1)} %copy-done, f32[16,512]{1,0:T(8,128)S(1)} %copy-done.1), custom_call_target="tpu_custom_call" | custom-call | tf_op jit(solution)/shard_map/finish/pallas_call | solution.py:230
  (3 shorter events, 0.1 us)
Async XLA Ops:
  1.3 13.3 %copy-start.2 = (s32[2]{0:T(128)S(1)}, s32[2]{0:T(128)}, u32[]{:S(2)}) copy-start(s32[2]{0:T(128)} %pad_add_fusion.place_ref) | copy-start | bytes 28
  7.4 16.8 %collective-permute-start = (f32[256,512]{1,0:T(8,128)}, f32[256,512]{1,0:T(8,128)S(1)}, u32[]{:S(2)}, u32[]{:S(2)}) collective-permute-start(f32[256,512]{1,0:T(8,128)} %get-tuple-element.14), channel_id=1, source_target_pairs={{0,64},{8,72},{16,80},{24,88},{32,96},{40,104},{48,112},{56,120},{... | collective-permute-start | bytes 1572872 | tf_op jit(solution)/shard_map/ppermute | solution.py:23
  11.0 15.5 %collective-permute-start.1 = (f32[256,512]{1,0:T(8,128)}, f32[256,512]{1,0:T(8,128)S(1)}, u32[]{:S(2)}, u32[]{:S(2)}) collective-permute-start(f32[256,512]{1,0:T(8,128)} %get-tuple-element.15), channel_id=1, source_target_pairs={{0,16},{8,24},{16,0},{24,8},{32,48},{40,56},{48,32},{56,40},{64,80... | collective-permute-start | bytes 1572872 | tf_op jit(solution)/shard_map/ppermute | solution.py:23
  22.4 60.3 %copy-start = (f32[16,512]{1,0:T(8,128)S(1)}, f32[16,512]{1,0:T(8,128)}, u32[]{:S(2)}) copy-start(f32[16,512]{1,0:T(8,128)} %weights_ref.1) | copy-start | bytes 98308
  22.4 60.3 %copy-start.1 = (f32[16,512]{1,0:T(8,128)S(1)}, f32[16,512]{1,0:T(8,128)}, u32[]{:S(2)}) copy-start(f32[16,512]{1,0:T(8,128)} %momentum_ref.1) | copy-start | bytes 98308
  22.4 12.6 %collective-permute-start.2 = (f32[256,512]{1,0:T(8,128)}, f32[256,512]{1,0:T(8,128)}, u32[]{:S(2)}, u32[]{:S(2)}) collective-permute-start(f32[256,512]{1,0:T(8,128)} %get-tuple-element.17), channel_id=1, source_target_pairs={{0,32},{8,40},{16,48},{24,56},{32,0},{40,8},{48,16},{56,24},{64,96... | collective-permute-start | bytes 1572872 | tf_op jit(solution)/shard_map/ppermute | solution.py:23
  22.8 13.2 %collective-permute-start.3 = (f32[256,512]{1,0:T(8,128)S(1)}, f32[256,512]{1,0:T(8,128)}, u32[]{:S(2)}, u32[]{:S(2)}) collective-permute-start(f32[256,512]{1,0:T(8,128)S(1)} %get-tuple-element.19), channel_id=1, source_target_pairs={{0,96},{8,104},{16,112},{24,120},{32,64},{40,72},{48,80},{56,88},{... | collective-permute-start | bytes 1572872 | tf_op jit(solution)/shard_map/ppermute | solution.py:23
  23.4 14.5 %collective-permute-start.4 = (f32[256,512]{1,0:T(8,128)S(1)}, f32[256,512]{1,0:T(8,128)}, u32[]{:S(2)}, u32[]{:S(2)}) collective-permute-start(f32[256,512]{1,0:T(8,128)S(1)} %get-tuple-element.18), channel_id=1, source_target_pairs={{0,8},{8,0},{16,24},{24,16},{32,40},{40,32},{48,56},{56,48},{64,72... | collective-permute-start | bytes 1572872 | tf_op jit(solution)/shard_map/ppermute | solution.py:23
  24.2 13.8 %collective-permute-start.5 = (f32[256,512]{1,0:T(8,128)S(1)}, f32[256,512]{1,0:T(8,128)}, u32[]{:S(2)}, u32[]{:S(2)}) collective-permute-start(f32[256,512]{1,0:T(8,128)S(1)} %get-tuple-element.20), channel_id=1, source_target_pairs={{0,24},{8,16},{16,8},{24,0},{32,56},{40,48},{48,40},{56,32},{64,88... | collective-permute-start | bytes 1572872 | tf_op jit(solution)/shard_map/ppermute | solution.py:23
  39.5 7.4 %collective-permute-start.6 = (f32[128,512]{1,0:T(8,128)S(1)}, f32[128,512]{1,0:T(8,128)S(1)}, u32[]{:S(2)}, u32[]{:S(2)}) collective-permute-start(f32[128,512]{1,0:T(8,128)S(1)} %get-tuple-element.26), channel_id=1, source_target_pairs={{0,16},{8,72},{16,0},{24,88},{32,96},{40,56},{48,112},{56,40},{64,... | collective-permute-start | bytes 786440 | tf_op jit(solution)/shard_map/ppermute | solution.py:209
  41.5 5.5 %collective-permute-start.7 = (f32[128,512]{1,0:T(8,128)S(1)}, f32[128,512]{1,0:T(8,128)S(1)}, u32[]{:S(2)}, u32[]{:S(2)}) collective-permute-start(f32[128,512]{1,0:T(8,128)S(1)} %get-tuple-element.28), channel_id=1, source_target_pairs={{0,32},{8,0},{16,48},{24,16},{32,40},{40,8},{48,56},{56,24},{64,96... | collective-permute-start | bytes 786440 | tf_op jit(solution)/shard_map/ppermute | solution.py:209
  41.5 13.4 %collective-permute-start.8 = (f32[128,512]{1,0:T(8,128)S(1)}, f32[128,512]{1,0:T(8,128)S(1)}, u32[]{:S(2)}, u32[]{:S(2)}) collective-permute-start(f32[128,512]{1,0:T(8,128)S(1)} %get-tuple-element.27), channel_id=1, source_target_pairs={{0,96},{8,16},{16,112},{24,0},{32,56},{40,72},{48,40},{56,88},{64,... | collective-permute-start | bytes 786440 | tf_op jit(solution)/shard_map/ppermute | solution.py:209
  55.0 1.6 %collective-permute-start.9 = (f32[4,16,512]{2,1,0:T(8,128)S(1)}, f32[4,16,512]{2,1,0:T(8,128)S(1)}, u32[]{:S(2)}, u32[]{:S(2)}) collective-permute-start(f32[4,16,512]{2,1,0:T(8,128)S(1)} %get-tuple-element.34), channel_id=1, source_target_pairs={{0,1},{1,0},{2,3},{3,2},{4,5},{5,4},{6,7},{7,6},{8,9},{9,8},{10,11... | collective-permute-start | bytes 393224 | tf_op jit(solution)/shard_map/ppermute | solution.py:23
  56.6 4.0 %collective-permute-start.10 = (f32[2,16,512]{2,1,0:T(8,128)S(1)}, f32[2,16,512]{2,1,0:T(8,128)S(1)}, u32[]{:S(2)}, u32[]{:S(2)}) collective-permute-start(f32[2,16,512]{2,1,0:T(8,128)S(1)} %get-tuple-element.31), channel_id=1, source_target_pairs={{0,2},{1,3},{2,0},{3,1},{4,6},{5,7},{6,4},{7,5},{8,10},{9,11},{10,... | collective-permute-start | bytes 196616 | tf_op jit(solution)/shard_map/ppermute | solution.py:23
  58.0 5.6 %collective-permute-start.11 = (f32[2,16,512]{2,1,0:T(8,128)S(1)}, f32[2,16,512]{2,1,0:T(8,128)S(1)}, u32[]{:S(2)}, u32[]{:S(2)}) collective-permute-start(f32[2,16,512]{2,1,0:T(8,128)S(1)} %get-tuple-element.30), channel_id=1, source_target_pairs={{0,4},{1,5},{2,6},{3,7},{4,0},{5,1},{6,2},{7,3},{8,12},{9,13},{10,... | collective-permute-start | bytes 196616 | tf_op jit(solution)/shard_map/ppermute | solution.py:23
  60.6 4.5 %collective-permute-start.12 = (f32[2,16,512]{2,1,0:T(8,128)S(1)}, f32[2,16,512]{2,1,0:T(8,128)S(1)}, u32[]{:S(2)}, u32[]{:S(2)}) collective-permute-start(f32[2,16,512]{2,1,0:T(8,128)S(1)} %get-tuple-element.29), channel_id=1, source_target_pairs={{0,6},{1,7},{2,4},{3,5},{4,2},{5,3},{6,0},{7,1},{8,14},{9,15},{10,... | collective-permute-start | bytes 196616 | tf_op jit(solution)/shard_map/ppermute | solution.py:23

commit v3 on v2

--- a/solution.py
+++ b/solution.py
@@ -14,7 +14,7 @@
 ROWS = 16
 COLS = 512
 PIECE = GROUPS * ROWS
-DEPTH = 1024
+DEPTH = 512
 TOTAL = 128
 CONTRACT = (((0,), (0,)), ((), ()))
 
@@ -27,18 +27,24 @@
     return [pl.BlockSpec(memory_space=pltpu.VMEM)] * count
 
 
-def piece_blocks(x, z, s):
-    along_x = [(x ^ s) * SIDE + ((x ^ s) & 1) + 2 * k for k in range(2)]
-    along_z = [((((z ^ s) & 1) ^ 1) + 2 * k) * SIDE + (z ^ s) for k in range(2)]
+def my_place():
+    blk, group = lax.axis_index("blk"), lax.axis_index("group")
+    return blk // SIDE, blk % SIDE, group % 2
+
+
+def piece_blocks(s):
+    x, z, core = my_place()
+    along_x = [(x ^ s) * SIDE + ((x ^ s ^ core) & 1) + 2 * k for k in range(2)]
+    along_z = [(((z ^ s ^ core ^ 1) & 1) + 2 * k) * SIDE + (z ^ s) for k in range(2)]
     return along_x + along_z
 
 
-def product_kernel(masks, depth, added, place_ref, act_ref, out_ref, *refs):
+def product_kernel(masks, depth, added, act_ref, out_ref, *refs):
     base_refs, refs = refs[: 2 * added], refs[2 * added :]
     pieces = refs[: 2 * len(masks)]
     held, grad, sems = refs[2 * len(masks) :]
     chunks = out_ref.shape[0] // depth
-    blocks = [piece_blocks(place_ref[0], place_ref[1], s) for s in masks]
+    blocks = [piece_blocks(s) for s in masks]
 
     def copies(k):
         rows = pl.ds(k * depth, depth)
@@ -76,13 +82,12 @@
                     piece[...] = mine
 
 
-def products(activations, grad_out, place, masks, depth, vmem, base=()):
+def products(activations, grad_out, masks, depth, vmem, base=()):
     tokens, cols = grad_out.shape
     count = 2 * len(masks)
     return pl.pallas_call(
         functools.partial(product_kernel, masks, depth, len(base) // 2),
-        in_specs=[pl.BlockSpec(memory_space=pltpu.SMEM)]
-        + [pl.BlockSpec(memory_space=pl.ANY)] * 2
+        in_specs=[pl.BlockSpec(memory_space=pl.ANY)] * 2
         + in_vmem(len(base)),
         out_specs=in_vmem(count),
         out_shape=[jax.ShapeDtypeStruct((2 * PIECE, cols), jnp.float32)] * count,
@@ -94,7 +99,34 @@
         compiler_params=pltpu.CompilerParams(vmem_limit_bytes=vmem << 20),
         cost_estimate=pl.CostEstimate(flops=1000, bytes_accessed=1000, transcendentals=0),
         name="products",
-    )(place, activations, grad_out, *base)
+    )(activations, grad_out, *base)
+
+
+def summed_kernel(*refs):
+    ways, out_refs = (refs[:3], refs[3:6]), refs[6:]
+    x, z, core = my_place()
+    along_x = ((x ^ z ^ core) & 1) == 1
+    for out_ref, s in zip(out_refs, (0, 2, 1, 3)):
+        from_first = jnp.logical_xor(along_x, s % 2 == 0)
+        for way, place in enumerate((z ^ s, x ^ s)):
+
+            @pl.when(from_first if way == 0 else jnp.logical_not(from_first))
+            def _(way=way, place=place):
+                rows = pl.ds(pl.multiple_of((place >> 1) * PIECE, PIECE), PIECE)
+                own, one, three = ways[way]
+                out_ref[...] = own[rows] + (one[rows] + three[rows])
+
+
+def summed(kept, first, third):
+    operands = [value for trio in zip(kept, first, third) for value in trio]
+    return pl.pallas_call(
+        summed_kernel,
+        in_specs=in_vmem(6),
+        out_specs=in_vmem(4),
+        out_shape=[jax.ShapeDtypeStruct((PIECE, COLS), jnp.float32)] * 4,
+        compiler_params=pltpu.CompilerParams(vmem_limit_bytes=8 << 20),
+        name="summed",
+    )(*operands)
 
 
 def pair_slots():
@@ -168,20 +200,17 @@
 
 def second_pairs(s):
     pairs = []
-    for k in range(SIDE * SIDE):
-        x, z = k // SIDE, k % SIDE
-        along_z = ((x ^ z) & 1 == 0) == (s == 2)
-        pairs.append((k, k ^ s if along_z else k ^ (SIDE * s)))
+    for k in range(TOTAL):
+        blk, core = k // GROUPS, k % 2
+        along_z = ((blk // SIDE ^ blk ^ core) & 1 == 0) == (s == 2)
+        pairs.append((k, k ^ (GROUPS * (s if along_z else SIDE * s))))
     return pairs
 
 
 def shards(activations, grad_out, weights, momentum):
-    blk = lax.axis_index("blk")
     group = lax.axis_index("group")
-    x, z = blk // SIDE, blk % SIDE
     y, core = group // 2, group % 2
     grad_scale = 1.0 / math.sqrt(activations.shape[0] * lax.axis_size("blk"))
-    place = jnp.stack([x, z]).astype(jnp.int32)
 
     def taken(value, index, dim):
         return lax.dynamic_index_in_dim(value, index, dim, keepdims=False)
@@ -189,24 +218,16 @@
     def both_ways(pair, s):
         return [exchanged(pair[0], "blk", SIDE * s), exchanged(pair[1], "blk", s)]
 
-    far = products(activations, grad_out, place, (2,), DEPTH, 62)
+    far = products(activations, grad_out, (2,), DEPTH, 62)
     far_came = both_ways(far, 2)
-    place, far = lax.optimization_barrier((place, far))
-    near = products(activations, grad_out, place, (1, 3), DEPTH, 50)
+    grad_out, far = lax.optimization_barrier((grad_out, far))
+    near = products(activations, grad_out, (1, 3), DEPTH, 50)
     near_came = both_ways(near[:2], 1), both_ways(near[2:], 3)
-    place, near = lax.optimization_barrier((place, near))
-    kept = products(activations, grad_out, place, (0,), DEPTH, 50, far_came)
-    rows = jnp.concatenate(
-        [own + a + b for own, a, b in zip(kept, *near_came)], axis=0
-    ).reshape(4, PIECE, COLS)
-    odd = (x ^ z) & 1
-    mine = taken(rows, jnp.where(odd == 0, z >> 1, 2 + (x >> 1)), 0)
-    for s in (2, 1, 3):
-        if s == 2:
-            sent = jnp.where(odd == 0, (z ^ 2) >> 1, 2 + ((x ^ 2) >> 1))
-        else:
-            sent = jnp.where(odd == 0, 2 + ((x ^ s) >> 1), (z ^ s) >> 1)
-        mine = mine + lax.ppermute(taken(rows, sent, 0), "blk", second_pairs(s))
+    grad_out, near = lax.optimization_barrier((grad_out, near))
+    kept = products(activations, grad_out, (0,), DEPTH, 50, far_came)
+    mine, *sent = summed(kept, *near_came)
+    for value, s in zip(sent, (2, 1, 3)):
+        mine = mine + lax.ppermute(value, ("blk", "group"), second_pairs(s))
     mine = (mine * grad_scale).reshape(SIDE, 2, ROWS, COLS)
     kept = taken(mine, core, 1)
     came = exchanged(taken(mine, core ^ 1, 1), "group", 1)

time: 83.9 us -> 78 us (0.930)
  other arithmetic: 3.56 us -> 0.11 us
  starting transfers between devices: 21.4 us -> 24.6 us
  waiting for transfers between devices: 20.5 us -> 17.8 us
  blocking collectives: 17.2 us -> 15.8 us
  Pallas kernels: 20.1 us -> 18.8 us
    ppermute x10, starting transfers between devices: 16 us -> 20.4 us  [exchanged(): lax.ppermute(value, axis, [(k, k ^ mask) for k in range(lax.axis_size(axi...]
    ppermute x3, waiting for transfers between devices: 9.99 us -> 5.75 us  [shards(): mine = mine + lax.ppermute(value, ('blk', 'group'), second_pairs(s))]
    add x2 -> x0, other arithmetic: 2.73 us -> none  [shards(): own + a + b]
    pallas_call x3, Pallas kernels: 18.7 us -> 17.2 us  [products(): pl.pallas_call(functools.partial(product_kernel, masks, depth, len(base)...]
    ppermute x10, waiting for transfers between devices: 10.5 us -> 12.1 us  [exchanged(): lax.ppermute(value, axis, [(k, k ^ mask) for k in range(lax.axis_size(axi...]
    all_to_all x1, blocking collectives: 17.2 us -> 15.8 us  [shards(): lax.all_to_all(sums, ('blk', 'group'), split_axis=0, concat_axis=0, tiled...]
    ppermute x3, starting transfers between devices: 5.44 us -> 4.16 us  [shards(): mine = mine + lax.ppermute(value, ('blk', 'group'), second_pairs(s))]
  transfers between devices with their start and end apart: 13 -> 13, of which waited for: 9 -> 8; matrix products, arithmetic and copies ran while one was open for 2% -> 0% of each run, Pallas kernels for 15% -> 15%
where the time goes in v3:
time: 78 us; the launch traced here: 77.8 us
  starting transfers between devices  24.6 us (32%)
  Pallas kernels  18.8 us (24%)
  waiting for transfers between devices  17.8 us (23%)
  blocking collectives  15.8 us (20%)
    ppermute x10, starting transfers between devices, exchanged(): lax.ppermute(value, axis, [(k, k ^ mask) for k in range(lax.axis_size(axi...  20.4 us
    pallas_call x3, Pallas kernels, products(): pl.pallas_call(functools.partial(product_kernel, masks, depth, len(base)...  17.2 us
    all_to_all x1, blocking collectives, shards(): lax.all_to_all(sums, ('blk', 'group'), split_axis=0, concat_axis=0, tiled...  15.8 us
    ppermute x10, waiting for transfers between devices, exchanged(): lax.ppermute(value, axis, [(k, k ^ mask) for k in range(lax.axis_size(axi...  12.1 us
    ppermute x3, waiting for transfers between devices, shards(): mine = mine + lax.ppermute(value, ('blk', 'group'), second_pairs(s))  5.75 us
    ppermute x3, starting transfers between devices, shards(): mine = mine + lax.ppermute(value, ('blk', 'group'), second_pairs(s))  4.16 us
  transfers between devices with their start and end apart: 13, of which 8 were waited for; matrix products, arithmetic and copies ran while one was open for 0% of the time, Pallas kernels for 15%

profile of v3, /device:TPU:1, one launch (start us, length us, event | category | flops | bytes accessed | tf_op | source)
XLA Modules:
  0.0 77.8 jit_solution(7459419931045559788)
XLA Ops:
  0.6 5.4 %products.3 = (f32[256,512]{1,0:T(8,128)}, f32[256,512]{1,0:T(8,128)}) custom-call(bf16[4096,2048]{1,0:T(8,128)(2,1)} %act_ref.5, bf16[4096,512]{1,0:T(8,128)(2,1)} %out_ref.3), custom_call_target="tpu_custom_call" | custom-call | flops 1000 | bytes 1000 | tf_op jit(solution)/shard_map/products/pallas_call | solution.py:88
  6.1 3.7 %collective-permute-start = (f32[256,512]{1,0:T(8,128)}, f32[256,512]{1,0:T(8,128)S(1)}, u32[]{:S(2)}, u32[]{:S(2)}) collective-permute-start(f32[256,512]{1,0:T(8,128)} %get-tuple-element.18), channel_id=1, source_target_pairs={{0,64},{8,72},{16,80},{24,88},{32,96},{40,104},{48,112},{56,120},{... | collective-permute-start | bytes 1572872 | tf_op jit(solution)/shard_map/ppermute | solution.py:23
  9.7 3.6 %collective-permute-start.1 = (f32[256,512]{1,0:T(8,128)}, f32[256,512]{1,0:T(8,128)S(1)}, u32[]{:S(2)}, u32[]{:S(2)}) collective-permute-start(f32[256,512]{1,0:T(8,128)} %get-tuple-element.19), channel_id=1, source_target_pairs={{0,16},{8,24},{16,0},{24,8},{32,48},{40,56},{48,32},{56,40},{64,80... | collective-permute-start | bytes 1572872 | tf_op jit(solution)/shard_map/ppermute | solution.py:23
  13.3 7.1 %products.4 = (f32[256,512]{1,0:T(8,128)S(1)}, f32[256,512]{1,0:T(8,128)S(1)}, f32[256,512]{1,0:T(8,128)S(1)}, f32[256,512]{1,0:T(8,128)S(1)}) custom-call(bf16[4096,2048]{1,0:T(8,128)(2,1)} %act_ref.5, bf16[4096,512]{1,0:T(8,128)(2,1)} %out_ref.3), custom_call_target="tpu_custom_call" | custom-call | flops 1000 | bytes 1000 | tf_op jit(solution)/shard_map/products/pallas_call | solution.py:88
  20.5 0.0 copy-start
  20.5 0.0 copy-start.1
  20.5 0.4 collective-permute-start.2
  20.9 0.6 collective-permute-start.3
  21.5 0.8 collective-permute-start.4
  22.3 0.0 collective-permute-done.refs_0_
  22.3 3.0 %collective-permute-start.5 = (f32[256,512]{1,0:T(8,128)S(1)}, f32[256,512]{1,0:T(8,128)S(1)}, u32[]{:S(2)}, u32[]{:S(2)}) collective-permute-start(f32[256,512]{1,0:T(8,128)S(1)} %get-tuple-element.24), channel_id=1, source_target_pairs={{0,24},{8,16},{16,8},{24,0},{32,56},{40,48},{48,40},{56,32},{64,88... | collective-permute-start | bytes 1572872 | tf_op jit(solution)/shard_map/ppermute | solution.py:23
  25.3 0.0 collective-permute-done.1.refs_1_
  25.3 4.6 %products.5 = (f32[256,512]{1,0:T(8,128)S(1)}, f32[256,512]{1,0:T(8,128)S(1)}) custom-call(bf16[4096,2048]{1,0:T(8,128)(2,1)} %act_ref.5, bf16[4096,512]{1,0:T(8,128)(2,1)} %out_ref.3, f32[256,512]{1,0:T(8,128)S(1)} %collective-permute-done.refs_0_, f32[256,512]{1,0:T(8,128)S(1)} %collective-permute-done.1.refs_1_), custom_call_target="tpu_custom_call" | custom-call | flops 1000 | bytes 1000 | tf_op jit(solution)/shard_map/products/pallas_call | solution.py:88
  29.9 2.9 %collective-permute-done.2.refs_1_ = f32[256,512]{1,0:T(8,128)S(1)} collective-permute-done((f32[256,512]{1,0:T(8,128)S(1)}, f32[256,512]{1,0:T(8,128)S(1)}, u32[]{:S(2)}, u32[]{:S(2)}) %collective-permute-start.2) | collective-permute-done | bytes 524320 | tf_op jit(solution)/shard_map/ppermute | solution.py:23
  32.8 1.3 %collective-permute-done.3.refs_2_ = f32[256,512]{1,0:T(8,128)S(1)} collective-permute-done((f32[256,512]{1,0:T(8,128)S(1)}, f32[256,512]{1,0:T(8,128)S(1)}, u32[]{:S(2)}, u32[]{:S(2)}) %collective-permute-start.3) | collective-permute-done | bytes 524320 | tf_op jit(solution)/shard_map/ppermute | solution.py:23
  34.0 2.4 %collective-permute-done.4.refs_4_ = f32[256,512]{1,0:T(8,128)S(1)} collective-permute-done((f32[256,512]{1,0:T(8,128)S(1)}, f32[256,512]{1,0:T(8,128)S(1)}, u32[]{:S(2)}, u32[]{:S(2)}) %collective-permute-start.4) | collective-permute-done | bytes 524320 | tf_op jit(solution)/shard_map/ppermute | solution.py:23
  36.5 0.0 collective-permute-done.5.refs_5_
  36.5 0.2 summed.1
  36.7 1.1 %collective-permute-start.6 = (f32[128,512]{1,0:T(8,128)S(1)}, f32[128,512]{1,0:T(8,128)S(1)}, u32[]{:S(2)}, u32[]{:S(2)}) collective-permute-start(f32[128,512]{1,0:T(8,128)S(1)} %get-tuple-element.29), channel_id=1, source_target_pairs={{0,16},{1,65},{2,18},{3,67},{4,20},{5,69},{6,22},{7,71},{8,72},{9,... | collective-permute-start | bytes 786440 | tf_op jit(solution)/shard_map/ppermute | solution.py:230
  37.8 1.7 %collective-permute-start.7 = (f32[128,512]{1,0:T(8,128)S(1)}, f32[128,512]{1,0:T(8,128)S(1)}, u32[]{:S(2)}, u32[]{:S(2)}) collective-permute-start(f32[128,512]{1,0:T(8,128)S(1)} %get-tuple-element.30), channel_id=1, source_target_pairs={{0,32},{1,9},{2,34},{3,11},{4,36},{5,13},{6,38},{7,15},{8,0},{9,41... | collective-permute-start | bytes 786440 | tf_op jit(solution)/shard_map/ppermute | solution.py:230
  39.5 1.3 %collective-permute-start.8 = (f32[128,512]{1,0:T(8,128)S(1)}, f32[128,512]{1,0:T(8,128)S(1)}, u32[]{:S(2)}, u32[]{:S(2)}) collective-permute-start(f32[128,512]{1,0:T(8,128)S(1)} %get-tuple-element.31), channel_id=1, source_target_pairs={{0,96},{1,25},{2,98},{3,27},{4,100},{5,29},{6,102},{7,31},{8,16},{... | collective-permute-start | bytes 786440 | tf_op jit(solution)/shard_map/ppermute | solution.py:230
  40.8 2.9 %collective-permute-done.6 = f32[128,512]{1,0:T(8,128)S(1)} collective-permute-done((f32[128,512]{1,0:T(8,128)S(1)}, f32[128,512]{1,0:T(8,128)S(1)}, u32[]{:S(2)}, u32[]{:S(2)}) %collective-permute-start.6) | collective-permute-done | bytes 262176 | tf_op jit(solution)/shard_map/ppermute | solution.py:230
  43.8 0.0 collective-permute-done.7
  43.8 2.8 %collective-permute-done.8 = f32[128,512]{1,0:T(8,128)S(1)} collective-permute-done((f32[128,512]{1,0:T(8,128)S(1)}, f32[128,512]{1,0:T(8,128)S(1)}, u32[]{:S(2)}, u32[]{:S(2)}) %collective-permute-start.8) | collective-permute-done | bytes 262176 | tf_op jit(solution)/shard_map/ppermute | solution.py:230
  46.6 0.1 add_multiply_fusion
  46.7 4.4 %collective-permute-start.9 = (f32[4,16,512]{2,1,0:T(8,128)S(1)}, f32[4,16,512]{2,1,0:T(8,128)S(1)}, u32[]{:S(2)}, u32[]{:S(2)}) collective-permute-start(f32[4,16,512]{2,1,0:T(8,128)S(1)} %get-tuple-element.39), channel_id=1, source_target_pairs={{0,1},{1,0},{2,3},{3,2},{4,5},{5,4},{6,7},{7,6},{8,9},{9,8},{10,11... | collective-permute-start | bytes 393224 | tf_op jit(solution)/shard_map/ppermute | solution.py:23
  51.1 1.0 %collective-permute-done.9 = f32[4,16,512]{2,1,0:T(8,128)S(1)} collective-permute-done((f32[4,16,512]{2,1,0:T(8,128)S(1)}, f32[4,16,512]{2,1,0:T(8,128)S(1)}, u32[]{:S(2)}, u32[]{:S(2)}) %collective-permute-start.9) | collective-permute-done | bytes 131104 | tf_op jit(solution)/shard_map/ppermute | solution.py:23
  52.1 1.4 %collective-permute-start.10 = (f32[2,16,512]{2,1,0:T(8,128)S(1)}, f32[2,16,512]{2,1,0:T(8,128)S(1)}, u32[]{:S(2)}, u32[]{:S(2)}) collective-permute-start(f32[2,16,512]{2,1,0:T(8,128)S(1)} %get-tuple-element.36), channel_id=1, source_target_pairs={{0,2},{1,3},{2,0},{3,1},{4,6},{5,7},{6,4},{7,5},{8,10},{9,11},{10,... | collective-permute-start | bytes 196616 | tf_op jit(solution)/shard_map/ppermute | solution.py:23
  53.5 2.6 %collective-permute-start.11 = (f32[2,16,512]{2,1,0:T(8,128)S(1)}, f32[2,16,512]{2,1,0:T(8,128)S(1)}, u32[]{:S(2)}, u32[]{:S(2)}) collective-permute-start(f32[2,16,512]{2,1,0:T(8,128)S(1)} %get-tuple-element.35), channel_id=1, source_target_pairs={{0,4},{1,5},{2,6},{3,7},{4,0},{5,1},{6,2},{7,3},{8,12},{9,13},{10,... | collective-permute-start | bytes 196616 | tf_op jit(solution)/shard_map/ppermute | solution.py:23
  56.2 0.0 collective-permute-start.12
  56.2 0.0 collective-permute-done.10.refs_1_
  56.2 3.0 %collective-permute-done.11.refs_2_ = f32[2,16,512]{2,1,0:T(8,128)S(1)} collective-permute-done((f32[2,16,512]{2,1,0:T(8,128)S(1)}, f32[2,16,512]{2,1,0:T(8,128)S(1)}, u32[]{:S(2)}, u32[]{:S(2)}) %collective-permute-start.11) | collective-permute-done | bytes 65568 | tf_op jit(solution)/shard_map/ppermute | solution.py:23
  59.1 1.5 %collective-permute-done.12.refs_3_ = f32[2,16,512]{2,1,0:T(8,128)S(1)} collective-permute-done((f32[2,16,512]{2,1,0:T(8,128)S(1)}, f32[2,16,512]{2,1,0:T(8,128)S(1)}, u32[]{:S(2)}, u32[]{:S(2)}) %collective-permute-start.12) | collective-permute-done | bytes 65568 | tf_op jit(solution)/shard_map/ppermute | solution.py:23
  60.6 0.3 gram.1
  61.0 15.8 %all_to_all.11 = f32[128,1,128]{2,1,0:T(1,128)S(1)} all-to-all(f32[128,1,128]{2,1,0:T(1,128)S(1)} %bitcast.18), channel_id=1, replica_groups=mesh['blk'=16,'group'=8] {'blk','group'}, dimensions={0} | all-to-all | bytes 131072 | tf_op jit(solution)/shard_map/all_to_all | solution.py:249
  76.7 0.0 copy-done
  76.7 0.0 copy-done.1
  76.7 1.1 %finish.1 = (f32[16,512]{1,0:T(8,128)}, f32[16,512]{1,0:T(8,128)}) custom-call(f32[128,128]{1,0:T(8,128)S(1)} %bitcast.17, f32[8,16,512]{2,1,0:T(8,128)S(1)} %get-tuple-element.33.ordered_ref, f32[16,512]{1,0:T(8,128)S(1)} %copy-done, f32[16,512]{1,0:T(8,128)S(1)} %copy-done.1), custom_call_target="tpu_custom_call" | custom-call | tf_op jit(solution)/shard_map/finish/pallas_call | solution.py:251
  (3 shorter events, 0.1 us)
Async XLA Ops:
  6.1 16.2 %collective-permute-start = (f32[256,512]{1,0:T(8,128)}, f32[256,512]{1,0:T(8,128)S(1)}, u32[]{:S(2)}, u32[]{:S(2)}) collective-permute-start(f32[256,512]{1,0:T(8,128)} %get-tuple-element.18), channel_id=1, source_target_pairs={{0,64},{8,72},{16,80},{24,88},{32,96},{40,104},{48,112},{56,120},{... | collective-permute-start | bytes 1572872 | tf_op jit(solution)/shard_map/ppermute | solution.py:23
  9.7 15.6 %collective-permute-start.1 = (f32[256,512]{1,0:T(8,128)}, f32[256,512]{1,0:T(8,128)S(1)}, u32[]{:S(2)}, u32[]{:S(2)}) collective-permute-start(f32[256,512]{1,0:T(8,128)} %get-tuple-element.19), channel_id=1, source_target_pairs={{0,16},{8,24},{16,0},{24,8},{32,48},{40,56},{48,32},{56,40},{64,80... | collective-permute-start | bytes 1572872 | tf_op jit(solution)/shard_map/ppermute | solution.py:23
  20.5 56.3 %copy-start = (f32[16,512]{1,0:T(8,128)S(1)}, f32[16,512]{1,0:T(8,128)}, u32[]{:S(2)}) copy-start(f32[16,512]{1,0:T(8,128)} %weights_ref.1) | copy-start | bytes 98308
  20.5 56.2 %copy-start.1 = (f32[16,512]{1,0:T(8,128)S(1)}, f32[16,512]{1,0:T(8,128)}, u32[]{:S(2)}) copy-start(f32[16,512]{1,0:T(8,128)} %momentum_ref.1) | copy-start | bytes 98308
  20.5 12.3 %collective-permute-start.2 = (f32[256,512]{1,0:T(8,128)S(1)}, f32[256,512]{1,0:T(8,128)S(1)}, u32[]{:S(2)}, u32[]{:S(2)}) collective-permute-start(f32[256,512]{1,0:T(8,128)S(1)} %get-tuple-element.21), channel_id=1, source_target_pairs={{0,32},{8,40},{16,48},{24,56},{32,0},{40,8},{48,16},{56,24},{64,96... | collective-permute-start | bytes 1572872 | tf_op jit(solution)/shard_map/ppermute | solution.py:23
  20.9 13.1 %collective-permute-start.3 = (f32[256,512]{1,0:T(8,128)S(1)}, f32[256,512]{1,0:T(8,128)S(1)}, u32[]{:S(2)}, u32[]{:S(2)}) collective-permute-start(f32[256,512]{1,0:T(8,128)S(1)} %get-tuple-element.23), channel_id=1, source_target_pairs={{0,96},{8,104},{16,112},{24,120},{32,64},{40,72},{48,80},{56,88},{... | collective-permute-start | bytes 1572872 | tf_op jit(solution)/shard_map/ppermute | solution.py:23
  21.5 15.0 %collective-permute-start.4 = (f32[256,512]{1,0:T(8,128)S(1)}, f32[256,512]{1,0:T(8,128)S(1)}, u32[]{:S(2)}, u32[]{:S(2)}) collective-permute-start(f32[256,512]{1,0:T(8,128)S(1)} %get-tuple-element.22), channel_id=1, source_target_pairs={{0,8},{8,0},{16,24},{24,16},{32,40},{40,32},{48,56},{56,48},{64,72... | collective-permute-start | bytes 1572872 | tf_op jit(solution)/shard_map/ppermute | solution.py:23
  22.3 14.2 %collective-permute-start.5 = (f32[256,512]{1,0:T(8,128)S(1)}, f32[256,512]{1,0:T(8,128)S(1)}, u32[]{:S(2)}, u32[]{:S(2)}) collective-permute-start(f32[256,512]{1,0:T(8,128)S(1)} %get-tuple-element.24), channel_id=1, source_target_pairs={{0,24},{8,16},{16,8},{24,0},{32,56},{40,48},{48,40},{56,32},{64,88... | collective-permute-start | bytes 1572872 | tf_op jit(solution)/shard_map/ppermute | solution.py:23
  36.7 7.1 %collective-permute-start.6 = (f32[128,512]{1,0:T(8,128)S(1)}, f32[128,512]{1,0:T(8,128)S(1)}, u32[]{:S(2)}, u32[]{:S(2)}) collective-permute-start(f32[128,512]{1,0:T(8,128)S(1)} %get-tuple-element.29), channel_id=1, source_target_pairs={{0,16},{1,65},{2,18},{3,67},{4,20},{5,69},{6,22},{7,71},{8,72},{9,... | collective-permute-start | bytes 786440 | tf_op jit(solution)/shard_map/ppermute | solution.py:230
  37.8 6.0 %collective-permute-start.7 = (f32[128,512]{1,0:T(8,128)S(1)}, f32[128,512]{1,0:T(8,128)S(1)}, u32[]{:S(2)}, u32[]{:S(2)}) collective-permute-start(f32[128,512]{1,0:T(8,128)S(1)} %get-tuple-element.30), channel_id=1, source_target_pairs={{0,32},{1,9},{2,34},{3,11},{4,36},{5,13},{6,38},{7,15},{8,0},{9,41... | collective-permute-start | bytes 786440 | tf_op jit(solution)/shard_map/ppermute | solution.py:230
  39.5 7.1 %collective-permute-start.8 = (f32[128,512]{1,0:T(8,128)S(1)}, f32[128,512]{1,0:T(8,128)S(1)}, u32[]{:S(2)}, u32[]{:S(2)}) collective-permute-start(f32[128,512]{1,0:T(8,128)S(1)} %get-tuple-element.31), channel_id=1, source_target_pairs={{0,96},{1,25},{2,98},{3,27},{4,100},{5,29},{6,102},{7,31},{8,16},{... | collective-permute-start | bytes 786440 | tf_op jit(solution)/shard_map/ppermute | solution.py:230
  46.7 5.4 %collective-permute-start.9 = (f32[4,16,512]{2,1,0:T(8,128)S(1)}, f32[4,16,512]{2,1,0:T(8,128)S(1)}, u32[]{:S(2)}, u32[]{:S(2)}) collective-permute-start(f32[4,16,512]{2,1,0:T(8,128)S(1)} %get-tuple-element.39), channel_id=1, source_target_pairs={{0,1},{1,0},{2,3},{3,2},{4,5},{5,4},{6,7},{7,6},{8,9},{9,8},{10,11... | collective-permute-start | bytes 393224 | tf_op jit(solution)/shard_map/ppermute | solution.py:23
  52.1 4.0 %collective-permute-start.10 = (f32[2,16,512]{2,1,0:T(8,128)S(1)}, f32[2,16,512]{2,1,0:T(8,128)S(1)}, u32[]{:S(2)}, u32[]{:S(2)}) collective-permute-start(f32[2,16,512]{2,1,0:T(8,128)S(1)} %get-tuple-element.36), channel_id=1, source_target_pairs={{0,2},{1,3},{2,0},{3,1},{4,6},{5,7},{6,4},{7,5},{8,10},{9,11},{10,... | collective-permute-start | bytes 196616 | tf_op jit(solution)/shard_map/ppermute | solution.py:23
  53.5 5.6 %collective-permute-start.11 = (f32[2,16,512]{2,1,0:T(8,128)S(1)}, f32[2,16,512]{2,1,0:T(8,128)S(1)}, u32[]{:S(2)}, u32[]{:S(2)}) collective-permute-start(f32[2,16,512]{2,1,0:T(8,128)S(1)} %get-tuple-element.35), channel_id=1, source_target_pairs={{0,4},{1,5},{2,6},{3,7},{4,0},{5,1},{6,2},{7,3},{8,12},{9,13},{10,... | collective-permute-start | bytes 196616 | tf_op jit(solution)/shard_map/ppermute | solution.py:23
  56.2 4.5 %collective-permute-start.12 = (f32[2,16,512]{2,1,0:T(8,128)S(1)}, f32[2,16,512]{2,1,0:T(8,128)S(1)}, u32[]{:S(2)}, u32[]{:S(2)}) collective-permute-start(f32[2,16,512]{2,1,0:T(8,128)S(1)} %get-tuple-element.34), channel_id=1, source_target_pairs={{0,6},{1,7},{2,4},{3,5},{4,2},{5,3},{6,0},{7,1},{8,14},{9,15},{10,... | collective-permute-start | bytes 196616 | tf_op jit(solution)/shard_map/ppermute | solution.py:23

commit v4 on v3

--- a/solution.py
+++ b/solution.py
@@ -15,6 +15,7 @@
 COLS = 512
 PIECE = GROUPS * ROWS
 DEPTH = 512
+ORDER = (2, 1, 3)
 TOTAL = 128
 CONTRACT = (((0,), (0,)), ((), ()))
 
@@ -28,33 +29,45 @@
 
 
 def my_place():
-    blk, group = lax.axis_index("blk"), lax.axis_index("group")
-    return blk // SIDE, blk % SIDE, group % 2
-
-
-def piece_blocks(s):
-    x, z, core = my_place()
-    along_x = [(x ^ s) * SIDE + ((x ^ s ^ core) & 1) + 2 * k for k in range(2)]
-    along_z = [(((z ^ s ^ core ^ 1) & 1) + 2 * k) * SIDE + (z ^ s) for k in range(2)]
-    return along_x + along_z
-
-
-def product_kernel(masks, depth, added, act_ref, out_ref, *refs):
-    base_refs, refs = refs[: 2 * added], refs[2 * added :]
-    pieces = refs[: 2 * len(masks)]
-    held, grad, sems = refs[2 * len(masks) :]
+    blk, core = lax.axis_index("blk"), lax.axis_index("group") % 2
+    x, z = blk // SIDE, blk % SIDE
+    return jnp.where(core == 0, x, z), jnp.where(core == 0, z, x), core
+
+
+def piece_blocks(units):
+    first, _, core = my_place()
+    return [
+        jnp.where(core == 0, (first ^ s) * SIDE + k, k * SIDE + (first ^ s))
+        for s, h in units
+        for k in (2 * h, 2 * h + 1)
+    ]
+
+
+def way_pairs(s, half):
+    along_x = [core == half for core in range(2)]
+    return [
+        (k, k ^ (GROUPS * s * (SIDE if along_x[k % 2] else 1))) for k in range(TOTAL)
+    ]
+
+
+def sent_over(value, s, half):
+    return lax.ppermute(value, ("blk", "group"), way_pairs(s, half))
+
+
+def product_kernel(units, depth, act_ref, out_ref, *refs):
+    *refs, held, grad, sems = refs
+    pieces, base = refs[-len(units) :], refs[: -len(units)]
     chunks = out_ref.shape[0] // depth
-    blocks = [piece_blocks(s) for s in masks]
+    blocks = piece_blocks(units)
 
     def copies(k):
         rows = pl.ds(k * depth, depth)
         ends = [(out_ref.at[rows], grad.at[rows])]
-        for n in range(len(masks)):
-            for c in range(4):
-                start = pl.multiple_of(blocks[n][c] * PIECE, PIECE)
-                ends.append(
-                    (act_ref.at[rows, pl.ds(start, PIECE)], held.at[n, rows, pl.ds(c * PIECE, PIECE)])
-                )
+        for c, block in enumerate(blocks):
+            start = pl.multiple_of(block * PIECE, PIECE)
+            ends.append(
+                (act_ref.at[rows, pl.ds(start, PIECE)], held.at[rows, pl.ds(c * PIECE, PIECE)])
+            )
         return [
             pltpu.make_async_copy(source, target, sems.at[k, place])
             for place, (source, target) in enumerate(ends)
@@ -67,34 +80,28 @@
         for copy in copies(k):
             copy.wait()
         rows = pl.ds(k * depth, depth)
-        for n in range(len(masks)):
-            part = lax.dot_general(
-                held[n, rows], grad[rows], CONTRACT, preferred_element_type=jnp.float32
-            )
-            for way in range(2):
-                piece = pieces[2 * n + way]
-                mine = part[way * 2 * PIECE : (way + 1) * 2 * PIECE]
-                if k:
-                    piece[...] += mine
-                elif added:
-                    piece[...] = base_refs[way][...] + mine
-                else:
-                    piece[...] = mine
-
-
-def products(activations, grad_out, masks, depth, vmem, base=()):
+        part = lax.dot_general(held[rows], grad[rows], CONTRACT, preferred_element_type=jnp.float32)
+        for n, piece in enumerate(pieces):
+            mine = part[n * 2 * PIECE : (n + 1) * 2 * PIECE]
+            if k:
+                piece[...] += mine
+            elif base:
+                piece[...] = base[n][...] + mine
+            else:
+                piece[...] = mine
+
+
+def products(activations, grad_out, units, vmem, base=()):
     tokens, cols = grad_out.shape
-    count = 2 * len(masks)
     return pl.pallas_call(
-        functools.partial(product_kernel, masks, depth, len(base) // 2),
-        in_specs=[pl.BlockSpec(memory_space=pl.ANY)] * 2
-        + in_vmem(len(base)),
-        out_specs=in_vmem(count),
-        out_shape=[jax.ShapeDtypeStruct((2 * PIECE, cols), jnp.float32)] * count,
+        functools.partial(product_kernel, units, DEPTH),
+        in_specs=[pl.BlockSpec(memory_space=pl.ANY)] * 2 + in_vmem(len(base)),
+        out_specs=in_vmem(len(units)),
+        out_shape=[jax.ShapeDtypeStruct((2 * PIECE, cols), jnp.float32)] * len(units),
         scratch_shapes=[
-            pltpu.VMEM((len(masks), tokens, 4 * PIECE), activations.dtype),
+            pltpu.VMEM((tokens, 2 * PIECE * len(units)), activations.dtype),
             pltpu.VMEM((tokens, cols), grad_out.dtype),
-            pltpu.SemaphoreType.DMA((tokens // depth, 1 + 4 * len(masks))),
+            pltpu.SemaphoreType.DMA((tokens // DEPTH, 1 + 2 * len(units))),
         ],
         compiler_params=pltpu.CompilerParams(vmem_limit_bytes=vmem << 20),
         cost_estimate=pl.CostEstimate(flops=1000, bytes_accessed=1000, transcendentals=0),
@@ -102,31 +109,30 @@
     )(activations, grad_out, *base)
 
 
-def summed_kernel(*refs):
-    ways, out_refs = (refs[:3], refs[3:6]), refs[6:]
-    x, z, core = my_place()
-    along_x = ((x ^ z ^ core) & 1) == 1
-    for out_ref, s in zip(out_refs, (0, 2, 1, 3)):
-        from_first = jnp.logical_xor(along_x, s % 2 == 0)
-        for way, place in enumerate((z ^ s, x ^ s)):
-
-            @pl.when(from_first if way == 0 else jnp.logical_not(from_first))
-            def _(way=way, place=place):
-                rows = pl.ds(pl.multiple_of((place >> 1) * PIECE, PIECE), PIECE)
-                own, one, three = ways[way]
-                out_ref[...] = own[rows] + (one[rows] + three[rows])
-
-
-def summed(kept, first, third):
-    operands = [value for trio in zip(kept, first, third) for value in trio]
+def summed_kernel(own_lower_ref, own_upper_ref, lower_ref, upper_ref, *out_refs):
+    _, second, _ = my_place()
+    for out_ref, s in zip(out_refs, (0, *ORDER)):
+        place = second ^ s
+        rows = pl.ds(pl.multiple_of((place & 1) * PIECE, PIECE), PIECE)
+
+        @pl.when(place < 2)
+        def _():
+            out_ref[...] = own_lower_ref[rows] + lower_ref[rows]
+
+        @pl.when(place >= 2)
+        def _():
+            out_ref[...] = own_upper_ref[rows] + upper_ref[rows]
+
+
+def summed(*values):
     return pl.pallas_call(
         summed_kernel,
-        in_specs=in_vmem(6),
+        in_specs=in_vmem(4),
         out_specs=in_vmem(4),
         out_shape=[jax.ShapeDtypeStruct((PIECE, COLS), jnp.float32)] * 4,
         compiler_params=pltpu.CompilerParams(vmem_limit_bytes=8 << 20),
         name="summed",
-    )(*operands)
+    )(*values)
 
 
 def pair_slots():
@@ -198,15 +204,6 @@
     new_weights_ref[...] = (1.0 - 0.1 * 0.1) * weights_ref[...] - 0.1 * new_momentum
 
 
-def second_pairs(s):
-    pairs = []
-    for k in range(TOTAL):
-        blk, core = k // GROUPS, k % 2
-        along_z = ((blk // SIDE ^ blk ^ core) & 1 == 0) == (s == 2)
-        pairs.append((k, k ^ (GROUPS * (s if along_z else SIDE * s))))
-    return pairs
-
-
 def shards(activations, grad_out, weights, momentum):
     group = lax.axis_index("group")
     y, core = group // 2, group % 2
@@ -215,19 +212,24 @@
     def taken(value, index, dim):
         return lax.dynamic_index_in_dim(value, index, dim, keepdims=False)
 
-    def both_ways(pair, s):
-        return [exchanged(pair[0], "blk", SIDE * s), exchanged(pair[1], "blk", s)]
-
-    far = products(activations, grad_out, (2,), DEPTH, 62)
-    far_came = both_ways(far, 2)
-    grad_out, far = lax.optimization_barrier((grad_out, far))
-    near = products(activations, grad_out, (1, 3), DEPTH, 50)
-    near_came = both_ways(near[:2], 1), both_ways(near[2:], 3)
-    grad_out, near = lax.optimization_barrier((grad_out, near))
-    kept = products(activations, grad_out, (0,), DEPTH, 50, far_came)
-    mine, *sent = summed(kept, *near_came)
-    for value, s in zip(sent, (2, 1, 3)):
-        mine = mine + lax.ppermute(value, ("blk", "group"), second_pairs(s))
+    def ordered(pair):
+        nonlocal grad_out
+        grad_out, pair = lax.optimization_barrier((grad_out, pair))
+        return pair
+
+    def to_neighbours(pair):
+        return sent_over(pair[0], 1, 0), sent_over(pair[1], 3, 0)
+
+    far = ordered(products(activations, grad_out, ((2, 0), (2, 1)), 60))
+    lower, upper = to_neighbours(far)
+    direct = ordered(products(activations, grad_out, ((1, 0), (3, 1)), 50))
+    direct_came = to_neighbours(direct)
+    passed = ordered(products(activations, grad_out, ((1, 1), (3, 0)), 50, (upper, lower)))
+    upper, lower = to_neighbours(passed)
+    kept = products(activations, grad_out, ((0, 0), (0, 1)), 50, direct_came)
+    mine, *sent = summed(*kept, lower, upper)
+    for value, s in zip(sent, ORDER):
+        mine = mine + sent_over(value, s, 1)
     mine = (mine * grad_scale).reshape(SIDE, 2, ROWS, COLS)
     kept = taken(mine, core, 1)
     came = exchanged(taken(mine, core ^ 1, 1), "group", 1)

time: 78 us -> 75 us (0.962)
  starting transfers between devices: 24.6 us -> 19.3 us
  Pallas kernels: 18.8 us -> 20.6 us
    ppermute x10 -> x4, starting transfers between devices: 20.4 us -> 8.3 us  [exchanged(): lax.ppermute(value, axis, [(k, k ^ mask) for k in range(lax.axis_size(axi...]
    ppermute x3 -> x9, starting transfers between devices: 4.16 us -> 11 us  [sent_over(): return lax.ppermute(value, ('blk', 'group'), way_pairs(s, half))]
    ppermute x3 -> x9, waiting for transfers between devices: 5.75 us -> 12.5 us  [sent_over(): return lax.ppermute(value, ('blk', 'group'), way_pairs(s, half))]
    ppermute x10 -> x4, waiting for transfers between devices: 12.1 us -> 5.44 us  [exchanged(): lax.ppermute(value, axis, [(k, k ^ mask) for k in range(lax.axis_size(axi...]
    pallas_call x4 -> x5, Pallas kernels: 17.3 us -> 19.2 us  [the longest x4 19.1 us: products(): pl.pallas_call(functools.partial(product_kernel, units, DEPTH), in_specs=...]
  transfers between devices with their start and end apart: 13 -> 13, of which waited for: 8 -> 9; matrix products, arithmetic and copies ran while one was open for 0% -> 0% of each run, Pallas kernels for 15% -> 18%
where the time goes in v4:
time: 75 us; the launch traced here: 74.8 us
  Pallas kernels  20.6 us (27%)
  starting transfers between devices  19.3 us (26%)
  waiting for transfers between devices  17.9 us (24%)
  blocking collectives  16.1 us (21%)
    pallas_call x4, Pallas kernels, products(): pl.pallas_call(functools.partial(product_kernel, units, DEPTH), in_specs=...  19.1 us
    all_to_all x1, blocking collectives, shards(): lax.all_to_all(sums, ('blk', 'group'), split_axis=0, concat_axis=0, tiled...  16.1 us
    ppermute x9, waiting for transfers between devices, sent_over(): return lax.ppermute(value, ('blk', 'group'), way_pairs(s, half))  12.5 us
    ppermute x9, starting transfers between devices, sent_over(): return lax.ppermute(value, ('blk', 'group'), way_pairs(s, half))  11 us
    ppermute x4, starting transfers between devices, exchanged(): lax.ppermute(value, axis, [(k, k ^ mask) for k in range(lax.axis_size(axi...  8.3 us
    ppermute x4, waiting for transfers between devices, exchanged(): lax.ppermute(value, axis, [(k, k ^ mask) for k in range(lax.axis_size(axi...  5.44 us
  transfers between devices with their start and end apart: 13, of which 9 were waited for; matrix products, arithmetic and copies ran while one was open for 0% of the time, Pallas kernels for 18%

profile of v4, /device:TPU:1, one launch (start us, length us, event | category | flops | bytes accessed | tf_op | source)
XLA Modules:
  0.0 74.8 jit_solution(8114132852094069753)
XLA Ops:
  0.6 5.4 %products.4 = (f32[256,512]{1,0:T(8,128)}, f32[256,512]{1,0:T(8,128)}) custom-call(bf16[4096,2048]{1,0:T(8,128)(2,1)} %act_ref.7, bf16[4096,512]{1,0:T(8,128)(2,1)} %out_ref.4), custom_call_target="tpu_custom_call" | custom-call | flops 1000 | bytes 1000 | tf_op jit(solution)/shard_map/products/pallas_call | solution.py:96
  6.1 4.7 %collective-permute-start = (f32[256,512]{1,0:T(8,128)}, f32[256,512]{1,0:T(8,128)S(1)}, u32[]{:S(2)}, u32[]{:S(2)}) collective-permute-start(f32[256,512]{1,0:T(8,128)} %get-tuple-element.31), channel_id=1, source_target_pairs={{0,96},{1,25},{2,98},{3,27},{4,100},{5,29},{6,102},{7,31},{8,104},... | collective-permute-start | bytes 1572872 | tf_op jit(solution)/shard_map/ppermute | solution.py:54
  10.8 0.0 collective-permute-start.1
  10.8 4.5 %products.5 = (f32[256,512]{1,0:T(8,128)S(1)}, f32[256,512]{1,0:T(8,128)S(1)}) custom-call(bf16[4096,2048]{1,0:T(8,128)(2,1)} %act_ref.7, bf16[4096,512]{1,0:T(8,128)(2,1)} %out_ref.4), custom_call_target="tpu_custom_call" | custom-call | flops 1000 | bytes 1000 | tf_op jit(solution)/shard_map/products/pallas_call | solution.py:96
  15.3 1.5 %collective-permute-start.2 = (f32[256,512]{1,0:T(8,128)S(1)}, f32[256,512]{1,0:T(8,128)S(1)}, u32[]{:S(2)}, u32[]{:S(2)}) collective-permute-start(f32[256,512]{1,0:T(8,128)S(1)} %get-tuple-element.36), channel_id=1, source_target_pairs={{0,32},{1,9},{2,34},{3,11},{4,36},{5,13},{6,38},{7,15},{8,40},{9,1... | collective-permute-start | bytes 1572872 | tf_op jit(solution)/shard_map/ppermute | solution.py:54
  16.8 0.1 collective-permute-start.3
  16.9 0.9 %collective-permute-done.refs_0_ = f32[256,512]{1,0:T(8,128)S(1)} collective-permute-done((f32[256,512]{1,0:T(8,128)}, f32[256,512]{1,0:T(8,128)S(1)}, u32[]{:S(2)}, u32[]{:S(2)}) %collective-permute-start) | collective-permute-done | bytes 524320 | tf_op jit(solution)/shard_map/ppermute | solution.py:54
  17.8 1.5 %collective-permute-done.1.refs_1_ = f32[256,512]{1,0:T(8,128)S(1)} collective-permute-done((f32[256,512]{1,0:T(8,128)}, f32[256,512]{1,0:T(8,128)S(1)}, u32[]{:S(2)}, u32[]{:S(2)}) %collective-permute-start.1) | collective-permute-done | bytes 524320 | tf_op jit(solution)/shard_map/ppermute | solution.py:54
  19.3 4.6 %products.6 = (f32[256,512]{1,0:T(8,128)S(1)}, f32[256,512]{1,0:T(8,128)S(1)}) custom-call(bf16[4096,2048]{1,0:T(8,128)(2,1)} %act_ref.7, bf16[4096,512]{1,0:T(8,128)(2,1)} %out_ref.4, f32[256,512]{1,0:T(8,128)S(1)} %collective-permute-done.refs_0_, f32[256,512]{1,0:T(8,128)S(1)} %collective-permute-done.1.refs_1_), custom_call_target="tpu_custom_call" | custom-call | flops 1000 | bytes 1000 | tf_op jit(solution)/shard_map/products/pallas_call | solution.py:96
  23.9 0.0 copy-start
  23.9 0.0 copy-start.1
  23.9 1.3 %collective-permute-start.4 = (f32[256,512]{1,0:T(8,128)S(1)}, f32[256,512]{1,0:T(8,128)S(1)}, u32[]{:S(2)}, u32[]{:S(2)}) collective-permute-start(f32[256,512]{1,0:T(8,128)S(1)} %get-tuple-element.40), channel_id=1, source_target_pairs={{0,96},{1,25},{2,98},{3,27},{4,100},{5,29},{6,102},{7,31},{8,104},... | collective-permute-start | bytes 1572872 | tf_op jit(solution)/shard_map/ppermute | solution.py:54
  25.2 0.0 collective-permute-start.5
  25.2 0.0 collective-permute-done.2.refs_0_
  25.2 1.2 %collective-permute-done.3.refs_1_ = f32[256,512]{1,0:T(8,128)S(1)} collective-permute-done((f32[256,512]{1,0:T(8,128)S(1)}, f32[256,512]{1,0:T(8,128)S(1)}, u32[]{:S(2)}, u32[]{:S(2)}) %collective-permute-start.3) | collective-permute-done | bytes 524320 | tf_op jit(solution)/shard_map/ppermute | solution.py:54
  26.4 4.6 %products.7 = (f32[256,512]{1,0:T(8,128)S(1)}, f32[256,512]{1,0:T(8,128)S(1)}) custom-call(bf16[4096,2048]{1,0:T(8,128)(2,1)} %act_ref.7, bf16[4096,512]{1,0:T(8,128)(2,1)} %out_ref.4, f32[256,512]{1,0:T(8,128)S(1)} %collective-permute-done.2.refs_0_, f32[256,512]{1,0:T(8,128)S(1)} %collective-permute-done.3.refs_1_), custom_call_target="tpu_custom_call" | custom-call | flops 1000 | bytes 1000 | tf_op jit(solution)/shard_map/products/pallas_call | solution.py:96
  30.9 2.6 %collective-permute-done.4.lower_ref = f32[256,512]{1,0:T(8,128)S(1)} collective-permute-done((f32[256,512]{1,0:T(8,128)S(1)}, f32[256,512]{1,0:T(8,128)S(1)}, u32[]{:S(2)}, u32[]{:S(2)}) %collective-permute-start.4) | collective-permute-done | bytes 524320 | tf_op jit(solution)/shard_map/ppermute | solution.py:54
  33.5 0.0 collective-permute-done.5.upper_ref
  33.5 0.1 summed.1
  33.7 2.5 %collective-permute-start.6 = (f32[128,512]{1,0:T(8,128)S(1)}, f32[128,512]{1,0:T(8,128)S(1)}, u32[]{:S(2)}, u32[]{:S(2)}) collective-permute-start(f32[128,512]{1,0:T(8,128)S(1)} %get-tuple-element.43), channel_id=1, source_target_pairs={{0,16},{1,65},{2,18},{3,67},{4,20},{5,69},{6,22},{7,71},{8,24},{9,... | collective-permute-start | bytes 786440 | tf_op jit(solution)/shard_map/ppermute | solution.py:54
  36.2 0.6 collective-permute-start.7
  36.8 0.3 collective-permute-start.8
  37.0 3.7 %collective-permute-done.6 = f32[128,512]{1,0:T(8,128)S(1)} collective-permute-done((f32[128,512]{1,0:T(8,128)S(1)}, f32[128,512]{1,0:T(8,128)S(1)}, u32[]{:S(2)}, u32[]{:S(2)}) %collective-permute-start.6) | collective-permute-done | bytes 262176 | tf_op jit(solution)/shard_map/ppermute | solution.py:54
  40.8 2.6 %collective-permute-done.7 = f32[128,512]{1,0:T(8,128)S(1)} collective-permute-done((f32[128,512]{1,0:T(8,128)S(1)}, f32[128,512]{1,0:T(8,128)S(1)}, u32[]{:S(2)}, u32[]{:S(2)}) %collective-permute-start.7) | collective-permute-done | bytes 262176 | tf_op jit(solution)/shard_map/ppermute | solution.py:54
  43.4 0.0 collective-permute-done.8
  43.4 0.1 add_multiply_fusion
  43.5 4.3 %collective-permute-start.9 = (f32[4,16,512]{2,1,0:T(8,128)S(1)}, f32[4,16,512]{2,1,0:T(8,128)S(1)}, u32[]{:S(2)}, u32[]{:S(2)}) collective-permute-start(f32[4,16,512]{2,1,0:T(8,128)S(1)} %get-tuple-element.53), channel_id=1, source_target_pairs={{0,1},{1,0},{2,3},{3,2},{4,5},{5,4},{6,7},{7,6},{8,9},{9,8},{10,11... | collective-permute-start | bytes 393224 | tf_op jit(solution)/shard_map/ppermute | solution.py:24
  47.8 1.0 %collective-permute-done.9 = f32[4,16,512]{2,1,0:T(8,128)S(1)} collective-permute-done((f32[4,16,512]{2,1,0:T(8,128)S(1)}, f32[4,16,512]{2,1,0:T(8,128)S(1)}, u32[]{:S(2)}, u32[]{:S(2)}) %collective-permute-start.9) | collective-permute-done | bytes 131104 | tf_op jit(solution)/shard_map/ppermute | solution.py:24
  48.9 1.4 %collective-permute-start.10 = (f32[2,16,512]{2,1,0:T(8,128)S(1)}, f32[2,16,512]{2,1,0:T(8,128)S(1)}, u32[]{:S(2)}, u32[]{:S(2)}) collective-permute-start(f32[2,16,512]{2,1,0:T(8,128)S(1)} %get-tuple-element.50), channel_id=1, source_target_pairs={{0,2},{1,3},{2,0},{3,1},{4,6},{5,7},{6,4},{7,5},{8,10},{9,11},{10,... | collective-permute-start | bytes 196616 | tf_op jit(solution)/shard_map/ppermute | solution.py:24
  50.3 2.6 %collective-permute-start.11 = (f32[2,16,512]{2,1,0:T(8,128)S(1)}, f32[2,16,512]{2,1,0:T(8,128)S(1)}, u32[]{:S(2)}, u32[]{:S(2)}) collective-permute-start(f32[2,16,512]{2,1,0:T(8,128)S(1)} %get-tuple-element.49), channel_id=1, source_target_pairs={{0,4},{1,5},{2,6},{3,7},{4,0},{5,1},{6,2},{7,3},{8,12},{9,13},{10,... | collective-permute-start | bytes 196616 | tf_op jit(solution)/shard_map/ppermute | solution.py:24
  52.8 0.0 collective-permute-start.12
  52.8 0.0 collective-permute-done.10.refs_1_
  52.8 3.0 %collective-permute-done.11.refs_2_ = f32[2,16,512]{2,1,0:T(8,128)S(1)} collective-permute-done((f32[2,16,512]{2,1,0:T(8,128)S(1)}, f32[2,16,512]{2,1,0:T(8,128)S(1)}, u32[]{:S(2)}, u32[]{:S(2)}) %collective-permute-start.11) | collective-permute-done | bytes 65568 | tf_op jit(solution)/shard_map/ppermute | solution.py:24
  55.8 1.5 %collective-permute-done.12.refs_3_ = f32[2,16,512]{2,1,0:T(8,128)S(1)} collective-permute-done((f32[2,16,512]{2,1,0:T(8,128)S(1)}, f32[2,16,512]{2,1,0:T(8,128)S(1)}, u32[]{:S(2)}, u32[]{:S(2)}) %collective-permute-start.12) | collective-permute-done | bytes 65568 | tf_op jit(solution)/shard_map/ppermute | solution.py:24
  57.3 0.3 gram.1
  57.6 16.1 %all_to_all.11 = f32[128,1,128]{2,1,0:T(1,128)S(1)} all-to-all(f32[128,1,128]{2,1,0:T(1,128)S(1)} %bitcast.18), channel_id=1, replica_groups=mesh['blk'=16,'group'=8] {'blk','group'}, dimensions={0} | all-to-all | bytes 131072 | tf_op jit(solution)/shard_map/all_to_all | solution.py:251
  73.7 0.0 copy-done
  73.7 0.0 copy-done.1
  73.7 1.1 %finish.1 = (f32[16,512]{1,0:T(8,128)}, f32[16,512]{1,0:T(8,128)}) custom-call(f32[128,128]{1,0:T(8,128)S(1)} %bitcast.17, f32[8,16,512]{2,1,0:T(8,128)S(1)} %get-tuple-element.47.ordered_ref, f32[16,512]{1,0:T(8,128)S(1)} %copy-done, f32[16,512]{1,0:T(8,128)S(1)} %copy-done.1), custom_call_target="tpu_custom_call" | custom-call | tf_op jit(solution)/shard_map/finish/pallas_call | solution.py:253
  (3 shorter events, 0.1 us)
Async XLA Ops:
  6.1 11.7 %collective-permute-start = (f32[256,512]{1,0:T(8,128)}, f32[256,512]{1,0:T(8,128)S(1)}, u32[]{:S(2)}, u32[]{:S(2)}) collective-permute-start(f32[256,512]{1,0:T(8,128)} %get-tuple-element.31), channel_id=1, source_target_pairs={{0,96},{1,25},{2,98},{3,27},{4,100},{5,29},{6,102},{7,31},{8,104},... | collective-permute-start | bytes 1572872 | tf_op jit(solution)/shard_map/ppermute | solution.py:54
  10.8 8.5 %collective-permute-start.1 = (f32[256,512]{1,0:T(8,128)}, f32[256,512]{1,0:T(8,128)S(1)}, u32[]{:S(2)}, u32[]{:S(2)}) collective-permute-start(f32[256,512]{1,0:T(8,128)} %get-tuple-element.32), channel_id=1, source_target_pairs={{0,32},{1,9},{2,34},{3,11},{4,36},{5,13},{6,38},{7,15},{8,40},{9,1... | collective-permute-start | bytes 1572872 | tf_op jit(solution)/shard_map/ppermute | solution.py:54
  15.3 9.9 %collective-permute-start.2 = (f32[256,512]{1,0:T(8,128)S(1)}, f32[256,512]{1,0:T(8,128)S(1)}, u32[]{:S(2)}, u32[]{:S(2)}) collective-permute-start(f32[256,512]{1,0:T(8,128)S(1)} %get-tuple-element.36), channel_id=1, source_target_pairs={{0,32},{1,9},{2,34},{3,11},{4,36},{5,13},{6,38},{7,15},{8,40},{9,1... | collective-permute-start | bytes 1572872 | tf_op jit(solution)/shard_map/ppermute | solution.py:54
  16.8 9.5 %collective-permute-start.3 = (f32[256,512]{1,0:T(8,128)S(1)}, f32[256,512]{1,0:T(8,128)S(1)}, u32[]{:S(2)}, u32[]{:S(2)}) collective-permute-start(f32[256,512]{1,0:T(8,128)S(1)} %get-tuple-element.37), channel_id=1, source_target_pairs={{0,96},{1,25},{2,98},{3,27},{4,100},{5,29},{6,102},{7,31},{8,104},... | collective-permute-start | bytes 1572872 | tf_op jit(solution)/shard_map/ppermute | solution.py:54
  23.9 49.9 %copy-start = (f32[16,512]{1,0:T(8,128)S(1)}, f32[16,512]{1,0:T(8,128)}, u32[]{:S(2)}) copy-start(f32[16,512]{1,0:T(8,128)} %weights_ref.1) | copy-start | bytes 98308
  23.9 49.9 %copy-start.1 = (f32[16,512]{1,0:T(8,128)S(1)}, f32[16,512]{1,0:T(8,128)}, u32[]{:S(2)}) copy-start(f32[16,512]{1,0:T(8,128)} %momentum_ref.1) | copy-start | bytes 98308
  23.9 9.6 %collective-permute-start.4 = (f32[256,512]{1,0:T(8,128)S(1)}, f32[256,512]{1,0:T(8,128)S(1)}, u32[]{:S(2)}, u32[]{:S(2)}) collective-permute-start(f32[256,512]{1,0:T(8,128)S(1)} %get-tuple-element.40), channel_id=1, source_target_pairs={{0,96},{1,25},{2,98},{3,27},{4,100},{5,29},{6,102},{7,31},{8,104},... | collective-permute-start | bytes 1572872 | tf_op jit(solution)/shard_map/ppermute | solution.py:54
  25.2 8.3 %collective-permute-start.5 = (f32[256,512]{1,0:T(8,128)S(1)}, f32[256,512]{1,0:T(8,128)S(1)}, u32[]{:S(2)}, u32[]{:S(2)}) collective-permute-start(f32[256,512]{1,0:T(8,128)S(1)} %get-tuple-element.41), channel_id=1, source_target_pairs={{0,32},{1,9},{2,34},{3,11},{4,36},{5,13},{6,38},{7,15},{8,40},{9,1... | collective-permute-start | bytes 1572872 | tf_op jit(solution)/shard_map/ppermute | solution.py:54
  33.7 7.1 %collective-permute-start.6 = (f32[128,512]{1,0:T(8,128)S(1)}, f32[128,512]{1,0:T(8,128)S(1)}, u32[]{:S(2)}, u32[]{:S(2)}) collective-permute-start(f32[128,512]{1,0:T(8,128)S(1)} %get-tuple-element.43), channel_id=1, source_target_pairs={{0,16},{1,65},{2,18},{3,67},{4,20},{5,69},{6,22},{7,71},{8,24},{9,... | collective-permute-start | bytes 786440 | tf_op jit(solution)/shard_map/ppermute | solution.py:54
  36.2 7.2 %collective-permute-start.7 = (f32[128,512]{1,0:T(8,128)S(1)}, f32[128,512]{1,0:T(8,128)S(1)}, u32[]{:S(2)}, u32[]{:S(2)}) collective-permute-start(f32[128,512]{1,0:T(8,128)S(1)} %get-tuple-element.44), channel_id=1, source_target_pairs={{0,8},{1,33},{2,10},{3,35},{4,12},{5,37},{6,14},{7,39},{8,0},{9,41... | collective-permute-start | bytes 786440 | tf_op jit(solution)/shard_map/ppermute | solution.py:54
  36.8 6.6 %collective-permute-start.8 = (f32[128,512]{1,0:T(8,128)S(1)}, f32[128,512]{1,0:T(8,128)S(1)}, u32[]{:S(2)}, u32[]{:S(2)}) collective-permute-start(f32[128,512]{1,0:T(8,128)S(1)} %get-tuple-element.45), channel_id=1, source_target_pairs={{0,24},{1,97},{2,26},{3,99},{4,28},{5,101},{6,30},{7,103},{8,16},{... | collective-permute-start | bytes 786440 | tf_op jit(solution)/shard_map/ppermute | solution.py:54
  43.5 5.3 %collective-permute-start.9 = (f32[4,16,512]{2,1,0:T(8,128)S(1)}, f32[4,16,512]{2,1,0:T(8,128)S(1)}, u32[]{:S(2)}, u32[]{:S(2)}) collective-permute-start(f32[4,16,512]{2,1,0:T(8,128)S(1)} %get-tuple-element.53), channel_id=1, source_target_pairs={{0,1},{1,0},{2,3},{3,2},{4,5},{5,4},{6,7},{7,6},{8,9},{9,8},{10,11... | collective-permute-start | bytes 393224 | tf_op jit(solution)/shard_map/ppermute | solution.py:24
  48.9 4.0 %collective-permute-start.10 = (f32[2,16,512]{2,1,0:T(8,128)S(1)}, f32[2,16,512]{2,1,0:T(8,128)S(1)}, u32[]{:S(2)}, u32[]{:S(2)}) collective-permute-start(f32[2,16,512]{2,1,0:T(8,128)S(1)} %get-tuple-element.50), channel_id=1, source_target_pairs={{0,2},{1,3},{2,0},{3,1},{4,6},{5,7},{6,4},{7,5},{8,10},{9,11},{10,... | collective-permute-start | bytes 196616 | tf_op jit(solution)/shard_map/ppermute | solution.py:24
  50.3 5.5 %collective-permute-start.11 = (f32[2,16,512]{2,1,0:T(8,128)S(1)}, f32[2,16,512]{2,1,0:T(8,128)S(1)}, u32[]{:S(2)}, u32[]{:S(2)}) collective-permute-start(f32[2,16,512]{2,1,0:T(8,128)S(1)} %get-tuple-element.49), channel_id=1, source_target_pairs={{0,4},{1,5},{2,6},{3,7},{4,0},{5,1},{6,2},{7,3},{8,12},{9,13},{10,... | collective-permute-start | bytes 196616 | tf_op jit(solution)/shard_map/ppermute | solution.py:24
  52.8 4.5 %collective-permute-start.12 = (f32[2,16,512]{2,1,0:T(8,128)S(1)}, f32[2,16,512]{2,1,0:T(8,128)S(1)}, u32[]{:S(2)}, u32[]{:S(2)}) collective-permute-start(f32[2,16,512]{2,1,0:T(8,128)S(1)} %get-tuple-element.48), channel_id=1, source_target_pairs={{0,6},{1,7},{2,4},{3,5},{4,2},{5,3},{6,0},{7,1},{8,14},{9,15},{10,... | collective-permute-start | bytes 196616 | tf_op jit(solution)/shard_map/ppermute | solution.py:24

commit v5 on v4

--- a/solution.py
+++ b/solution.py
@@ -54,59 +54,107 @@
     return lax.ppermute(value, ("blk", "group"), way_pairs(s, half))
 
 
-def product_kernel(units, depth, act_ref, out_ref, *refs):
-    *refs, held, grad, sems = refs
-    pieces, base = refs[-len(units) :], refs[: -len(units)]
-    chunks = out_ref.shape[0] // depth
-    blocks = piece_blocks(units)
-
-    def copies(k):
-        rows = pl.ds(k * depth, depth)
-        ends = [(out_ref.at[rows], grad.at[rows])]
-        for c, block in enumerate(blocks):
-            start = pl.multiple_of(block * PIECE, PIECE)
-            ends.append(
-                (act_ref.at[rows, pl.ds(start, PIECE)], held.at[rows, pl.ds(c * PIECE, PIECE)])
-            )
-        return [
-            pltpu.make_async_copy(source, target, sems.at[k, place])
+def product_kernel(units, later, held_ready, grad_ready, based, *refs):
+    refs = list(refs)
+    act_ref, out_ref = refs.pop(0), refs.pop(0)
+    held = refs.pop(0) if held_ready else None
+    base = [refs.pop(0) for _ in units] if based else ()
+    pieces = [refs.pop(0) for _ in units]
+    grad = out_ref if grad_ready else refs.pop(0)
+    later_held = refs.pop(0) if later else None
+    held = held if held_ready else refs.pop(0)
+    tokens = grad.shape[0]
+    chunks = tokens // DEPTH
+
+    def block_copies(units, held, k):
+        rows = pl.ds(k * DEPTH, DEPTH)
+        ends = []
+        for c, block in enumerate(piece_blocks(units)):
+            columns = pl.ds(pl.multiple_of(block * PIECE, PIECE), PIECE)
+            ends.append((act_ref.at[rows, columns], held.at[rows, pl.ds(c * PIECE, PIECE)]))
+        return ends
+
+    def started(ends, k):
+        copies = [
+            pltpu.make_async_copy(source, target, refs[0].at[k, place])
             for place, (source, target) in enumerate(ends)
         ]
-
+        for copy in copies:
+            copy.start()
+        return copies
+
+    copies = []
     for k in range(chunks):
-        for copy in copies(k):
-            copy.start()
+        rows = pl.ds(k * DEPTH, DEPTH)
+        ends = [] if held_ready else block_copies(units, held, k)
+        if not grad_ready:
+            ends.append((out_ref.at[rows], grad.at[rows]))
+        copies.append(started(ends, k) if ends else [])
+    if later:
+        for k in range(chunks):
+            copies.append(started(block_copies(later, later_held, k), chunks + k))
     for k in range(chunks):
-        for copy in copies(k):
+        for copy in copies[k]:
             copy.wait()
-        rows = pl.ds(k * depth, depth)
+        rows = pl.ds(k * DEPTH, DEPTH)
         part = lax.dot_general(held[rows], grad[rows], CONTRACT, preferred_element_type=jnp.float32)
         for n, piece in enumerate(pieces):
             mine = part[n * 2 * PIECE : (n + 1) * 2 * PIECE]
             if k:
                 piece[...] += mine
-            elif base:
+            elif based:
                 piece[...] = base[n][...] + mine
             else:
                 piece[...] = mine
-
-
-def products(activations, grad_out, units, vmem, base=()):
+    for chunk in copies[chunks:]:
+        for copy in chunk:
+            copy.wait()
+
+
+def products(activations, grad_out, units, later=(), held=None, grad_ready=True, base=()):
     tokens, cols = grad_out.shape
+    wide = jax.ShapeDtypeStruct((tokens, 2 * PIECE * len(units)), activations.dtype)
+    flat = jax.ShapeDtypeStruct((tokens, cols), grad_out.dtype)
+    chunks = tokens // DEPTH * (2 if later else 1)
+    scratch = [] if held is not None else [pltpu.VMEM(wide.shape, wide.dtype)]
+    scratch.append(pltpu.SemaphoreType.DMA((chunks, 1 + 2 * len(units))))
+
+    def placed(value, ready):
+        return pltpu.with_memory_space_constraint(value, pltpu.VMEM if ready else pltpu.HBM)
+
+    def spec(ready):
+        return pl.BlockSpec(memory_space=pltpu.VMEM if ready else pl.ANY)
+
+    ready = [] if held is None else [placed(held, True)]
+    outs = [jax.ShapeDtypeStruct((2 * PIECE, cols), jnp.float32)] * len(units)
+    outs += ([] if grad_ready else [flat]) + ([wide] if later else [])
     return pl.pallas_call(
-        functools.partial(product_kernel, units, DEPTH),
-        in_specs=[pl.BlockSpec(memory_space=pl.ANY)] * 2 + in_vmem(len(base)),
-        out_specs=in_vmem(len(units)),
-        out_shape=[jax.ShapeDtypeStruct((2 * PIECE, cols), jnp.float32)] * len(units),
-        scratch_shapes=[
-            pltpu.VMEM((tokens, 2 * PIECE * len(units)), activations.dtype),
-            pltpu.VMEM((tokens, cols), grad_out.dtype),
-            pltpu.SemaphoreType.DMA((tokens // DEPTH, 1 + 2 * len(units))),
-        ],
-        compiler_params=pltpu.CompilerParams(vmem_limit_bytes=vmem << 20),
+        functools.partial(product_kernel, units, later, held is not None, grad_ready, bool(base)),
+        in_specs=[spec(False), spec(grad_ready)] + in_vmem(len(ready) + len(base)),
+        out_specs=in_vmem(len(outs)),
+        out_shape=outs,
+        scratch_shapes=scratch,
+        compiler_params=pltpu.CompilerParams(vmem_limit_bytes=24 << 20),
         cost_estimate=pl.CostEstimate(flops=1000, bytes_accessed=1000, transcendentals=0),
         name="products",
-    )(activations, grad_out, *base)
+    )(placed(activations, False), placed(grad_out, grad_ready), *ready, *base)
+
+
+def relayed_kernel(*refs):
+    for one_ref, other_ref, out_ref in zip(refs[:2], refs[2:4], refs[4:]):
+        out_ref[...] = one_ref[...] + other_ref[...]
+
+
+def relayed(own, came):
+    return pl.pallas_call(
+        relayed_kernel,
+        in_specs=in_vmem(4),
+        out_specs=in_vmem(2),
+        out_shape=[jax.ShapeDtypeStruct(value.shape, value.dtype) for value in own],
+        compiler_params=pltpu.CompilerParams(vmem_limit_bytes=8 << 20),
+        cost_estimate=pl.CostEstimate(flops=1000, bytes_accessed=1000, transcendentals=0),
+        name="relayed",
+    )(*own, *came)
 
 
 def summed_kernel(own_lower_ref, own_upper_ref, lower_ref, upper_ref, *out_refs):
@@ -212,21 +260,17 @@
     def taken(value, index, dim):
         return lax.dynamic_index_in_dim(value, index, dim, keepdims=False)
 
-    def ordered(pair):
-        nonlocal grad_out
-        grad_out, pair = lax.optimization_barrier((grad_out, pair))
-        return pair
-
     def to_neighbours(pair):
         return sent_over(pair[0], 1, 0), sent_over(pair[1], 3, 0)
 
-    far = ordered(products(activations, grad_out, ((2, 0), (2, 1)), 60))
+    after, own = ((1, 1), (3, 0)), ((0, 0), (0, 1))
+    *far, grad = products(activations, grad_out, ((2, 0), (2, 1)), grad_ready=False)
     lower, upper = to_neighbours(far)
-    direct = ordered(products(activations, grad_out, ((1, 0), (3, 1)), 50))
+    *direct, held = products(activations, grad, ((1, 0), (3, 1)), later=after)
     direct_came = to_neighbours(direct)
-    passed = ordered(products(activations, grad_out, ((1, 1), (3, 0)), 50, (upper, lower)))
-    upper, lower = to_neighbours(passed)
-    kept = products(activations, grad_out, ((0, 0), (0, 1)), 50, direct_came)
+    *passed, held = products(activations, grad, after, later=own, held=held)
+    upper, lower = to_neighbours(relayed(passed, (upper, lower)))
+    kept = products(activations, grad, own, held=held, base=direct_came)
     mine, *sent = summed(*kept, lower, upper)
     for value, s in zip(sent, ORDER):
         mine = mine + sent_over(value, s, 1)

time: 75 us -> 73.4 us (0.979)
  Pallas kernels: 20.6 us -> 19 us
  starting transfers between devices: 19.3 us -> 20.8 us
  blocking collectives: 16.1 us -> 15 us
    pallas_call x4 -> x5, Pallas kernels: 19.1 us -> 17.5 us  [the longest x4 17.4 us: products(): pl.pallas_call(functools.partial(product_kernel, units, later, held is no...]
    ppermute x9, starting transfers between devices: 11 us -> 12.4 us  [sent_over(): return lax.ppermute(value, ('blk', 'group'), way_pairs(s, half))]
    all_to_all x1, blocking collectives: 16.1 us -> 15 us  [shards(): lax.all_to_all(sums, ('blk', 'group'), split_axis=0, concat_axis=0, tiled...]
  transfers between devices with their start and end apart: 13 -> 13, of which waited for: 9 -> 9; matrix products, arithmetic and copies ran while one was open for 0% -> 0% of each run, Pallas kernels for 18% -> 17%
where the time goes in v5:
time: 73.4 us; the launch traced here: 73.2 us
  starting transfers between devices  20.8 us (28%)
  Pallas kernels  19 us (26%)
  waiting for transfers between devices  17.5 us (24%)
  blocking collectives  15 us (20%)
  between operations  0.75 us (1%)
    pallas_call x4, Pallas kernels, products(): pl.pallas_call(functools.partial(product_kernel, units, later, held is no...  17.4 us
    all_to_all x1, blocking collectives, shards(): lax.all_to_all(sums, ('blk', 'group'), split_axis=0, concat_axis=0, tiled...  15 us
    ppermute x9, starting transfers between devices, sent_over(): return lax.ppermute(value, ('blk', 'group'), way_pairs(s, half))  12.4 us
    ppermute x9, waiting for transfers between devices, sent_over(): return lax.ppermute(value, ('blk', 'group'), way_pairs(s, half))  12 us
    ppermute x4, starting transfers between devices, exchanged(): lax.ppermute(value, axis, [(k, k ^ mask) for k in range(lax.axis_size(axi...  8.37 us
    ppermute x4, waiting for transfers between devices, exchanged(): lax.ppermute(value, axis, [(k, k ^ mask) for k in range(lax.axis_size(axi...  5.44 us
  transfers between devices with their start and end apart: 13, of which 9 were waited for; matrix products, arithmetic and copies ran while one was open for 0% of the time, Pallas kernels for 17%

profile of v5, /device:TPU:1, one launch (start us, length us, event | category | flops | bytes accessed | tf_op | source)
XLA Modules:
  0.0 73.2 jit_solution(3202505110145834699)
XLA Ops:
  0.6 4.7 %products.4 = (f32[256,512]{1,0:T(8,128)S(1)}, f32[256,512]{1,0:T(8,128)S(1)}, bf16[4096,512]{1,0:T(8,128)(2,1)S(1)}) custom-call(bf16[4096,2048]{1,0:T(8,128)(2,1)} %refs_0_.7, bf16[4096,512]{1,0:T(8,128)(2,1)} %refs_1_.1), custom_call_target="tpu_custom_call" | custom-call | flops 1000 | bytes 1000 | tf_op jit(solution)/shard_map/products/pallas_call | solution.py:131
  5.3 4.6 %collective-permute-start.2 = (f32[256,512]{1,0:T(8,128)S(1)}, f32[256,512]{1,0:T(8,128)S(1)}, u32[]{:S(2)}, u32[]{:S(2)}) collective-permute-start(f32[256,512]{1,0:T(8,128)S(1)} %get-tuple-element.30), channel_id=1, source_target_pairs={{0,96},{1,25},{2,98},{3,27},{4,100},{5,29},{6,102},{7,31},{8,104},... | collective-permute-start | bytes 1572872 | tf_op jit(solution)/shard_map/ppermute | solution.py:54
  9.9 0.0 collective-permute-start.3
  9.9 4.8 %products.5 = (f32[256,512]{1,0:T(8,128)S(1)}, f32[256,512]{1,0:T(8,128)S(1)}, bf16[4096,512]{1,0:T(8,128)(2,1)S(1)}) custom-call(bf16[4096,2048]{1,0:T(8,128)(2,1)} %refs_0_.7, bf16[4096,512]{1,0:T(8,128)(2,1)S(1)} %get-tuple-element.21.refs_1_), custom_call_target="tpu_custom_call" | custom-call | flops 1000 | bytes 1000 | tf_op jit(solution)/shard_map/products/pallas_call | solution.py:131
  14.8 1.5 %collective-permute-start = (f32[256,512]{1,0:T(8,128)S(1)}, f32[256,512]{1,0:T(8,128)S(1)}, u32[]{:S(2)}, u32[]{:S(2)}) collective-permute-start(f32[256,512]{1,0:T(8,128)S(1)} %get-tuple-element.24), channel_id=1, source_target_pairs={{0,32},{1,9},{2,34},{3,11},{4,36},{5,13},{6,38},{7,15},{8,40},{9,1... | collective-permute-start | bytes 1572872 | tf_op jit(solution)/shard_map/ppermute | solution.py:54
  16.3 0.1 collective-permute-start.1
  16.4 5.2 %products.6 = (f32[256,512]{1,0:T(8,128)S(1)}, f32[256,512]{1,0:T(8,128)S(1)}, bf16[4096,512]{1,0:T(8,128)(2,1)S(1)}) custom-call(bf16[4096,2048]{1,0:T(8,128)(2,1)} %refs_0_.7, bf16[4096,512]{1,0:T(8,128)(2,1)S(1)} %get-tuple-element.21.refs_1_, bf16[4096,512]{1,0:T(8,128)(2,1)S(1)} %get-tuple-element.22.refs_2_), custom_call_target="tpu_custom_call" | custom-call | flops 1000 | bytes 1000 | tf_op jit(solution)/shard_map/products/pallas_call | solution.py:131
  21.6 0.0 collective-permute-done.2.refs_2_
  21.6 0.0 collective-permute-done.3.refs_3_
  21.6 0.1 relayed.1
  21.7 2.7 %collective-permute-start.4 = (f32[256,512]{1,0:T(8,128)S(1)}, f32[256,512]{1,0:T(8,128)S(1)}, u32[]{:S(2)}, u32[]{:S(2)}) collective-permute-start(f32[256,512]{1,0:T(8,128)S(1)} %get-tuple-element.32), channel_id=1, source_target_pairs={{0,96},{1,25},{2,98},{3,27},{4,100},{5,29},{6,102},{7,31},{8,104},... | collective-permute-start | bytes 1572872 | tf_op jit(solution)/shard_map/ppermute | solution.py:54
  24.4 0.0 collective-permute-start.5
  24.4 0.0 collective-permute-done.refs_3_
  24.4 1.5 %collective-permute-done.1.refs_4_ = f32[256,512]{1,0:T(8,128)S(1)} collective-permute-done((f32[256,512]{1,0:T(8,128)S(1)}, f32[256,512]{1,0:T(8,128)S(1)}, u32[]{:S(2)}, u32[]{:S(2)}) %collective-permute-start.1) | collective-permute-done | bytes 524320 | tf_op jit(solution)/shard_map/ppermute | solution.py:54
  25.8 2.7 %products.7 = (f32[256,512]{1,0:T(8,128)S(1)}, f32[256,512]{1,0:T(8,128)S(1)}) custom-call(bf16[4096,2048]{1,0:T(8,128)(2,1)} %refs_0_.7, bf16[4096,512]{1,0:T(8,128)(2,1)S(1)} %get-tuple-element.21.refs_1_, bf16[4096,512]{1,0:T(8,128)(2,1)S(1)} %get-tuple-element.23.refs_2_, f32[256,512]{1,0:T(8,128)S(1)} %collective-permute-done.refs_3_, ...), custom_call_target="tpu_custom_call" | custom-call | flops 1000 | bytes 1000 | tf_op jit(solution)/shard_map/products/pallas_call | solution.py:131
  28.6 0.0 copy-start
  28.6 0.0 copy-start.1
  28.6 2.9 %collective-permute-done.4.lower_ref = f32[256,512]{1,0:T(8,128)S(1)} collective-permute-done((f32[256,512]{1,0:T(8,128)S(1)}, f32[256,512]{1,0:T(8,128)S(1)}, u32[]{:S(2)}, u32[]{:S(2)}) %collective-permute-start.4) | collective-permute-done | bytes 524320 | tf_op jit(solution)/shard_map/ppermute | solution.py:54
  31.5 1.2 %collective-permute-done.5.upper_ref = f32[256,512]{1,0:T(8,128)S(1)} collective-permute-done((f32[256,512]{1,0:T(8,128)S(1)}, f32[256,512]{1,0:T(8,128)S(1)}, u32[]{:S(2)}, u32[]{:S(2)}) %collective-permute-start.5) | collective-permute-done | bytes 524320 | tf_op jit(solution)/shard_map/ppermute | solution.py:54
  32.7 0.1 summed.1
  32.8 2.6 %collective-permute-start.6 = (f32[128,512]{1,0:T(8,128)S(1)}, f32[128,512]{1,0:T(8,128)S(1)}, u32[]{:S(2)}, u32[]{:S(2)}) collective-permute-start(f32[128,512]{1,0:T(8,128)S(1)} %get-tuple-element.35), channel_id=1, source_target_pairs={{0,16},{1,65},{2,18},{3,67},{4,20},{5,69},{6,22},{7,71},{8,24},{9,... | collective-permute-start | bytes 786440 | tf_op jit(solution)/shard_map/ppermute | solution.py:54
  35.4 0.3 collective-permute-start.7
  35.7 0.6 collective-permute-start.8
  36.3 3.4 %collective-permute-done.6 = f32[128,512]{1,0:T(8,128)S(1)} collective-permute-done((f32[128,512]{1,0:T(8,128)S(1)}, f32[128,512]{1,0:T(8,128)S(1)}, u32[]{:S(2)}, u32[]{:S(2)}) %collective-permute-start.6) | collective-permute-done | bytes 262176 | tf_op jit(solution)/shard_map/ppermute | solution.py:54
  39.7 2.9 %collective-permute-done.7 = f32[128,512]{1,0:T(8,128)S(1)} collective-permute-done((f32[128,512]{1,0:T(8,128)S(1)}, f32[128,512]{1,0:T(8,128)S(1)}, u32[]{:S(2)}, u32[]{:S(2)}) %collective-permute-start.7) | collective-permute-done | bytes 262176 | tf_op jit(solution)/shard_map/ppermute | solution.py:54
  42.6 0.2 collective-permute-done.8
  42.8 0.1 add_multiply_fusion
  42.9 4.4 %collective-permute-start.9 = (f32[4,16,512]{2,1,0:T(8,128)S(1)}, f32[4,16,512]{2,1,0:T(8,128)S(1)}, u32[]{:S(2)}, u32[]{:S(2)}) collective-permute-start(f32[4,16,512]{2,1,0:T(8,128)S(1)} %get-tuple-element.45), channel_id=1, source_target_pairs={{0,1},{1,0},{2,3},{3,2},{4,5},{5,4},{6,7},{7,6},{8,9},{9,8},{10,11... | collective-permute-start | bytes 393224 | tf_op jit(solution)/shard_map/ppermute | solution.py:24
  47.3 1.0 %collective-permute-done.9 = f32[4,16,512]{2,1,0:T(8,128)S(1)} collective-permute-done((f32[4,16,512]{2,1,0:T(8,128)S(1)}, f32[4,16,512]{2,1,0:T(8,128)S(1)}, u32[]{:S(2)}, u32[]{:S(2)}) %collective-permute-start.9) | collective-permute-done | bytes 131104 | tf_op jit(solution)/shard_map/ppermute | solution.py:24
  48.3 1.4 %collective-permute-start.10 = (f32[2,16,512]{2,1,0:T(8,128)S(1)}, f32[2,16,512]{2,1,0:T(8,128)S(1)}, u32[]{:S(2)}, u32[]{:S(2)}) collective-permute-start(f32[2,16,512]{2,1,0:T(8,128)S(1)} %get-tuple-element.42), channel_id=1, source_target_pairs={{0,2},{1,3},{2,0},{3,1},{4,6},{5,7},{6,4},{7,5},{8,10},{9,11},{10,... | collective-permute-start | bytes 196616 | tf_op jit(solution)/shard_map/ppermute | solution.py:24
  49.7 2.6 %collective-permute-start.11 = (f32[2,16,512]{2,1,0:T(8,128)S(1)}, f32[2,16,512]{2,1,0:T(8,128)S(1)}, u32[]{:S(2)}, u32[]{:S(2)}) collective-permute-start(f32[2,16,512]{2,1,0:T(8,128)S(1)} %get-tuple-element.41), channel_id=1, source_target_pairs={{0,4},{1,5},{2,6},{3,7},{4,0},{5,1},{6,2},{7,3},{8,12},{9,13},{10,... | collective-permute-start | bytes 196616 | tf_op jit(solution)/shard_map/ppermute | solution.py:24
  52.3 0.0 collective-permute-start.12
  52.3 0.0 collective-permute-done.10.refs_1_
  52.3 3.0 %collective-permute-done.11.refs_2_ = f32[2,16,512]{2,1,0:T(8,128)S(1)} collective-permute-done((f32[2,16,512]{2,1,0:T(8,128)S(1)}, f32[2,16,512]{2,1,0:T(8,128)S(1)}, u32[]{:S(2)}, u32[]{:S(2)}) %collective-permute-start.11) | collective-permute-done | bytes 65568 | tf_op jit(solution)/shard_map/ppermute | solution.py:24
  55.3 1.5 %collective-permute-done.12.refs_3_ = f32[2,16,512]{2,1,0:T(8,128)S(1)} collective-permute-done((f32[2,16,512]{2,1,0:T(8,128)S(1)}, f32[2,16,512]{2,1,0:T(8,128)S(1)}, u32[]{:S(2)}, u32[]{:S(2)}) %collective-permute-start.12) | collective-permute-done | bytes 65568 | tf_op jit(solution)/shard_map/ppermute | solution.py:24
  56.8 0.3 gram.1
  57.1 15.0 %all_to_all.11 = f32[128,1,128]{2,1,0:T(1,128)S(1)} all-to-all(f32[128,1,128]{2,1,0:T(1,128)S(1)} %bitcast.18), channel_id=1, replica_groups=mesh['blk'=16,'group'=8] {'blk','group'}, dimensions={0} | all-to-all | bytes 131072 | tf_op jit(solution)/shard_map/all_to_all | solution.py:295
  72.1 0.0 copy-done
  72.1 0.0 copy-done.1
  72.1 1.1 %finish.1 = (f32[16,512]{1,0:T(8,128)}, f32[16,512]{1,0:T(8,128)}) custom-call(f32[128,128]{1,0:T(8,128)S(1)} %bitcast.17, f32[8,16,512]{2,1,0:T(8,128)S(1)} %get-tuple-element.39.ordered_ref, f32[16,512]{1,0:T(8,128)S(1)} %copy-done, f32[16,512]{1,0:T(8,128)S(1)} %copy-done.1), custom_call_target="tpu_custom_call" | custom-call | tf_op jit(solution)/shard_map/finish/pallas_call | solution.py:297
  (3 shorter events, 0.1 us)
Async XLA Ops:
  5.3 16.3 %collective-permute-start.2 = (f32[256,512]{1,0:T(8,128)S(1)}, f32[256,512]{1,0:T(8,128)S(1)}, u32[]{:S(2)}, u32[]{:S(2)}) collective-permute-start(f32[256,512]{1,0:T(8,128)S(1)} %get-tuple-element.30), channel_id=1, source_target_pairs={{0,96},{1,25},{2,98},{3,27},{4,100},{5,29},{6,102},{7,31},{8,104},... | collective-permute-start | bytes 1572872 | tf_op jit(solution)/shard_map/ppermute | solution.py:54
  9.9 11.6 %collective-permute-start.3 = (f32[256,512]{1,0:T(8,128)S(1)}, f32[256,512]{1,0:T(8,128)S(1)}, u32[]{:S(2)}, u32[]{:S(2)}) collective-permute-start(f32[256,512]{1,0:T(8,128)S(1)} %get-tuple-element.31), channel_id=1, source_target_pairs={{0,32},{1,9},{2,34},{3,11},{4,36},{5,13},{6,38},{7,15},{8,40},{9,1... | collective-permute-start | bytes 1572872 | tf_op jit(solution)/shard_map/ppermute | solution.py:54
  14.8 9.6 %collective-permute-start = (f32[256,512]{1,0:T(8,128)S(1)}, f32[256,512]{1,0:T(8,128)S(1)}, u32[]{:S(2)}, u32[]{:S(2)}) collective-permute-start(f32[256,512]{1,0:T(8,128)S(1)} %get-tuple-element.24), channel_id=1, source_target_pairs={{0,32},{1,9},{2,34},{3,11},{4,36},{5,13},{6,38},{7,15},{8,40},{9,1... | collective-permute-start | bytes 1572872 | tf_op jit(solution)/shard_map/ppermute | solution.py:54
  16.3 9.5 %collective-permute-start.1 = (f32[256,512]{1,0:T(8,128)S(1)}, f32[256,512]{1,0:T(8,128)S(1)}, u32[]{:S(2)}, u32[]{:S(2)}) collective-permute-start(f32[256,512]{1,0:T(8,128)S(1)} %get-tuple-element.25), channel_id=1, source_target_pairs={{0,96},{1,25},{2,98},{3,27},{4,100},{5,29},{6,102},{7,31},{8,104},... | collective-permute-start | bytes 1572872 | tf_op jit(solution)/shard_map/ppermute | solution.py:54
  21.7 9.8 %collective-permute-start.4 = (f32[256,512]{1,0:T(8,128)S(1)}, f32[256,512]{1,0:T(8,128)S(1)}, u32[]{:S(2)}, u32[]{:S(2)}) collective-permute-start(f32[256,512]{1,0:T(8,128)S(1)} %get-tuple-element.32), channel_id=1, source_target_pairs={{0,96},{1,25},{2,98},{3,27},{4,100},{5,29},{6,102},{7,31},{8,104},... | collective-permute-start | bytes 1572872 | tf_op jit(solution)/shard_map/ppermute | solution.py:54
  24.4 8.3 %collective-permute-start.5 = (f32[256,512]{1,0:T(8,128)S(1)}, f32[256,512]{1,0:T(8,128)S(1)}, u32[]{:S(2)}, u32[]{:S(2)}) collective-permute-start(f32[256,512]{1,0:T(8,128)S(1)} %get-tuple-element.33), channel_id=1, source_target_pairs={{0,32},{1,9},{2,34},{3,11},{4,36},{5,13},{6,38},{7,15},{8,40},{9,1... | collective-permute-start | bytes 1572872 | tf_op jit(solution)/shard_map/ppermute | solution.py:54
  28.6 43.6 %copy-start = (f32[16,512]{1,0:T(8,128)S(1)}, f32[16,512]{1,0:T(8,128)}, u32[]{:S(2)}) copy-start(f32[16,512]{1,0:T(8,128)} %weights_ref.1) | copy-start | bytes 98308
  28.6 43.6 %copy-start.1 = (f32[16,512]{1,0:T(8,128)S(1)}, f32[16,512]{1,0:T(8,128)}, u32[]{:S(2)}) copy-start(f32[16,512]{1,0:T(8,128)} %momentum_ref.1) | copy-start | bytes 98308
  32.8 6.8 %collective-permute-start.6 = (f32[128,512]{1,0:T(8,128)S(1)}, f32[128,512]{1,0:T(8,128)S(1)}, u32[]{:S(2)}, u32[]{:S(2)}) collective-permute-start(f32[128,512]{1,0:T(8,128)S(1)} %get-tuple-element.35), channel_id=1, source_target_pairs={{0,16},{1,65},{2,18},{3,67},{4,20},{5,69},{6,22},{7,71},{8,24},{9,... | collective-permute-start | bytes 786440 | tf_op jit(solution)/shard_map/ppermute | solution.py:54
  35.4 7.2 %collective-permute-start.7 = (f32[128,512]{1,0:T(8,128)S(1)}, f32[128,512]{1,0:T(8,128)S(1)}, u32[]{:S(2)}, u32[]{:S(2)}) collective-permute-start(f32[128,512]{1,0:T(8,128)S(1)} %get-tuple-element.36), channel_id=1, source_target_pairs={{0,8},{1,33},{2,10},{3,35},{4,12},{5,37},{6,14},{7,39},{8,0},{9,41... | collective-permute-start | bytes 786440 | tf_op jit(solution)/shard_map/ppermute | solution.py:54
  35.7 7.1 %collective-permute-start.8 = (f32[128,512]{1,0:T(8,128)S(1)}, f32[128,512]{1,0:T(8,128)S(1)}, u32[]{:S(2)}, u32[]{:S(2)}) collective-permute-start(f32[128,512]{1,0:T(8,128)S(1)} %get-tuple-element.37), channel_id=1, source_target_pairs={{0,24},{1,97},{2,26},{3,99},{4,28},{5,101},{6,30},{7,103},{8,16},{... | collective-permute-start | bytes 786440 | tf_op jit(solution)/shard_map/ppermute | solution.py:54
  42.9 5.4 %collective-permute-start.9 = (f32[4,16,512]{2,1,0:T(8,128)S(1)}, f32[4,16,512]{2,1,0:T(8,128)S(1)}, u32[]{:S(2)}, u32[]{:S(2)}) collective-permute-start(f32[4,16,512]{2,1,0:T(8,128)S(1)} %get-tuple-element.45), channel_id=1, source_target_pairs={{0,1},{1,0},{2,3},{3,2},{4,5},{5,4},{6,7},{7,6},{8,9},{9,8},{10,11... | collective-permute-start | bytes 393224 | tf_op jit(solution)/shard_map/ppermute | solution.py:24
  48.3 4.0 %collective-permute-start.10 = (f32[2,16,512]{2,1,0:T(8,128)S(1)}, f32[2,16,512]{2,1,0:T(8,128)S(1)}, u32[]{:S(2)}, u32[]{:S(2)}) collective-permute-start(f32[2,16,512]{2,1,0:T(8,128)S(1)} %get-tuple-element.42), channel_id=1, source_target_pairs={{0,2},{1,3},{2,0},{3,1},{4,6},{5,7},{6,4},{7,5},{8,10},{9,11},{10,... | collective-permute-start | bytes 196616 | tf_op jit(solution)/shard_map/ppermute | solution.py:24
  49.7 5.6 %collective-permute-start.11 = (f32[2,16,512]{2,1,0:T(8,128)S(1)}, f32[2,16,512]{2,1,0:T(8,128)S(1)}, u32[]{:S(2)}, u32[]{:S(2)}) collective-permute-start(f32[2,16,512]{2,1,0:T(8,128)S(1)} %get-tuple-element.41), channel_id=1, source_target_pairs={{0,4},{1,5},{2,6},{3,7},{4,0},{5,1},{6,2},{7,3},{8,12},{9,13},{10,... | collective-permute-start | bytes 196616 | tf_op jit(solution)/shard_map/ppermute | solution.py:24
  52.3 4.5 %collective-permute-start.12 = (f32[2,16,512]{2,1,0:T(8,128)S(1)}, f32[2,16,512]{2,1,0:T(8,128)S(1)}, u32[]{:S(2)}, u32[]{:S(2)}) collective-permute-start(f32[2,16,512]{2,1,0:T(8,128)S(1)} %get-tuple-element.40), channel_id=1, source_target_pairs={{0,6},{1,7},{2,4},{3,5},{4,2},{5,3},{6,0},{7,1},{8,14},{9,15},{10,... | collective-permute-start | bytes 196616 | tf_op jit(solution)/shard_map/ppermute | solution.py:24

commit v6 on v5

--- a/solution.py
+++ b/solution.py
@@ -54,45 +54,30 @@
     return lax.ppermute(value, ("blk", "group"), way_pairs(s, half))
 
 
-def product_kernel(units, later, held_ready, grad_ready, based, *refs):
+def product_kernel(units, grad_ready, based, *refs):
     refs = list(refs)
     act_ref, out_ref = refs.pop(0), refs.pop(0)
-    held = refs.pop(0) if held_ready else None
     base = [refs.pop(0) for _ in units] if based else ()
     pieces = [refs.pop(0) for _ in units]
     grad = out_ref if grad_ready else refs.pop(0)
-    later_held = refs.pop(0) if later else None
-    held = held if held_ready else refs.pop(0)
-    tokens = grad.shape[0]
-    chunks = tokens // DEPTH
-
-    def block_copies(units, held, k):
-        rows = pl.ds(k * DEPTH, DEPTH)
-        ends = []
-        for c, block in enumerate(piece_blocks(units)):
-            columns = pl.ds(pl.multiple_of(block * PIECE, PIECE), PIECE)
-            ends.append((act_ref.at[rows, columns], held.at[rows, pl.ds(c * PIECE, PIECE)]))
-        return ends
-
-    def started(ends, k):
-        copies = [
-            pltpu.make_async_copy(source, target, refs[0].at[k, place])
-            for place, (source, target) in enumerate(ends)
-        ]
-        for copy in copies:
-            copy.start()
-        return copies
-
+    held, sems = refs
+    chunks = grad.shape[0] // DEPTH
+    blocks = piece_blocks(units)
     copies = []
     for k in range(chunks):
         rows = pl.ds(k * DEPTH, DEPTH)
-        ends = [] if held_ready else block_copies(units, held, k)
-        if not grad_ready:
-            ends.append((out_ref.at[rows], grad.at[rows]))
-        copies.append(started(ends, k) if ends else [])
-    if later:
-        for k in range(chunks):
-            copies.append(started(block_copies(later, later_held, k), chunks + k))
+        ends = [] if grad_ready else [(out_ref.at[rows], grad.at[rows])]
+        for c, block in enumerate(blocks):
+            columns = pl.ds(pl.multiple_of(block * PIECE, PIECE), PIECE)
+            ends.append((act_ref.at[rows, columns], held.at[rows, pl.ds(c * PIECE, PIECE)]))
+        copies.append(
+            [
+                pltpu.make_async_copy(source, target, sems.at[k, place])
+                for place, (source, target) in enumerate(ends)
+            ]
+        )
+        for copy in copies[k]:
+            copy.start()
     for k in range(chunks):
         for copy in copies[k]:
             copy.wait()
@@ -106,38 +91,35 @@
                 piece[...] = base[n][...] + mine
             else:
                 piece[...] = mine
-    for chunk in copies[chunks:]:
-        for copy in chunk:
-            copy.wait()
-
-
-def products(activations, grad_out, units, later=(), held=None, grad_ready=True, base=()):
+
+
+def products(activations, grad_out, units, grad_ready=True, base=()):
     tokens, cols = grad_out.shape
-    wide = jax.ShapeDtypeStruct((tokens, 2 * PIECE * len(units)), activations.dtype)
     flat = jax.ShapeDtypeStruct((tokens, cols), grad_out.dtype)
-    chunks = tokens // DEPTH * (2 if later else 1)
-    scratch = [] if held is not None else [pltpu.VMEM(wide.shape, wide.dtype)]
-    scratch.append(pltpu.SemaphoreType.DMA((chunks, 1 + 2 * len(units))))
-
-    def placed(value, ready):
-        return pltpu.with_memory_space_constraint(value, pltpu.VMEM if ready else pltpu.HBM)
-
-    def spec(ready):
-        return pl.BlockSpec(memory_space=pltpu.VMEM if ready else pl.ANY)
-
-    ready = [] if held is None else [placed(held, True)]
     outs = [jax.ShapeDtypeStruct((2 * PIECE, cols), jnp.float32)] * len(units)
-    outs += ([] if grad_ready else [flat]) + ([wide] if later else [])
+    outs += [] if grad_ready else [flat]
+    out_space = pltpu.VMEM if grad_ready else pltpu.HBM
     return pl.pallas_call(
-        functools.partial(product_kernel, units, later, held is not None, grad_ready, bool(base)),
-        in_specs=[spec(False), spec(grad_ready)] + in_vmem(len(ready) + len(base)),
+        functools.partial(product_kernel, units, grad_ready, bool(base)),
+        in_specs=[
+            pl.BlockSpec(memory_space=pl.ANY),
+            pl.BlockSpec(memory_space=pltpu.VMEM if grad_ready else pl.ANY),
+        ]
+        + in_vmem(len(base)),
         out_specs=in_vmem(len(outs)),
         out_shape=outs,
-        scratch_shapes=scratch,
+        scratch_shapes=[
+            pltpu.VMEM((tokens, 2 * PIECE * len(units)), activations.dtype),
+            pltpu.SemaphoreType.DMA((tokens // DEPTH, 1 + 2 * len(units))),
+        ],
         compiler_params=pltpu.CompilerParams(vmem_limit_bytes=24 << 20),
         cost_estimate=pl.CostEstimate(flops=1000, bytes_accessed=1000, transcendentals=0),
         name="products",
-    )(placed(activations, False), placed(grad_out, grad_ready), *ready, *base)
+    )(
+        pltpu.with_memory_space_constraint(activations, pltpu.HBM),
+        pltpu.with_memory_space_constraint(grad_out, out_space),
+        *base,
+    )
 
 
 def relayed_kernel(*refs):
@@ -266,11 +248,11 @@
     after, own = ((1, 1), (3, 0)), ((0, 0), (0, 1))
     *far, grad = products(activations, grad_out, ((2, 0), (2, 1)), grad_ready=False)
     lower, upper = to_neighbours(far)
-    *direct, held = products(activations, grad, ((1, 0), (3, 1)), later=after)
+    direct = products(activations, grad, ((1, 0), (3, 1)))
     direct_came = to_neighbours(direct)
-    *passed, held = products(activations, grad, after, later=own, held=held)
+    passed = products(activations, grad, after)
     upper, lower = to_neighbours(relayed(passed, (upper, lower)))
-    kept = products(activations, grad, own, held=held, base=direct_came)
+    kept = products(activations, grad, own, base=direct_came)
     mine, *sent = summed(*kept, lower, upper)
     for value, s in zip(sent, ORDER):
         mine = mine + sent_over(value, s, 1)

time: 73.4 us -> 72 us (0.981)
  waiting for transfers between devices: 17.5 us -> 15.7 us
    ppermute x9, waiting for transfers between devices: 12 us -> 10.3 us  [sent_over(): return lax.ppermute(value, ('blk', 'group'), way_pairs(s, half))]
  transfers between devices with their start and end apart: 13 -> 13, of which waited for: 9 -> 10; matrix products, arithmetic and copies ran while one was open for 0% -> 0% of each run, Pallas kernels for 17% -> 19%
where the time goes in v6:
time: 72 us; the launch traced here: 71.9 us
  starting transfers between devices  20.8 us (29%)
  Pallas kernels  19.4 us (27%)
  waiting for transfers between devices  15.7 us (22%)
  blocking collectives  15 us (21%)
  between operations  0.75 us (1%)
    pallas_call x4, Pallas kernels, products(): pl.pallas_call(functools.partial(product_kernel, units, grad_ready, bool(...  17.8 us
    all_to_all x1, blocking collectives, shards(): lax.all_to_all(sums, ('blk', 'group'), split_axis=0, concat_axis=0, tiled...  15 us
    ppermute x9, starting transfers between devices, sent_over(): return lax.ppermute(value, ('blk', 'group'), way_pairs(s, half))  12.4 us
    ppermute x9, waiting for transfers between devices, sent_over(): return lax.ppermute(value, ('blk', 'group'), way_pairs(s, half))  10.3 us
    ppermute x4, starting transfers between devices, exchanged(): lax.ppermute(value, axis, [(k, k ^ mask) for k in range(lax.axis_size(axi...  8.35 us
    ppermute x4, waiting for transfers between devices, exchanged(): lax.ppermute(value, axis, [(k, k ^ mask) for k in range(lax.axis_size(axi...  5.44 us
  transfers between devices with their start and end apart: 13, of which 10 were waited for; matrix products, arithmetic and copies ran while one was open for 0% of the time, Pallas kernels for 19%

profile of v6, /device:TPU:1, one launch (start us, length us, event | category | flops | bytes accessed | tf_op | source)
XLA Modules:
  0.0 71.9 jit_solution(17684911558604645447)
XLA Ops:
  0.6 4.5 %products.4 = (f32[256,512]{1,0:T(8,128)S(1)}, f32[256,512]{1,0:T(8,128)S(1)}, bf16[4096,512]{1,0:T(8,128)(2,1)S(1)}) custom-call(bf16[4096,2048]{1,0:T(8,128)(2,1)} %refs_0_.7, bf16[4096,512]{1,0:T(8,128)(2,1)} %refs_1_.1), custom_call_target="tpu_custom_call" | custom-call | flops 1000 | bytes 1000 | tf_op jit(solution)/shard_map/products/pallas_call | solution.py:102
  5.1 4.7 %collective-permute-start.2 = (f32[256,512]{1,0:T(8,128)S(1)}, f32[256,512]{1,0:T(8,128)S(1)}, u32[]{:S(2)}, u32[]{:S(2)}) collective-permute-start(f32[256,512]{1,0:T(8,128)S(1)} %get-tuple-element.26), channel_id=1, source_target_pairs={{0,96},{1,25},{2,98},{3,27},{4,100},{5,29},{6,102},{7,31},{8,104},... | collective-permute-start | bytes 1572872 | tf_op jit(solution)/shard_map/ppermute | solution.py:54
  9.8 0.0 collective-permute-start.3
  9.8 4.4 %products.5 = (f32[256,512]{1,0:T(8,128)S(1)}, f32[256,512]{1,0:T(8,128)S(1)}) custom-call(bf16[4096,2048]{1,0:T(8,128)(2,1)} %refs_0_.7, bf16[4096,512]{1,0:T(8,128)(2,1)S(1)} %get-tuple-element.19.refs_1_), custom_call_target="tpu_custom_call" | custom-call | flops 1000 | bytes 1000 | tf_op jit(solution)/shard_map/products/pallas_call | solution.py:102
  14.2 1.5 %collective-permute-start = (f32[256,512]{1,0:T(8,128)S(1)}, f32[256,512]{1,0:T(8,128)S(1)}, u32[]{:S(2)}, u32[]{:S(2)}) collective-permute-start(f32[256,512]{1,0:T(8,128)S(1)} %get-tuple-element.20), channel_id=1, source_target_pairs={{0,32},{1,9},{2,34},{3,11},{4,36},{5,13},{6,38},{7,15},{8,40},{9,1... | collective-permute-start | bytes 1572872 | tf_op jit(solution)/shard_map/ppermute | solution.py:54
  15.8 0.1 collective-permute-start.1
  15.9 4.4 %products.7 = (f32[256,512]{1,0:T(8,128)S(1)}, f32[256,512]{1,0:T(8,128)S(1)}) custom-call(bf16[4096,2048]{1,0:T(8,128)(2,1)} %refs_0_.7, bf16[4096,512]{1,0:T(8,128)(2,1)S(1)} %get-tuple-element.19.refs_1_), custom_call_target="tpu_custom_call" | custom-call | flops 1000 | bytes 1000 | tf_op jit(solution)/shard_map/products/pallas_call | solution.py:102
  20.3 0.0 collective-permute-done.2.refs_2_
  20.3 0.0 collective-permute-done.3.refs_3_
  20.3 0.1 relayed.1
  20.4 2.7 %collective-permute-start.4 = (f32[256,512]{1,0:T(8,128)S(1)}, f32[256,512]{1,0:T(8,128)S(1)}, u32[]{:S(2)}, u32[]{:S(2)}) collective-permute-start(f32[256,512]{1,0:T(8,128)S(1)} %get-tuple-element.28), channel_id=1, source_target_pairs={{0,96},{1,25},{2,98},{3,27},{4,100},{5,29},{6,102},{7,31},{8,104},... | collective-permute-start | bytes 1572872 | tf_op jit(solution)/shard_map/ppermute | solution.py:54
  23.1 0.0 collective-permute-start.5
  23.1 0.7 collective-permute-done.refs_2_
  23.8 1.5 %collective-permute-done.1.refs_3_ = f32[256,512]{1,0:T(8,128)S(1)} collective-permute-done((f32[256,512]{1,0:T(8,128)S(1)}, f32[256,512]{1,0:T(8,128)S(1)}, u32[]{:S(2)}, u32[]{:S(2)}) %collective-permute-start.1) | collective-permute-done | bytes 524320 | tf_op jit(solution)/shard_map/ppermute | solution.py:54
  25.3 4.5 %products.6 = (f32[256,512]{1,0:T(8,128)S(1)}, f32[256,512]{1,0:T(8,128)S(1)}) custom-call(bf16[4096,2048]{1,0:T(8,128)(2,1)} %refs_0_.7, bf16[4096,512]{1,0:T(8,128)(2,1)S(1)} %get-tuple-element.19.refs_1_, f32[256,512]{1,0:T(8,128)S(1)} %collective-permute-done.refs_2_, f32[256,512]{1,0:T(8,128)S(1)} %collective-permute-done.1.refs_3_), custom_call_target="tpu_custom_call" | custom-call | flops 1000 | bytes 1000 | tf_op jit(solution)/shard_map/products/pallas_call | solution.py:102
  29.8 0.0 copy-start
  29.8 0.0 copy-start.1
  29.8 1.1 %collective-permute-done.4.lower_ref = f32[256,512]{1,0:T(8,128)S(1)} collective-permute-done((f32[256,512]{1,0:T(8,128)S(1)}, f32[256,512]{1,0:T(8,128)S(1)}, u32[]{:S(2)}, u32[]{:S(2)}) %collective-permute-start.4) | collective-permute-done | bytes 524320 | tf_op jit(solution)/shard_map/ppermute | solution.py:54
  30.9 0.5 collective-permute-done.5.upper_ref
  31.4 0.1 summed.1
  31.6 2.5 %collective-permute-start.6 = (f32[128,512]{1,0:T(8,128)S(1)}, f32[128,512]{1,0:T(8,128)S(1)}, u32[]{:S(2)}, u32[]{:S(2)}) collective-permute-start(f32[128,512]{1,0:T(8,128)S(1)} %get-tuple-element.31), channel_id=1, source_target_pairs={{0,16},{1,65},{2,18},{3,67},{4,20},{5,69},{6,22},{7,71},{8,24},{9,... | collective-permute-start | bytes 786440 | tf_op jit(solution)/shard_map/ppermute | solution.py:54
  34.1 0.3 collective-permute-start.7
  34.4 0.6 collective-permute-start.8
  35.0 3.4 %collective-permute-done.6 = f32[128,512]{1,0:T(8,128)S(1)} collective-permute-done((f32[128,512]{1,0:T(8,128)S(1)}, f32[128,512]{1,0:T(8,128)S(1)}, u32[]{:S(2)}, u32[]{:S(2)}) %collective-permute-start.6) | collective-permute-done | bytes 262176 | tf_op jit(solution)/shard_map/ppermute | solution.py:54
  38.4 2.9 %collective-permute-done.7 = f32[128,512]{1,0:T(8,128)S(1)} collective-permute-done((f32[128,512]{1,0:T(8,128)S(1)}, f32[128,512]{1,0:T(8,128)S(1)}, u32[]{:S(2)}, u32[]{:S(2)}) %collective-permute-start.7) | collective-permute-done | bytes 262176 | tf_op jit(solution)/shard_map/ppermute | solution.py:54
  41.3 0.2 collective-permute-done.8
  41.5 0.1 add_multiply_fusion
  41.6 4.4 %collective-permute-start.9 = (f32[4,16,512]{2,1,0:T(8,128)S(1)}, f32[4,16,512]{2,1,0:T(8,128)S(1)}, u32[]{:S(2)}, u32[]{:S(2)}) collective-permute-start(f32[4,16,512]{2,1,0:T(8,128)S(1)} %get-tuple-element.41), channel_id=1, source_target_pairs={{0,1},{1,0},{2,3},{3,2},{4,5},{5,4},{6,7},{7,6},{8,9},{9,8},{10,11... | collective-permute-start | bytes 393224 | tf_op jit(solution)/shard_map/ppermute | solution.py:24
  46.0 1.0 %collective-permute-done.9 = f32[4,16,512]{2,1,0:T(8,128)S(1)} collective-permute-done((f32[4,16,512]{2,1,0:T(8,128)S(1)}, f32[4,16,512]{2,1,0:T(8,128)S(1)}, u32[]{:S(2)}, u32[]{:S(2)}) %collective-permute-start.9) | collective-permute-done | bytes 131104 | tf_op jit(solution)/shard_map/ppermute | solution.py:24
  47.0 1.3 %collective-permute-start.10 = (f32[2,16,512]{2,1,0:T(8,128)S(1)}, f32[2,16,512]{2,1,0:T(8,128)S(1)}, u32[]{:S(2)}, u32[]{:S(2)}) collective-permute-start(f32[2,16,512]{2,1,0:T(8,128)S(1)} %get-tuple-element.38), channel_id=1, source_target_pairs={{0,2},{1,3},{2,0},{3,1},{4,6},{5,7},{6,4},{7,5},{8,10},{9,11},{10,... | collective-permute-start | bytes 196616 | tf_op jit(solution)/shard_map/ppermute | solution.py:24
  48.4 2.6 %collective-permute-start.11 = (f32[2,16,512]{2,1,0:T(8,128)S(1)}, f32[2,16,512]{2,1,0:T(8,128)S(1)}, u32[]{:S(2)}, u32[]{:S(2)}) collective-permute-start(f32[2,16,512]{2,1,0:T(8,128)S(1)} %get-tuple-element.37), channel_id=1, source_target_pairs={{0,4},{1,5},{2,6},{3,7},{4,0},{5,1},{6,2},{7,3},{8,12},{9,13},{10,... | collective-permute-start | bytes 196616 | tf_op jit(solution)/shard_map/ppermute | solution.py:24
  51.0 0.0 collective-permute-start.12
  51.0 0.0 collective-permute-done.10.refs_1_
  51.0 3.0 %collective-permute-done.11.refs_2_ = f32[2,16,512]{2,1,0:T(8,128)S(1)} collective-permute-done((f32[2,16,512]{2,1,0:T(8,128)S(1)}, f32[2,16,512]{2,1,0:T(8,128)S(1)}, u32[]{:S(2)}, u32[]{:S(2)}) %collective-permute-start.11) | collective-permute-done | bytes 65568 | tf_op jit(solution)/shard_map/ppermute | solution.py:24
  53.9 1.5 %collective-permute-done.12.refs_3_ = f32[2,16,512]{2,1,0:T(8,128)S(1)} collective-permute-done((f32[2,16,512]{2,1,0:T(8,128)S(1)}, f32[2,16,512]{2,1,0:T(8,128)S(1)}, u32[]{:S(2)}, u32[]{:S(2)}) %collective-permute-start.12) | collective-permute-done | bytes 65568 | tf_op jit(solution)/shard_map/ppermute | solution.py:24
  55.4 0.3 gram.1
  55.8 15.0 %all_to_all.11 = f32[128,1,128]{2,1,0:T(1,128)S(1)} all-to-all(f32[128,1,128]{2,1,0:T(1,128)S(1)} %bitcast.18), channel_id=1, replica_groups=mesh['blk'=16,'group'=8] {'blk','group'}, dimensions={0} | all-to-all | bytes 131072 | tf_op jit(solution)/shard_map/all_to_all | solution.py:277
  70.8 0.0 copy-done
  70.8 0.0 copy-done.1
  70.8 1.1 %finish.1 = (f32[16,512]{1,0:T(8,128)}, f32[16,512]{1,0:T(8,128)}) custom-call(f32[128,128]{1,0:T(8,128)S(1)} %bitcast.17, f32[8,16,512]{2,1,0:T(8,128)S(1)} %get-tuple-element.35.ordered_ref, f32[16,512]{1,0:T(8,128)S(1)} %copy-done, f32[16,512]{1,0:T(8,128)S(1)} %copy-done.1), custom_call_target="tpu_custom_call" | custom-call | tf_op jit(solution)/shard_map/finish/pallas_call | solution.py:279
  (3 shorter events, 0.1 us)
Async XLA Ops:
  5.1 15.2 %collective-permute-start.2 = (f32[256,512]{1,0:T(8,128)S(1)}, f32[256,512]{1,0:T(8,128)S(1)}, u32[]{:S(2)}, u32[]{:S(2)}) collective-permute-start(f32[256,512]{1,0:T(8,128)S(1)} %get-tuple-element.26), channel_id=1, source_target_pairs={{0,96},{1,25},{2,98},{3,27},{4,100},{5,29},{6,102},{7,31},{8,104},... | collective-permute-start | bytes 1572872 | tf_op jit(solution)/shard_map/ppermute | solution.py:54
  9.8 10.5 %collective-permute-start.3 = (f32[256,512]{1,0:T(8,128)S(1)}, f32[256,512]{1,0:T(8,128)S(1)}, u32[]{:S(2)}, u32[]{:S(2)}) collective-permute-start(f32[256,512]{1,0:T(8,128)S(1)} %get-tuple-element.27), channel_id=1, source_target_pairs={{0,32},{1,9},{2,34},{3,11},{4,36},{5,13},{6,38},{7,15},{8,40},{9,1... | collective-permute-start | bytes 1572872 | tf_op jit(solution)/shard_map/ppermute | solution.py:54
  14.2 9.5 %collective-permute-start = (f32[256,512]{1,0:T(8,128)S(1)}, f32[256,512]{1,0:T(8,128)S(1)}, u32[]{:S(2)}, u32[]{:S(2)}) collective-permute-start(f32[256,512]{1,0:T(8,128)S(1)} %get-tuple-element.20), channel_id=1, source_target_pairs={{0,32},{1,9},{2,34},{3,11},{4,36},{5,13},{6,38},{7,15},{8,40},{9,1... | collective-permute-start | bytes 1572872 | tf_op jit(solution)/shard_map/ppermute | solution.py:54
  15.8 9.5 %collective-permute-start.1 = (f32[256,512]{1,0:T(8,128)S(1)}, f32[256,512]{1,0:T(8,128)S(1)}, u32[]{:S(2)}, u32[]{:S(2)}) collective-permute-start(f32[256,512]{1,0:T(8,128)S(1)} %get-tuple-element.21), channel_id=1, source_target_pairs={{0,96},{1,25},{2,98},{3,27},{4,100},{5,29},{6,102},{7,31},{8,104},... | collective-permute-start | bytes 1572872 | tf_op jit(solution)/shard_map/ppermute | solution.py:54
  20.4 10.5 %collective-permute-start.4 = (f32[256,512]{1,0:T(8,128)S(1)}, f32[256,512]{1,0:T(8,128)S(1)}, u32[]{:S(2)}, u32[]{:S(2)}) collective-permute-start(f32[256,512]{1,0:T(8,128)S(1)} %get-tuple-element.28), channel_id=1, source_target_pairs={{0,96},{1,25},{2,98},{3,27},{4,100},{5,29},{6,102},{7,31},{8,104},... | collective-permute-start | bytes 1572872 | tf_op jit(solution)/shard_map/ppermute | solution.py:54
  23.1 8.3 %collective-permute-start.5 = (f32[256,512]{1,0:T(8,128)S(1)}, f32[256,512]{1,0:T(8,128)S(1)}, u32[]{:S(2)}, u32[]{:S(2)}) collective-permute-start(f32[256,512]{1,0:T(8,128)S(1)} %get-tuple-element.29), channel_id=1, source_target_pairs={{0,32},{1,9},{2,34},{3,11},{4,36},{5,13},{6,38},{7,15},{8,40},{9,1... | collective-permute-start | bytes 1572872 | tf_op jit(solution)/shard_map/ppermute | solution.py:54
  29.8 41.0 %copy-start = (f32[16,512]{1,0:T(8,128)S(1)}, f32[16,512]{1,0:T(8,128)}, u32[]{:S(2)}) copy-start(f32[16,512]{1,0:T(8,128)} %weights_ref.1) | copy-start | bytes 98308
  29.8 41.0 %copy-start.1 = (f32[16,512]{1,0:T(8,128)S(1)}, f32[16,512]{1,0:T(8,128)}, u32[]{:S(2)}) copy-start(f32[16,512]{1,0:T(8,128)} %momentum_ref.1) | copy-start | bytes 98308
  31.6 6.8 %collective-permute-start.6 = (f32[128,512]{1,0:T(8,128)S(1)}, f32[128,512]{1,0:T(8,128)S(1)}, u32[]{:S(2)}, u32[]{:S(2)}) collective-permute-start(f32[128,512]{1,0:T(8,128)S(1)} %get-tuple-element.31), channel_id=1, source_target_pairs={{0,16},{1,65},{2,18},{3,67},{4,20},{5,69},{6,22},{7,71},{8,24},{9,... | collective-permute-start | bytes 786440 | tf_op jit(solution)/shard_map/ppermute | solution.py:54
  34.1 7.2 %collective-permute-start.7 = (f32[128,512]{1,0:T(8,128)S(1)}, f32[128,512]{1,0:T(8,128)S(1)}, u32[]{:S(2)}, u32[]{:S(2)}) collective-permute-start(f32[128,512]{1,0:T(8,128)S(1)} %get-tuple-element.32), channel_id=1, source_target_pairs={{0,8},{1,33},{2,10},{3,35},{4,12},{5,37},{6,14},{7,39},{8,0},{9,41... | collective-permute-start | bytes 786440 | tf_op jit(solution)/shard_map/ppermute | solution.py:54
  34.4 7.1 %collective-permute-start.8 = (f32[128,512]{1,0:T(8,128)S(1)}, f32[128,512]{1,0:T(8,128)S(1)}, u32[]{:S(2)}, u32[]{:S(2)}) collective-permute-start(f32[128,512]{1,0:T(8,128)S(1)} %get-tuple-element.33), channel_id=1, source_target_pairs={{0,24},{1,97},{2,26},{3,99},{4,28},{5,101},{6,30},{7,103},{8,16},{... | collective-permute-start | bytes 786440 | tf_op jit(solution)/shard_map/ppermute | solution.py:54
  41.6 5.4 %collective-permute-start.9 = (f32[4,16,512]{2,1,0:T(8,128)S(1)}, f32[4,16,512]{2,1,0:T(8,128)S(1)}, u32[]{:S(2)}, u32[]{:S(2)}) collective-permute-start(f32[4,16,512]{2,1,0:T(8,128)S(1)} %get-tuple-element.41), channel_id=1, source_target_pairs={{0,1},{1,0},{2,3},{3,2},{4,5},{5,4},{6,7},{7,6},{8,9},{9,8},{10,11... | collective-permute-start | bytes 393224 | tf_op jit(solution)/shard_map/ppermute | solution.py:24
  47.0 4.0 %collective-permute-start.10 = (f32[2,16,512]{2,1,0:T(8,128)S(1)}, f32[2,16,512]{2,1,0:T(8,128)S(1)}, u32[]{:S(2)}, u32[]{:S(2)}) collective-permute-start(f32[2,16,512]{2,1,0:T(8,128)S(1)} %get-tuple-element.38), channel_id=1, source_target_pairs={{0,2},{1,3},{2,0},{3,1},{4,6},{5,7},{6,4},{7,5},{8,10},{9,11},{10,... | collective-permute-start | bytes 196616 | tf_op jit(solution)/shard_map/ppermute | solution.py:24
  48.4 5.6 %collective-permute-start.11 = (f32[2,16,512]{2,1,0:T(8,128)S(1)}, f32[2,16,512]{2,1,0:T(8,128)S(1)}, u32[]{:S(2)}, u32[]{:S(2)}) collective-permute-start(f32[2,16,512]{2,1,0:T(8,128)S(1)} %get-tuple-element.37), channel_id=1, source_target_pairs={{0,4},{1,5},{2,6},{3,7},{4,0},{5,1},{6,2},{7,3},{8,12},{9,13},{10,... | collective-permute-start | bytes 196616 | tf_op jit(solution)/shard_map/ppermute | solution.py:24
  51.0 4.5 %collective-permute-start.12 = (f32[2,16,512]{2,1,0:T(8,128)S(1)}, f32[2,16,512]{2,1,0:T(8,128)S(1)}, u32[]{:S(2)}, u32[]{:S(2)}) collective-permute-start(f32[2,16,512]{2,1,0:T(8,128)S(1)} %get-tuple-element.36), channel_id=1, source_target_pairs={{0,6},{1,7},{2,4},{3,5},{4,2},{5,3},{6,0},{7,1},{8,14},{9,15},{10,... | collective-permute-start | bytes 196616 | tf_op jit(solution)/shard_map/ppermute | solution.py:24

commit v7 on v6

--- a/solution.py
+++ b/solution.py
@@ -15,6 +15,7 @@
 COLS = 512
 PIECE = GROUPS * ROWS
 DEPTH = 512
+HEAD = 4
 ORDER = (2, 1, 3)
 TOTAL = 128
 CONTRACT = (((0,), (0,)), ((), ()))
@@ -54,35 +55,44 @@
     return lax.ppermute(value, ("blk", "group"), way_pairs(s, half))
 
 
-def product_kernel(units, grad_ready, based, *refs):
+def product_kernel(units, later, head_ready, grad_ready, based, *refs):
     refs = list(refs)
     act_ref, out_ref = refs.pop(0), refs.pop(0)
+    head = refs.pop(0) if head_ready else None
     base = [refs.pop(0) for _ in units] if based else ()
     pieces = [refs.pop(0) for _ in units]
     grad = out_ref if grad_ready else refs.pop(0)
+    later_head = refs.pop(0) if later else None
     held, sems = refs
     chunks = grad.shape[0] // DEPTH
-    blocks = piece_blocks(units)
     copies = []
-    for k in range(chunks):
+
+    def start(units, held, k, with_grad):
         rows = pl.ds(k * DEPTH, DEPTH)
-        ends = [] if grad_ready else [(out_ref.at[rows], grad.at[rows])]
-        for c, block in enumerate(blocks):
+        ends = [(out_ref.at[rows], grad.at[rows])] if with_grad else []
+        for c, block in enumerate(piece_blocks(units) if units else ()):
             columns = pl.ds(pl.multiple_of(block * PIECE, PIECE), PIECE)
             ends.append((act_ref.at[rows, columns], held.at[rows, pl.ds(c * PIECE, PIECE)]))
         copies.append(
             [
-                pltpu.make_async_copy(source, target, sems.at[k, place])
+                pltpu.make_async_copy(source, target, sems.at[len(copies), place])
                 for place, (source, target) in enumerate(ends)
             ]
         )
-        for copy in copies[k]:
+        for copy in copies[-1]:
             copy.start()
+
+    for k in range(chunks):
+        start(() if head_ready and k < HEAD else units, held, k, not grad_ready)
+    if later:
+        for k in range(HEAD):
+            start(later, later_head, k, False)
     for k in range(chunks):
         for copy in copies[k]:
             copy.wait()
         rows = pl.ds(k * DEPTH, DEPTH)
-        part = lax.dot_general(held[rows], grad[rows], CONTRACT, preferred_element_type=jnp.float32)
+        source = head if head_ready and k < HEAD else held
+        part = lax.dot_general(source[rows], grad[rows], CONTRACT, preferred_element_type=jnp.float32)
         for n, piece in enumerate(pieces):
             mine = part[n * 2 * PIECE : (n + 1) * 2 * PIECE]
             if k:
@@ -91,26 +101,31 @@
                 piece[...] = base[n][...] + mine
             else:
                 piece[...] = mine
-
-
-def products(activations, grad_out, units, grad_ready=True, base=()):
+    for chunk in copies[chunks:]:
+        for copy in chunk:
+            copy.wait()
+
+
+def products(activations, grad_out, units, later=(), head=None, grad_ready=True, base=()):
     tokens, cols = grad_out.shape
-    flat = jax.ShapeDtypeStruct((tokens, cols), grad_out.dtype)
+    width = 2 * PIECE * len(units)
     outs = [jax.ShapeDtypeStruct((2 * PIECE, cols), jnp.float32)] * len(units)
-    outs += [] if grad_ready else [flat]
+    outs += [] if grad_ready else [jax.ShapeDtypeStruct((tokens, cols), grad_out.dtype)]
+    outs += [jax.ShapeDtypeStruct((HEAD * DEPTH, width), activations.dtype)] if later else []
     out_space = pltpu.VMEM if grad_ready else pltpu.HBM
+    ready = [] if head is None else [pltpu.with_memory_space_constraint(head, pltpu.VMEM)]
     return pl.pallas_call(
-        functools.partial(product_kernel, units, grad_ready, bool(base)),
+        functools.partial(product_kernel, units, later, bool(ready), grad_ready, bool(base)),
         in_specs=[
             pl.BlockSpec(memory_space=pl.ANY),
             pl.BlockSpec(memory_space=pltpu.VMEM if grad_ready else pl.ANY),
         ]
-        + in_vmem(len(base)),
+        + in_vmem(len(ready) + len(base)),
         out_specs=in_vmem(len(outs)),
         out_shape=outs,
         scratch_shapes=[
-            pltpu.VMEM((tokens, 2 * PIECE * len(units)), activations.dtype),
-            pltpu.SemaphoreType.DMA((tokens // DEPTH, 1 + 2 * len(units))),
+            pltpu.VMEM((tokens, width), activations.dtype),
+            pltpu.SemaphoreType.DMA((tokens // DEPTH + HEAD, 1 + 2 * len(units))),
         ],
         compiler_params=pltpu.CompilerParams(vmem_limit_bytes=24 << 20),
         cost_estimate=pl.CostEstimate(flops=1000, bytes_accessed=1000, transcendentals=0),
@@ -118,6 +133,7 @@
     )(
         pltpu.with_memory_space_constraint(activations, pltpu.HBM),
         pltpu.with_memory_space_constraint(grad_out, out_space),
+        *ready,
         *base,
     )
 
@@ -245,12 +261,12 @@
     def to_neighbours(pair):
         return sent_over(pair[0], 1, 0), sent_over(pair[1], 3, 0)
 
-    after, own = ((1, 1), (3, 0)), ((0, 0), (0, 1))
-    *far, grad = products(activations, grad_out, ((2, 0), (2, 1)), grad_ready=False)
+    near, after, own = ((1, 0), (3, 1)), ((1, 1), (3, 0)), ((0, 0), (0, 1))
+    *far, grad, head = products(activations, grad_out, ((2, 0), (2, 1)), near, grad_ready=False)
     lower, upper = to_neighbours(far)
-    direct = products(activations, grad, ((1, 0), (3, 1)))
+    *direct, head = products(activations, grad, near, after, head)
     direct_came = to_neighbours(direct)
-    passed = products(activations, grad, after)
+    passed = products(activations, grad, after, head=head)
     upper, lower = to_neighbours(relayed(passed, (upper, lower)))
     kept = products(activations, grad, own, base=direct_came)
     mine, *sent = summed(*kept, lower, upper)

time: 72 us -> 71.8 us (level)
  transfers between devices with their start and end apart: 13 -> 13, of which waited for: 10 -> 10; matrix products, arithmetic and copies ran while one was open for 0% -> 0% of each run, Pallas kernels for 19% -> 18%
where the time goes in v7:
time: 71.8 us; the launch traced here: 71.6 us
  starting transfers between devices  20.8 us (29%)
  Pallas kernels  19.3 us (27%)
  waiting for transfers between devices  15.6 us (22%)
  blocking collectives  15 us (21%)
  between operations  0.75 us (1%)
    pallas_call x4, Pallas kernels, products(): pl.pallas_call(functools.partial(product_kernel, units, later, bool(ready...  17.7 us
    all_to_all x1, blocking collectives, shards(): lax.all_to_all(sums, ('blk', 'group'), split_axis=0, concat_axis=0, tiled...  15 us
    ppermute x9, starting transfers between devices, sent_over(): return lax.ppermute(value, ('blk', 'group'), way_pairs(s, half))  12.4 us
    ppermute x9, waiting for transfers between devices, sent_over(): return lax.ppermute(value, ('blk', 'group'), way_pairs(s, half))  10.1 us
    ppermute x4, starting transfers between devices, exchanged(): lax.ppermute(value, axis, [(k, k ^ mask) for k in range(lax.axis_size(axi...  8.35 us
    ppermute x4, waiting for transfers between devices, exchanged(): lax.ppermute(value, axis, [(k, k ^ mask) for k in range(lax.axis_size(axi...  5.44 us
  transfers between devices with their start and end apart: 13, of which 10 were waited for; matrix products, arithmetic and copies ran while one was open for 0% of the time, Pallas kernels for 18%

profile of v7, /device:TPU:1, one launch (start us, length us, event | category | flops | bytes accessed | tf_op | source)
XLA Modules:
  0.0 71.6 jit_solution(10152938032789462199)
XLA Ops:
  0.6 4.7 %products.4 = (f32[256,512]{1,0:T(8,128)S(1)}, f32[256,512]{1,0:T(8,128)S(1)}, bf16[4096,512]{1,0:T(8,128)(2,1)S(1)}, bf16[2048,512]{1,0:T(8,128)(2,1)S(1)}) custom-call(bf16[4096,2048]{1,0:T(8,128)(2,1)} %refs_0_.7, bf16[4096,512]{1,0:T(8,128)(2,1)} %refs_1_.1), custom_call_target="tpu_custom_call" | custom-call | flops 1000 | bytes 1000 | tf_op jit(solution)/shard_map/products/pallas_call | solution.py:117
  5.4 4.7 %collective-permute-start.2 = (f32[256,512]{1,0:T(8,128)S(1)}, f32[256,512]{1,0:T(8,128)S(1)}, u32[]{:S(2)}, u32[]{:S(2)}) collective-permute-start(f32[256,512]{1,0:T(8,128)S(1)} %get-tuple-element.30), channel_id=1, source_target_pairs={{0,96},{1,25},{2,98},{3,27},{4,100},{5,29},{6,102},{7,31},{8,104},... | collective-permute-start | bytes 1572872 | tf_op jit(solution)/shard_map/ppermute | solution.py:55
  10.0 0.0 collective-permute-start.3
  10.0 4.2 %products.5 = (f32[256,512]{1,0:T(8,128)S(1)}, f32[256,512]{1,0:T(8,128)S(1)}, bf16[2048,512]{1,0:T(8,128)(2,1)S(1)}) custom-call(bf16[4096,2048]{1,0:T(8,128)(2,1)} %refs_0_.7, bf16[4096,512]{1,0:T(8,128)(2,1)S(1)} %get-tuple-element.21.refs_1_, bf16[2048,512]{1,0:T(8,128)(2,1)S(1)} %get-tuple-element.22.refs_2_), custom_call_target="tpu_custom_call" | custom-call | flops 1000 | bytes 1000 | tf_op jit(solution)/shard_map/products/pallas_call | solution.py:117
  14.2 1.5 %collective-permute-start = (f32[256,512]{1,0:T(8,128)S(1)}, f32[256,512]{1,0:T(8,128)S(1)}, u32[]{:S(2)}, u32[]{:S(2)}) collective-permute-start(f32[256,512]{1,0:T(8,128)S(1)} %get-tuple-element.23), channel_id=1, source_target_pairs={{0,32},{1,9},{2,34},{3,11},{4,36},{5,13},{6,38},{7,15},{8,40},{9,1... | collective-permute-start | bytes 1572872 | tf_op jit(solution)/shard_map/ppermute | solution.py:55
  15.7 0.1 collective-permute-start.1
  15.8 4.1 %products.7 = (f32[256,512]{1,0:T(8,128)S(1)}, f32[256,512]{1,0:T(8,128)S(1)}) custom-call(bf16[4096,2048]{1,0:T(8,128)(2,1)} %refs_0_.7, bf16[4096,512]{1,0:T(8,128)(2,1)S(1)} %get-tuple-element.21.refs_1_, bf16[2048,512]{1,0:T(8,128)(2,1)S(1)} %get-tuple-element.27.refs_2_), custom_call_target="tpu_custom_call" | custom-call | flops 1000 | bytes 1000 | tf_op jit(solution)/shard_map/products/pallas_call | solution.py:117
  20.0 0.0 collective-permute-done.2.refs_2_
  20.0 0.0 collective-permute-done.3.refs_3_
  20.0 0.1 relayed.1
  20.1 2.7 %collective-permute-start.4 = (f32[256,512]{1,0:T(8,128)S(1)}, f32[256,512]{1,0:T(8,128)S(1)}, u32[]{:S(2)}, u32[]{:S(2)}) collective-permute-start(f32[256,512]{1,0:T(8,128)S(1)} %get-tuple-element.32), channel_id=1, source_target_pairs={{0,96},{1,25},{2,98},{3,27},{4,100},{5,29},{6,102},{7,31},{8,104},... | collective-permute-start | bytes 1572872 | tf_op jit(solution)/shard_map/ppermute | solution.py:55
  22.8 0.0 collective-permute-start.5
  22.8 1.2 %collective-permute-done.refs_2_ = f32[256,512]{1,0:T(8,128)S(1)} collective-permute-done((f32[256,512]{1,0:T(8,128)S(1)}, f32[256,512]{1,0:T(8,128)S(1)}, u32[]{:S(2)}, u32[]{:S(2)}) %collective-permute-start) | collective-permute-done | bytes 524320 | tf_op jit(solution)/shard_map/ppermute | solution.py:55
  24.0 1.3 %collective-permute-done.1.refs_3_ = f32[256,512]{1,0:T(8,128)S(1)} collective-permute-done((f32[256,512]{1,0:T(8,128)S(1)}, f32[256,512]{1,0:T(8,128)S(1)}, u32[]{:S(2)}, u32[]{:S(2)}) %collective-permute-start.1) | collective-permute-done | bytes 524320 | tf_op jit(solution)/shard_map/ppermute | solution.py:55
  25.3 4.6 %products.6 = (f32[256,512]{1,0:T(8,128)S(1)}, f32[256,512]{1,0:T(8,128)S(1)}) custom-call(bf16[4096,2048]{1,0:T(8,128)(2,1)} %refs_0_.7, bf16[4096,512]{1,0:T(8,128)(2,1)S(1)} %get-tuple-element.21.refs_1_, f32[256,512]{1,0:T(8,128)S(1)} %collective-permute-done.refs_2_, f32[256,512]{1,0:T(8,128)S(1)} %collective-permute-done.1.refs_3_), custom_call_target="tpu_custom_call" | custom-call | flops 1000 | bytes 1000 | tf_op jit(solution)/shard_map/products/pallas_call | solution.py:117
  29.9 0.0 copy-start
  30.0 0.0 copy-start.1
  30.0 0.9 %collective-permute-done.4.lower_ref = f32[256,512]{1,0:T(8,128)S(1)} collective-permute-done((f32[256,512]{1,0:T(8,128)S(1)}, f32[256,512]{1,0:T(8,128)S(1)}, u32[]{:S(2)}, u32[]{:S(2)}) %collective-permute-start.4) | collective-permute-done | bytes 524320 | tf_op jit(solution)/shard_map/ppermute | solution.py:55
  30.9 0.2 collective-permute-done.5.upper_ref
  31.1 0.1 summed.1
  31.3 2.5 %collective-permute-start.6 = (f32[128,512]{1,0:T(8,128)S(1)}, f32[128,512]{1,0:T(8,128)S(1)}, u32[]{:S(2)}, u32[]{:S(2)}) collective-permute-start(f32[128,512]{1,0:T(8,128)S(1)} %get-tuple-element.35), channel_id=1, source_target_pairs={{0,16},{1,65},{2,18},{3,67},{4,20},{5,69},{6,22},{7,71},{8,24},{9,... | collective-permute-start | bytes 786440 | tf_op jit(solution)/shard_map/ppermute | solution.py:55
  33.8 0.3 collective-permute-start.7
  34.1 0.6 collective-permute-start.8
  34.7 3.4 %collective-permute-done.6 = f32[128,512]{1,0:T(8,128)S(1)} collective-permute-done((f32[128,512]{1,0:T(8,128)S(1)}, f32[128,512]{1,0:T(8,128)S(1)}, u32[]{:S(2)}, u32[]{:S(2)}) %collective-permute-start.6) | collective-permute-done | bytes 262176 | tf_op jit(solution)/shard_map/ppermute | solution.py:55
  38.1 2.9 %collective-permute-done.7 = f32[128,512]{1,0:T(8,128)S(1)} collective-permute-done((f32[128,512]{1,0:T(8,128)S(1)}, f32[128,512]{1,0:T(8,128)S(1)}, u32[]{:S(2)}, u32[]{:S(2)}) %collective-permute-start.7) | collective-permute-done | bytes 262176 | tf_op jit(solution)/shard_map/ppermute | solution.py:55
  41.0 0.2 collective-permute-done.8
  41.2 0.1 add_multiply_fusion
  41.3 4.4 %collective-permute-start.9 = (f32[4,16,512]{2,1,0:T(8,128)S(1)}, f32[4,16,512]{2,1,0:T(8,128)S(1)}, u32[]{:S(2)}, u32[]{:S(2)}) collective-permute-start(f32[4,16,512]{2,1,0:T(8,128)S(1)} %get-tuple-element.45), channel_id=1, source_target_pairs={{0,1},{1,0},{2,3},{3,2},{4,5},{5,4},{6,7},{7,6},{8,9},{9,8},{10,11... | collective-permute-start | bytes 393224 | tf_op jit(solution)/shard_map/ppermute | solution.py:25
  45.7 1.0 %collective-permute-done.9 = f32[4,16,512]{2,1,0:T(8,128)S(1)} collective-permute-done((f32[4,16,512]{2,1,0:T(8,128)S(1)}, f32[4,16,512]{2,1,0:T(8,128)S(1)}, u32[]{:S(2)}, u32[]{:S(2)}) %collective-permute-start.9) | collective-permute-done | bytes 131104 | tf_op jit(solution)/shard_map/ppermute | solution.py:25
  46.7 1.4 %collective-permute-start.10 = (f32[2,16,512]{2,1,0:T(8,128)S(1)}, f32[2,16,512]{2,1,0:T(8,128)S(1)}, u32[]{:S(2)}, u32[]{:S(2)}) collective-permute-start(f32[2,16,512]{2,1,0:T(8,128)S(1)} %get-tuple-element.42), channel_id=1, source_target_pairs={{0,2},{1,3},{2,0},{3,1},{4,6},{5,7},{6,4},{7,5},{8,10},{9,11},{10,... | collective-permute-start | bytes 196616 | tf_op jit(solution)/shard_map/ppermute | solution.py:25
  48.1 2.6 %collective-permute-start.11 = (f32[2,16,512]{2,1,0:T(8,128)S(1)}, f32[2,16,512]{2,1,0:T(8,128)S(1)}, u32[]{:S(2)}, u32[]{:S(2)}) collective-permute-start(f32[2,16,512]{2,1,0:T(8,128)S(1)} %get-tuple-element.41), channel_id=1, source_target_pairs={{0,4},{1,5},{2,6},{3,7},{4,0},{5,1},{6,2},{7,3},{8,12},{9,13},{10,... | collective-permute-start | bytes 196616 | tf_op jit(solution)/shard_map/ppermute | solution.py:25
  50.7 0.0 collective-permute-start.12
  50.7 0.0 collective-permute-done.10.refs_1_
  50.7 3.0 %collective-permute-done.11.refs_2_ = f32[2,16,512]{2,1,0:T(8,128)S(1)} collective-permute-done((f32[2,16,512]{2,1,0:T(8,128)S(1)}, f32[2,16,512]{2,1,0:T(8,128)S(1)}, u32[]{:S(2)}, u32[]{:S(2)}) %collective-permute-start.11) | collective-permute-done | bytes 65568 | tf_op jit(solution)/shard_map/ppermute | solution.py:25
  53.7 1.5 %collective-permute-done.12.refs_3_ = f32[2,16,512]{2,1,0:T(8,128)S(1)} collective-permute-done((f32[2,16,512]{2,1,0:T(8,128)S(1)}, f32[2,16,512]{2,1,0:T(8,128)S(1)}, u32[]{:S(2)}, u32[]{:S(2)}) %collective-permute-start.12) | collective-permute-done | bytes 65568 | tf_op jit(solution)/shard_map/ppermute | solution.py:25
  55.1 0.3 gram.1
  55.5 15.0 %all_to_all.11 = f32[128,1,128]{2,1,0:T(1,128)S(1)} all-to-all(f32[128,1,128]{2,1,0:T(1,128)S(1)} %bitcast.18), channel_id=1, replica_groups=mesh['blk'=16,'group'=8] {'blk','group'}, dimensions={0} | all-to-all | bytes 131072 | tf_op jit(solution)/shard_map/all_to_all | solution.py:293
  70.5 0.0 copy-done
  70.5 0.0 copy-done.1
  70.5 1.1 %finish.1 = (f32[16,512]{1,0:T(8,128)}, f32[16,512]{1,0:T(8,128)}) custom-call(f32[128,128]{1,0:T(8,128)S(1)} %bitcast.17, f32[8,16,512]{2,1,0:T(8,128)S(1)} %get-tuple-element.39.ordered_ref, f32[16,512]{1,0:T(8,128)S(1)} %copy-done, f32[16,512]{1,0:T(8,128)S(1)} %copy-done.1), custom_call_target="tpu_custom_call" | custom-call | tf_op jit(solution)/shard_map/finish/pallas_call | solution.py:295
  (3 shorter events, 0.1 us)
Async XLA Ops:
  5.4 14.6 %collective-permute-start.2 = (f32[256,512]{1,0:T(8,128)S(1)}, f32[256,512]{1,0:T(8,128)S(1)}, u32[]{:S(2)}, u32[]{:S(2)}) collective-permute-start(f32[256,512]{1,0:T(8,128)S(1)} %get-tuple-element.30), channel_id=1, source_target_pairs={{0,96},{1,25},{2,98},{3,27},{4,100},{5,29},{6,102},{7,31},{8,104},... | collective-permute-start | bytes 1572872 | tf_op jit(solution)/shard_map/ppermute | solution.py:55
  10.0 10.0 %collective-permute-start.3 = (f32[256,512]{1,0:T(8,128)S(1)}, f32[256,512]{1,0:T(8,128)S(1)}, u32[]{:S(2)}, u32[]{:S(2)}) collective-permute-start(f32[256,512]{1,0:T(8,128)S(1)} %get-tuple-element.31), channel_id=1, source_target_pairs={{0,32},{1,9},{2,34},{3,11},{4,36},{5,13},{6,38},{7,15},{8,40},{9,1... | collective-permute-start | bytes 1572872 | tf_op jit(solution)/shard_map/ppermute | solution.py:55
  14.2 9.8 %collective-permute-start = (f32[256,512]{1,0:T(8,128)S(1)}, f32[256,512]{1,0:T(8,128)S(1)}, u32[]{:S(2)}, u32[]{:S(2)}) collective-permute-start(f32[256,512]{1,0:T(8,128)S(1)} %get-tuple-element.23), channel_id=1, source_target_pairs={{0,32},{1,9},{2,34},{3,11},{4,36},{5,13},{6,38},{7,15},{8,40},{9,1... | collective-permute-start | bytes 1572872 | tf_op jit(solution)/shard_map/ppermute | solution.py:55
  15.7 9.5 %collective-permute-start.1 = (f32[256,512]{1,0:T(8,128)S(1)}, f32[256,512]{1,0:T(8,128)S(1)}, u32[]{:S(2)}, u32[]{:S(2)}) collective-permute-start(f32[256,512]{1,0:T(8,128)S(1)} %get-tuple-element.24), channel_id=1, source_target_pairs={{0,96},{1,25},{2,98},{3,27},{4,100},{5,29},{6,102},{7,31},{8,104},... | collective-permute-start | bytes 1572872 | tf_op jit(solution)/shard_map/ppermute | solution.py:55
  20.1 10.8 %collective-permute-start.4 = (f32[256,512]{1,0:T(8,128)S(1)}, f32[256,512]{1,0:T(8,128)S(1)}, u32[]{:S(2)}, u32[]{:S(2)}) collective-permute-start(f32[256,512]{1,0:T(8,128)S(1)} %get-tuple-element.32), channel_id=1, source_target_pairs={{0,96},{1,25},{2,98},{3,27},{4,100},{5,29},{6,102},{7,31},{8,104},... | collective-permute-start | bytes 1572872 | tf_op jit(solution)/shard_map/ppermute | solution.py:55
  22.8 8.3 %collective-permute-start.5 = (f32[256,512]{1,0:T(8,128)S(1)}, f32[256,512]{1,0:T(8,128)S(1)}, u32[]{:S(2)}, u32[]{:S(2)}) collective-permute-start(f32[256,512]{1,0:T(8,128)S(1)} %get-tuple-element.33), channel_id=1, source_target_pairs={{0,32},{1,9},{2,34},{3,11},{4,36},{5,13},{6,38},{7,15},{8,40},{9,1... | collective-permute-start | bytes 1572872 | tf_op jit(solution)/shard_map/ppermute | solution.py:55
  29.9 40.6 %copy-start = (f32[16,512]{1,0:T(8,128)S(1)}, f32[16,512]{1,0:T(8,128)}, u32[]{:S(2)}) copy-start(f32[16,512]{1,0:T(8,128)} %weights_ref.1) | copy-start | bytes 98308
  30.0 40.6 %copy-start.1 = (f32[16,512]{1,0:T(8,128)S(1)}, f32[16,512]{1,0:T(8,128)}, u32[]{:S(2)}) copy-start(f32[16,512]{1,0:T(8,128)} %momentum_ref.1) | copy-start | bytes 98308
  31.3 6.8 %collective-permute-start.6 = (f32[128,512]{1,0:T(8,128)S(1)}, f32[128,512]{1,0:T(8,128)S(1)}, u32[]{:S(2)}, u32[]{:S(2)}) collective-permute-start(f32[128,512]{1,0:T(8,128)S(1)} %get-tuple-element.35), channel_id=1, source_target_pairs={{0,16},{1,65},{2,18},{3,67},{4,20},{5,69},{6,22},{7,71},{8,24},{9,... | collective-permute-start | bytes 786440 | tf_op jit(solution)/shard_map/ppermute | solution.py:55
  33.8 7.2 %collective-permute-start.7 = (f32[128,512]{1,0:T(8,128)S(1)}, f32[128,512]{1,0:T(8,128)S(1)}, u32[]{:S(2)}, u32[]{:S(2)}) collective-permute-start(f32[128,512]{1,0:T(8,128)S(1)} %get-tuple-element.36), channel_id=1, source_target_pairs={{0,8},{1,33},{2,10},{3,35},{4,12},{5,37},{6,14},{7,39},{8,0},{9,41... | collective-permute-start | bytes 786440 | tf_op jit(solution)/shard_map/ppermute | solution.py:55
  34.1 7.1 %collective-permute-start.8 = (f32[128,512]{1,0:T(8,128)S(1)}, f32[128,512]{1,0:T(8,128)S(1)}, u32[]{:S(2)}, u32[]{:S(2)}) collective-permute-start(f32[128,512]{1,0:T(8,128)S(1)} %get-tuple-element.37), channel_id=1, source_target_pairs={{0,24},{1,97},{2,26},{3,99},{4,28},{5,101},{6,30},{7,103},{8,16},{... | collective-permute-start | bytes 786440 | tf_op jit(solution)/shard_map/ppermute | solution.py:55
  41.3 5.4 %collective-permute-start.9 = (f32[4,16,512]{2,1,0:T(8,128)S(1)}, f32[4,16,512]{2,1,0:T(8,128)S(1)}, u32[]{:S(2)}, u32[]{:S(2)}) collective-permute-start(f32[4,16,512]{2,1,0:T(8,128)S(1)} %get-tuple-element.45), channel_id=1, source_target_pairs={{0,1},{1,0},{2,3},{3,2},{4,5},{5,4},{6,7},{7,6},{8,9},{9,8},{10,11... | collective-permute-start | bytes 393224 | tf_op jit(solution)/shard_map/ppermute | solution.py:25
  46.7 4.0 %collective-permute-start.10 = (f32[2,16,512]{2,1,0:T(8,128)S(1)}, f32[2,16,512]{2,1,0:T(8,128)S(1)}, u32[]{:S(2)}, u32[]{:S(2)}) collective-permute-start(f32[2,16,512]{2,1,0:T(8,128)S(1)} %get-tuple-element.42), channel_id=1, source_target_pairs={{0,2},{1,3},{2,0},{3,1},{4,6},{5,7},{6,4},{7,5},{8,10},{9,11},{10,... | collective-permute-start | bytes 196616 | tf_op jit(solution)/shard_map/ppermute | solution.py:25
  48.1 5.6 %collective-permute-start.11 = (f32[2,16,512]{2,1,0:T(8,128)S(1)}, f32[2,16,512]{2,1,0:T(8,128)S(1)}, u32[]{:S(2)}, u32[]{:S(2)}) collective-permute-start(f32[2,16,512]{2,1,0:T(8,128)S(1)} %get-tuple-element.41), channel_id=1, source_target_pairs={{0,4},{1,5},{2,6},{3,7},{4,0},{5,1},{6,2},{7,3},{8,12},{9,13},{10,... | collective-permute-start | bytes 196616 | tf_op jit(solution)/shard_map/ppermute | solution.py:25
  50.7 4.5 %collective-permute-start.12 = (f32[2,16,512]{2,1,0:T(8,128)S(1)}, f32[2,16,512]{2,1,0:T(8,128)S(1)}, u32[]{:S(2)}, u32[]{:S(2)}) collective-permute-start(f32[2,16,512]{2,1,0:T(8,128)S(1)} %get-tuple-element.40), channel_id=1, source_target_pairs={{0,6},{1,7},{2,4},{3,5},{4,2},{5,3},{6,0},{7,1},{8,14},{9,15},{10,... | collective-permute-start | bytes 196616 | tf_op jit(solution)/shard_map/ppermute | solution.py:25

commit v8 on v7

--- a/solution.py
+++ b/solution.py
@@ -15,7 +15,7 @@
 COLS = 512
 PIECE = GROUPS * ROWS
 DEPTH = 512
-HEAD = 4
+HEAD = 6
 ORDER = (2, 1, 3)
 TOTAL = 128
 CONTRACT = (((0,), (0,)), ((), ()))

time: 71.8 us -> 72.4 us (level)
  transfers between devices with their start and end apart: 13 -> 13, of which waited for: 10 -> 10; matrix products, arithmetic and copies ran while one was open for 0% -> 0% of each run, Pallas kernels for 18% -> 19%
where the time goes in v8:
time: 72.4 us; the launch traced here: 72.3 us
  starting transfers between devices  20.8 us (29%)
  Pallas kernels  20 us (28%)
  waiting for transfers between devices  15.5 us (21%)
  blocking collectives  15 us (21%)
  between operations  0.75 us (1%)
    pallas_call x4, Pallas kernels, products(): pl.pallas_call(functools.partial(product_kernel, units, later, bool(ready...  18.4 us
    all_to_all x1, blocking collectives, shards(): lax.all_to_all(sums, ('blk', 'group'), split_axis=0, concat_axis=0, tiled...  15 us
    ppermute x9, starting transfers between devices, sent_over(): return lax.ppermute(value, ('blk', 'group'), way_pairs(s, half))  12.4 us
    ppermute x9, waiting for transfers between devices, sent_over(): return lax.ppermute(value, ('blk', 'group'), way_pairs(s, half))  10 us
    ppermute x4, starting transfers between devices, exchanged(): lax.ppermute(value, axis, [(k, k ^ mask) for k in range(lax.axis_size(axi...  8.36 us
    ppermute x4, waiting for transfers between devices, exchanged(): lax.ppermute(value, axis, [(k, k ^ mask) for k in range(lax.axis_size(axi...  5.44 us
  transfers between devices with their start and end apart: 13, of which 10 were waited for; matrix products, arithmetic and copies ran while one was open for 0% of the time, Pallas kernels for 19%

profile of v8, /device:TPU:1, one launch (start us, length us, event | category | flops | bytes accessed | tf_op | source)
XLA Modules:
  0.0 72.3 jit_solution(13688647308412193719)
XLA Ops:
  0.6 5.1 %products.4 = (f32[256,512]{1,0:T(8,128)S(1)}, f32[256,512]{1,0:T(8,128)S(1)}, bf16[4096,512]{1,0:T(8,128)(2,1)S(1)}, bf16[3072,512]{1,0:T(8,128)(2,1)S(1)}) custom-call(bf16[4096,2048]{1,0:T(8,128)(2,1)} %refs_0_.7, bf16[4096,512]{1,0:T(8,128)(2,1)} %refs_1_.1), custom_call_target="tpu_custom_call" | custom-call | flops 1000 | bytes 1000 | tf_op jit(solution)/shard_map/products/pallas_call | solution.py:117
  5.7 4.7 %collective-permute-start.2 = (f32[256,512]{1,0:T(8,128)S(1)}, f32[256,512]{1,0:T(8,128)S(1)}, u32[]{:S(2)}, u32[]{:S(2)}) collective-permute-start(f32[256,512]{1,0:T(8,128)S(1)} %get-tuple-element.30), channel_id=1, source_target_pairs={{0,96},{1,25},{2,98},{3,27},{4,100},{5,29},{6,102},{7,31},{8,104},... | collective-permute-start | bytes 1572872 | tf_op jit(solution)/shard_map/ppermute | solution.py:55
  10.4 0.0 collective-permute-start.3
  10.4 4.5 %products.5 = (f32[256,512]{1,0:T(8,128)S(1)}, f32[256,512]{1,0:T(8,128)S(1)}, bf16[3072,512]{1,0:T(8,128)(2,1)S(1)}) custom-call(bf16[4096,2048]{1,0:T(8,128)(2,1)} %refs_0_.7, bf16[4096,512]{1,0:T(8,128)(2,1)S(1)} %get-tuple-element.21.refs_1_, bf16[3072,512]{1,0:T(8,128)(2,1)S(1)} %get-tuple-element.22.refs_2_), custom_call_target="tpu_custom_call" | custom-call | flops 1000 | bytes 1000 | tf_op jit(solution)/shard_map/products/pallas_call | solution.py:117
  14.9 1.5 %collective-permute-start = (f32[256,512]{1,0:T(8,128)S(1)}, f32[256,512]{1,0:T(8,128)S(1)}, u32[]{:S(2)}, u32[]{:S(2)}) collective-permute-start(f32[256,512]{1,0:T(8,128)S(1)} %get-tuple-element.23), channel_id=1, source_target_pairs={{0,32},{1,9},{2,34},{3,11},{4,36},{5,13},{6,38},{7,15},{8,40},{9,1... | collective-permute-start | bytes 1572872 | tf_op jit(solution)/shard_map/ppermute | solution.py:55
  16.4 0.1 collective-permute-start.1
  16.5 4.1 %products.7 = (f32[256,512]{1,0:T(8,128)S(1)}, f32[256,512]{1,0:T(8,128)S(1)}) custom-call(bf16[4096,2048]{1,0:T(8,128)(2,1)} %refs_0_.7, bf16[4096,512]{1,0:T(8,128)(2,1)S(1)} %get-tuple-element.21.refs_1_, bf16[3072,512]{1,0:T(8,128)(2,1)S(1)} %get-tuple-element.27.refs_2_), custom_call_target="tpu_custom_call" | custom-call | flops 1000 | bytes 1000 | tf_op jit(solution)/shard_map/products/pallas_call | solution.py:117
  20.6 0.0 collective-permute-done.2.refs_2_
  20.6 0.0 collective-permute-done.3.refs_3_
  20.6 0.1 relayed.1
  20.7 2.7 %collective-permute-start.4 = (f32[256,512]{1,0:T(8,128)S(1)}, f32[256,512]{1,0:T(8,128)S(1)}, u32[]{:S(2)}, u32[]{:S(2)}) collective-permute-start(f32[256,512]{1,0:T(8,128)S(1)} %get-tuple-element.32), channel_id=1, source_target_pairs={{0,96},{1,25},{2,98},{3,27},{4,100},{5,29},{6,102},{7,31},{8,104},... | collective-permute-start | bytes 1572872 | tf_op jit(solution)/shard_map/ppermute | solution.py:55
  23.4 0.0 collective-permute-start.5
  23.4 0.9 %collective-permute-done.refs_2_ = f32[256,512]{1,0:T(8,128)S(1)} collective-permute-done((f32[256,512]{1,0:T(8,128)S(1)}, f32[256,512]{1,0:T(8,128)S(1)}, u32[]{:S(2)}, u32[]{:S(2)}) %collective-permute-start) | collective-permute-done | bytes 524320 | tf_op jit(solution)/shard_map/ppermute | solution.py:55
  24.3 1.6 %collective-permute-done.1.refs_3_ = f32[256,512]{1,0:T(8,128)S(1)} collective-permute-done((f32[256,512]{1,0:T(8,128)S(1)}, f32[256,512]{1,0:T(8,128)S(1)}, u32[]{:S(2)}, u32[]{:S(2)}) %collective-permute-start.1) | collective-permute-done | bytes 524320 | tf_op jit(solution)/shard_map/ppermute | solution.py:55
  26.0 4.7 %products.6 = (f32[256,512]{1,0:T(8,128)S(1)}, f32[256,512]{1,0:T(8,128)S(1)}) custom-call(bf16[4096,2048]{1,0:T(8,128)(2,1)} %refs_0_.7, bf16[4096,512]{1,0:T(8,128)(2,1)S(1)} %get-tuple-element.21.refs_1_, f32[256,512]{1,0:T(8,128)S(1)} %collective-permute-done.refs_2_, f32[256,512]{1,0:T(8,128)S(1)} %collective-permute-done.1.refs_3_), custom_call_target="tpu_custom_call" | custom-call | flops 1000 | bytes 1000 | tf_op jit(solution)/shard_map/products/pallas_call | solution.py:117
  30.7 0.0 copy-start
  30.7 0.0 copy-start.1
  30.8 0.8 %collective-permute-done.4.lower_ref = f32[256,512]{1,0:T(8,128)S(1)} collective-permute-done((f32[256,512]{1,0:T(8,128)S(1)}, f32[256,512]{1,0:T(8,128)S(1)}, u32[]{:S(2)}, u32[]{:S(2)}) %collective-permute-start.4) | collective-permute-done | bytes 524320 | tf_op jit(solution)/shard_map/ppermute | solution.py:55
  31.6 0.1 collective-permute-done.5.upper_ref
  31.7 0.1 summed.1
  31.9 2.5 %collective-permute-start.6 = (f32[128,512]{1,0:T(8,128)S(1)}, f32[128,512]{1,0:T(8,128)S(1)}, u32[]{:S(2)}, u32[]{:S(2)}) collective-permute-start(f32[128,512]{1,0:T(8,128)S(1)} %get-tuple-element.35), channel_id=1, source_target_pairs={{0,16},{1,65},{2,18},{3,67},{4,20},{5,69},{6,22},{7,71},{8,24},{9,... | collective-permute-start | bytes 786440 | tf_op jit(solution)/shard_map/ppermute | solution.py:55
  34.4 0.3 collective-permute-start.7
  34.7 0.6 collective-permute-start.8
  35.3 3.4 %collective-permute-done.6 = f32[128,512]{1,0:T(8,128)S(1)} collective-permute-done((f32[128,512]{1,0:T(8,128)S(1)}, f32[128,512]{1,0:T(8,128)S(1)}, u32[]{:S(2)}, u32[]{:S(2)}) %collective-permute-start.6) | collective-permute-done | bytes 262176 | tf_op jit(solution)/shard_map/ppermute | solution.py:55
  38.7 2.9 %collective-permute-done.7 = f32[128,512]{1,0:T(8,128)S(1)} collective-permute-done((f32[128,512]{1,0:T(8,128)S(1)}, f32[128,512]{1,0:T(8,128)S(1)}, u32[]{:S(2)}, u32[]{:S(2)}) %collective-permute-start.7) | collective-permute-done | bytes 262176 | tf_op jit(solution)/shard_map/ppermute | solution.py:55
  41.6 0.2 collective-permute-done.8
  41.8 0.1 add_multiply_fusion
  41.9 4.4 %collective-permute-start.9 = (f32[4,16,512]{2,1,0:T(8,128)S(1)}, f32[4,16,512]{2,1,0:T(8,128)S(1)}, u32[]{:S(2)}, u32[]{:S(2)}) collective-permute-start(f32[4,16,512]{2,1,0:T(8,128)S(1)} %get-tuple-element.45), channel_id=1, source_target_pairs={{0,1},{1,0},{2,3},{3,2},{4,5},{5,4},{6,7},{7,6},{8,9},{9,8},{10,11... | collective-permute-start | bytes 393224 | tf_op jit(solution)/shard_map/ppermute | solution.py:25
  46.3 1.0 %collective-permute-done.9 = f32[4,16,512]{2,1,0:T(8,128)S(1)} collective-permute-done((f32[4,16,512]{2,1,0:T(8,128)S(1)}, f32[4,16,512]{2,1,0:T(8,128)S(1)}, u32[]{:S(2)}, u32[]{:S(2)}) %collective-permute-start.9) | collective-permute-done | bytes 131104 | tf_op jit(solution)/shard_map/ppermute | solution.py:25
  47.3 1.4 %collective-permute-start.10 = (f32[2,16,512]{2,1,0:T(8,128)S(1)}, f32[2,16,512]{2,1,0:T(8,128)S(1)}, u32[]{:S(2)}, u32[]{:S(2)}) collective-permute-start(f32[2,16,512]{2,1,0:T(8,128)S(1)} %get-tuple-element.42), channel_id=1, source_target_pairs={{0,2},{1,3},{2,0},{3,1},{4,6},{5,7},{6,4},{7,5},{8,10},{9,11},{10,... | collective-permute-start | bytes 196616 | tf_op jit(solution)/shard_map/ppermute | solution.py:25
  48.7 2.6 %collective-permute-start.11 = (f32[2,16,512]{2,1,0:T(8,128)S(1)}, f32[2,16,512]{2,1,0:T(8,128)S(1)}, u32[]{:S(2)}, u32[]{:S(2)}) collective-permute-start(f32[2,16,512]{2,1,0:T(8,128)S(1)} %get-tuple-element.41), channel_id=1, source_target_pairs={{0,4},{1,5},{2,6},{3,7},{4,0},{5,1},{6,2},{7,3},{8,12},{9,13},{10,... | collective-permute-start | bytes 196616 | tf_op jit(solution)/shard_map/ppermute | solution.py:25
  51.3 0.0 collective-permute-start.12
  51.3 0.0 collective-permute-done.10.refs_1_
  51.3 3.0 %collective-permute-done.11.refs_2_ = f32[2,16,512]{2,1,0:T(8,128)S(1)} collective-permute-done((f32[2,16,512]{2,1,0:T(8,128)S(1)}, f32[2,16,512]{2,1,0:T(8,128)S(1)}, u32[]{:S(2)}, u32[]{:S(2)}) %collective-permute-start.11) | collective-permute-done | bytes 65568 | tf_op jit(solution)/shard_map/ppermute | solution.py:25
  54.3 1.5 %collective-permute-done.12.refs_3_ = f32[2,16,512]{2,1,0:T(8,128)S(1)} collective-permute-done((f32[2,16,512]{2,1,0:T(8,128)S(1)}, f32[2,16,512]{2,1,0:T(8,128)S(1)}, u32[]{:S(2)}, u32[]{:S(2)}) %collective-permute-start.12) | collective-permute-done | bytes 65568 | tf_op jit(solution)/shard_map/ppermute | solution.py:25
  55.8 0.3 gram.1
  56.1 15.0 %all_to_all.11 = f32[128,1,128]{2,1,0:T(1,128)S(1)} all-to-all(f32[128,1,128]{2,1,0:T(1,128)S(1)} %bitcast.18), channel_id=1, replica_groups=mesh['blk'=16,'group'=8] {'blk','group'}, dimensions={0} | all-to-all | bytes 131072 | tf_op jit(solution)/shard_map/all_to_all | solution.py:293
  71.2 0.0 copy-done
  71.2 0.0 copy-done.1
  71.2 1.1 %finish.1 = (f32[16,512]{1,0:T(8,128)}, f32[16,512]{1,0:T(8,128)}) custom-call(f32[128,128]{1,0:T(8,128)S(1)} %bitcast.17, f32[8,16,512]{2,1,0:T(8,128)S(1)} %get-tuple-element.39.ordered_ref, f32[16,512]{1,0:T(8,128)S(1)} %copy-done, f32[16,512]{1,0:T(8,128)S(1)} %copy-done.1), custom_call_target="tpu_custom_call" | custom-call | tf_op jit(solution)/shard_map/finish/pallas_call | solution.py:295
  (3 shorter events, 0.1 us)
Async XLA Ops:
  5.7 14.9 %collective-permute-start.2 = (f32[256,512]{1,0:T(8,128)S(1)}, f32[256,512]{1,0:T(8,128)S(1)}, u32[]{:S(2)}, u32[]{:S(2)}) collective-permute-start(f32[256,512]{1,0:T(8,128)S(1)} %get-tuple-element.30), channel_id=1, source_target_pairs={{0,96},{1,25},{2,98},{3,27},{4,100},{5,29},{6,102},{7,31},{8,104},... | collective-permute-start | bytes 1572872 | tf_op jit(solution)/shard_map/ppermute | solution.py:55
  10.4 10.2 %collective-permute-start.3 = (f32[256,512]{1,0:T(8,128)S(1)}, f32[256,512]{1,0:T(8,128)S(1)}, u32[]{:S(2)}, u32[]{:S(2)}) collective-permute-start(f32[256,512]{1,0:T(8,128)S(1)} %get-tuple-element.31), channel_id=1, source_target_pairs={{0,32},{1,9},{2,34},{3,11},{4,36},{5,13},{6,38},{7,15},{8,40},{9,1... | collective-permute-start | bytes 1572872 | tf_op jit(solution)/shard_map/ppermute | solution.py:55
  14.9 9.4 %collective-permute-start = (f32[256,512]{1,0:T(8,128)S(1)}, f32[256,512]{1,0:T(8,128)S(1)}, u32[]{:S(2)}, u32[]{:S(2)}) collective-permute-start(f32[256,512]{1,0:T(8,128)S(1)} %get-tuple-element.23), channel_id=1, source_target_pairs={{0,32},{1,9},{2,34},{3,11},{4,36},{5,13},{6,38},{7,15},{8,40},{9,1... | collective-permute-start | bytes 1572872 | tf_op jit(solution)/shard_map/ppermute | solution.py:55
  16.4 9.5 %collective-permute-start.1 = (f32[256,512]{1,0:T(8,128)S(1)}, f32[256,512]{1,0:T(8,128)S(1)}, u32[]{:S(2)}, u32[]{:S(2)}) collective-permute-start(f32[256,512]{1,0:T(8,128)S(1)} %get-tuple-element.24), channel_id=1, source_target_pairs={{0,96},{1,25},{2,98},{3,27},{4,100},{5,29},{6,102},{7,31},{8,104},... | collective-permute-start | bytes 1572872 | tf_op jit(solution)/shard_map/ppermute | solution.py:55
  20.7 10.9 %collective-permute-start.4 = (f32[256,512]{1,0:T(8,128)S(1)}, f32[256,512]{1,0:T(8,128)S(1)}, u32[]{:S(2)}, u32[]{:S(2)}) collective-permute-start(f32[256,512]{1,0:T(8,128)S(1)} %get-tuple-element.32), channel_id=1, source_target_pairs={{0,96},{1,25},{2,98},{3,27},{4,100},{5,29},{6,102},{7,31},{8,104},... | collective-permute-start | bytes 1572872 | tf_op jit(solution)/shard_map/ppermute | solution.py:55
  23.4 8.3 %collective-permute-start.5 = (f32[256,512]{1,0:T(8,128)S(1)}, f32[256,512]{1,0:T(8,128)S(1)}, u32[]{:S(2)}, u32[]{:S(2)}) collective-permute-start(f32[256,512]{1,0:T(8,128)S(1)} %get-tuple-element.33), channel_id=1, source_target_pairs={{0,32},{1,9},{2,34},{3,11},{4,36},{5,13},{6,38},{7,15},{8,40},{9,1... | collective-permute-start | bytes 1572872 | tf_op jit(solution)/shard_map/ppermute | solution.py:55
  30.7 40.4 %copy-start = (f32[16,512]{1,0:T(8,128)S(1)}, f32[16,512]{1,0:T(8,128)}, u32[]{:S(2)}) copy-start(f32[16,512]{1,0:T(8,128)} %weights_ref.1) | copy-start | bytes 98308
  30.7 40.4 %copy-start.1 = (f32[16,512]{1,0:T(8,128)S(1)}, f32[16,512]{1,0:T(8,128)}, u32[]{:S(2)}) copy-start(f32[16,512]{1,0:T(8,128)} %momentum_ref.1) | copy-start | bytes 98308
  31.9 6.8 %collective-permute-start.6 = (f32[128,512]{1,0:T(8,128)S(1)}, f32[128,512]{1,0:T(8,128)S(1)}, u32[]{:S(2)}, u32[]{:S(2)}) collective-permute-start(f32[128,512]{1,0:T(8,128)S(1)} %get-tuple-element.35), channel_id=1, source_target_pairs={{0,16},{1,65},{2,18},{3,67},{4,20},{5,69},{6,22},{7,71},{8,24},{9,... | collective-permute-start | bytes 786440 | tf_op jit(solution)/shard_map/ppermute | solution.py:55
  34.4 7.2 %collective-permute-start.7 = (f32[128,512]{1,0:T(8,128)S(1)}, f32[128,512]{1,0:T(8,128)S(1)}, u32[]{:S(2)}, u32[]{:S(2)}) collective-permute-start(f32[128,512]{1,0:T(8,128)S(1)} %get-tuple-element.36), channel_id=1, source_target_pairs={{0,8},{1,33},{2,10},{3,35},{4,12},{5,37},{6,14},{7,39},{8,0},{9,41... | collective-permute-start | bytes 786440 | tf_op jit(solution)/shard_map/ppermute | solution.py:55
  34.7 7.1 %collective-permute-start.8 = (f32[128,512]{1,0:T(8,128)S(1)}, f32[128,512]{1,0:T(8,128)S(1)}, u32[]{:S(2)}, u32[]{:S(2)}) collective-permute-start(f32[128,512]{1,0:T(8,128)S(1)} %get-tuple-element.37), channel_id=1, source_target_pairs={{0,24},{1,97},{2,26},{3,99},{4,28},{5,101},{6,30},{7,103},{8,16},{... | collective-permute-start | bytes 786440 | tf_op jit(solution)/shard_map/ppermute | solution.py:55
  41.9 5.4 %collective-permute-start.9 = (f32[4,16,512]{2,1,0:T(8,128)S(1)}, f32[4,16,512]{2,1,0:T(8,128)S(1)}, u32[]{:S(2)}, u32[]{:S(2)}) collective-permute-start(f32[4,16,512]{2,1,0:T(8,128)S(1)} %get-tuple-element.45), channel_id=1, source_target_pairs={{0,1},{1,0},{2,3},{3,2},{4,5},{5,4},{6,7},{7,6},{8,9},{9,8},{10,11... | collective-permute-start | bytes 393224 | tf_op jit(solution)/shard_map/ppermute | solution.py:25
  47.3 4.0 %collective-permute-start.10 = (f32[2,16,512]{2,1,0:T(8,128)S(1)}, f32[2,16,512]{2,1,0:T(8,128)S(1)}, u32[]{:S(2)}, u32[]{:S(2)}) collective-permute-start(f32[2,16,512]{2,1,0:T(8,128)S(1)} %get-tuple-element.42), channel_id=1, source_target_pairs={{0,2},{1,3},{2,0},{3,1},{4,6},{5,7},{6,4},{7,5},{8,10},{9,11},{10,... | collective-permute-start | bytes 196616 | tf_op jit(solution)/shard_map/ppermute | solution.py:25
  48.7 5.6 %collective-permute-start.11 = (f32[2,16,512]{2,1,0:T(8,128)S(1)}, f32[2,16,512]{2,1,0:T(8,128)S(1)}, u32[]{:S(2)}, u32[]{:S(2)}) collective-permute-start(f32[2,16,512]{2,1,0:T(8,128)S(1)} %get-tuple-element.41), channel_id=1, source_target_pairs={{0,4},{1,5},{2,6},{3,7},{4,0},{5,1},{6,2},{7,3},{8,12},{9,13},{10,... | collective-permute-start | bytes 196616 | tf_op jit(solution)/shard_map/ppermute | solution.py:25
  51.3 4.5 %collective-permute-start.12 = (f32[2,16,512]{2,1,0:T(8,128)S(1)}, f32[2,16,512]{2,1,0:T(8,128)S(1)}, u32[]{:S(2)}, u32[]{:S(2)}) collective-permute-start(f32[2,16,512]{2,1,0:T(8,128)S(1)} %get-tuple-element.40), channel_id=1, source_target_pairs={{0,6},{1,7},{2,4},{3,5},{4,2},{5,3},{6,0},{7,1},{8,14},{9,15},{10,... | collective-permute-start | bytes 196616 | tf_op jit(solution)/shard_map/ppermute | solution.py:25
